TPU v7x, 32 devices: a whole 2x2x4 slice. The times are simulated.
32 devices in a mesh: grp: 2 (over y), gy: 4 (over z), gx: 2 (over x), ch: 2 (over core).
Axes of the slice: x: 2, y: 2, z: 4, core: 2. Of those that a mesh axis runs over, the one named last changes fastest.
Arguments:
- cells: bfloat16 [128, 128, 512], P(('grp', 'gy'), 'gx'), parts along dimension 0, may hold values from -6 to 6
- w_expand: bfloat16 [512, 2048], P(None, 'ch'), may hold values from -0.25 to 0.25
- b_expand: float32 [2048], P('ch'), may hold values from -3 to 3
- w_depth: bfloat16 [3, 3, 2048], P(None, None, 'ch'), may hold values from -2 to 2
- b_depth: float32 [2048], P('ch'), may hold values from -3 to 3
- w_project: bfloat16 [2048, 512], P('ch'), may hold values from -0.125 to 0.125
- b_project: float32 [512], replicated, may hold values from -3 to 3
- ln_gain: float32 [512], replicated, may hold values from 0.5 to 1.5
- w_qkv: bfloat16 [512, 3, 512], P(None, None, 'ch'), as said below
- w_out: bfloat16 [512, 512], P('ch'), may hold values from -0.25 to 0.25
- b_out: float32 [512], P('ch'), may hold values from -3 to 3
Outputs:
- result: bfloat16 [128, 128, 512], P(('grp', 'gy'), 'gx', 'ch'), parts along dimension 0
There are 2 independent parts, one for each index of `grp`. A program takes and returns all parts, laid end to end along the dimension named above; an argument that names none is the same for every part. Nothing has to cross between parts.
Inputs may be any that keep to these rules, and one draw needn't show every extreme that they name: `w_qkv`: dense projection weights of every head.
All inputs are finite; a program needn't handle non-finite values.
Results may differ from a plain program's by a relative error of at most 0.01.
Values may be sent and summed in bfloat16 or wider, within the bound.
No kernel may reach another device: no remote copies, remote signals or barrier semaphores. Data moves between devices by JAX's collectives and lax.ppermute only.
A program may use at most 64 MiB of HBM per device.

v0:
```python
import jax
import jax.numpy as jnp
from jax import lax
from jax.sharding import PartitionSpec as P

HEAD_DIM = 32
GRID = 8


def extended(block, sides, width):
    for axis, dim in sides:
        count = lax.axis_size(axis)
        forward = [(i, i + 1) for i in range(count - 1)]
        backward = [(target, source) for source, target in forward]
        low = lax.ppermute(
            lax.slice_in_dim(block, block.shape[dim] - width, None, axis=dim), axis, forward
        )
        high = lax.ppermute(lax.slice_in_dim(block, 0, width, axis=dim), axis, backward)
        block = jnp.concatenate([low, block, high], axis=dim)
    return block


def gelu_exact(values):
    return jax.nn.gelu(values, approximate=False)


def expand_cells(source, w_expand, b_expand):
    pre = jnp.einsum("hwc,ce->hwe", source, w_expand, preferred_element_type=jnp.float32)
    return gelu_exact(pre + b_expand).astype(jnp.bfloat16)


def depthwise(padded, w_depth, b_depth, tile_h, tile_w):
    summed = jnp.zeros((tile_h, tile_w, padded.shape[2]), jnp.float32)
    for row_off in range(3):
        for col_off in range(3):
            summed = summed + padded[row_off : row_off + tile_h, col_off : col_off + tile_w].astype(
                jnp.float32
            ) * w_depth[row_off, col_off].astype(jnp.float32)
    return gelu_exact(summed + b_depth).astype(jnp.bfloat16)


def split_order(tile, depth_h, depth_w):
    tile_h, tile_w, width = tile.shape
    shaped = tile.reshape(tile_h // depth_h, depth_h, tile_w // depth_w, depth_w, width)
    return shaped.transpose(1, 0, 3, 2, 4)


def join_order(arranged):
    depth_h, outer_h, depth_w, outer_w, width = arranged.shape
    return arranged.transpose(1, 0, 3, 2, 4).reshape(outer_h * depth_h, outer_w * depth_w, width)


def into_windows(arrived, steps_h, steps_w):
    local_h, span_h, local_w, span_w, width = arrived.shape
    grouped = arrived.reshape(local_h, GRID, steps_h, local_w, GRID, steps_w, width)
    grouped = grouped.transpose(2, 0, 5, 3, 1, 4, 6)
    return grouped.reshape(steps_h * local_h * steps_w * local_w, GRID * GRID, width)


def out_of_windows(windows, local_h, steps_h, local_w, steps_w):
    width = windows.shape[2]
    grouped = windows.reshape(steps_h, local_h, steps_w, local_w, GRID, GRID, width)
    grouped = grouped.transpose(1, 4, 0, 3, 5, 2, 6)
    return grouped.reshape(local_h, GRID * steps_h, local_w, GRID * steps_w, width)


def attend(window_full, ln_gain, w_qkv):
    values = window_full.astype(jnp.float32)
    centre = jnp.mean(values, axis=-1, keepdims=True)
    centered = values - centre
    spread = jnp.mean(centered * centered, axis=-1, keepdims=True)
    normed = (centered * lax.rsqrt(spread + 1e-05) * ln_gain).astype(jnp.bfloat16)
    projected = jnp.einsum(
        "wtc,cke->kwte", normed, w_qkv, preferred_element_type=jnp.float32
    ).astype(jnp.bfloat16)
    window_count = projected.shape[1]
    tokens = projected.shape[2]
    own_width = projected.shape[3]
    heads_own = own_width // HEAD_DIM
    shaped = projected.reshape(3, window_count, tokens, heads_own, HEAD_DIM)
    scores = jnp.einsum(
        "wqhd,wkhd->whqk", shaped[0], shaped[1], preferred_element_type=jnp.float32
    ) * HEAD_DIM ** (-0.5)
    weights = jax.nn.softmax(scores, axis=-1).astype(jnp.bfloat16)
    heads_out = jnp.einsum(
        "whqk,wkhd->wqhd", weights, shaped[2], preferred_element_type=jnp.float32
    ).astype(jnp.bfloat16)
    return heads_out.reshape(window_count, tokens, own_width)


def per_device(
    cells, w_expand, b_expand, w_depth, b_depth, w_project, b_project, ln_gain, w_qkv, w_out, b_out
):
    tile_h, tile_w, width = cells.shape
    n_rows = lax.axis_size("gy")
    n_cols = lax.axis_size("gx")
    half = width // lax.axis_size("ch")
    own = lax.axis_index("ch")
    stride_h = tile_h * n_rows // GRID
    stride_w = tile_w * n_cols // GRID
    depth_h = min(tile_h, stride_h)
    depth_w = min(tile_w, stride_w)
    steps_h = stride_h // depth_h
    steps_w = stride_w // depth_w
    local_h = depth_h // n_rows
    local_w = depth_w // n_cols
    expanded = expand_cells(cells, w_expand, b_expand)
    padded = extended(expanded, (("gy", 0), ("gx", 1)), 1)
    depth = depthwise(padded, w_depth, b_depth, tile_h, tile_w)
    partial_value = jnp.einsum("hwe,ec->hwc", depth, w_project, preferred_element_type=jnp.float32)
    share = lax.psum_scatter(
        partial_value.astype(jnp.bfloat16), "ch", scatter_dimension=2, tiled=True
    ).astype(jnp.float32)
    cells_own = lax.dynamic_slice_in_dim(cells, own * half, half, 2)
    bias_own = lax.dynamic_slice_in_dim(b_project, own * half, half, 0)
    mixed_own = (cells_own.astype(jnp.float32) + share + bias_own).astype(jnp.bfloat16)
    arranged = split_order(mixed_own, depth_h, depth_w)
    arrived = lax.all_to_all(
        lax.all_to_all(arranged, "gy", split_axis=0, concat_axis=1, tiled=True),
        "gx",
        split_axis=2,
        concat_axis=3,
        tiled=True,
    )
    window_own = into_windows(arrived, steps_h, steps_w)
    window_full = lax.all_gather(window_own, "ch", axis=2, tiled=True)
    heads_out = attend(window_full, ln_gain, w_qkv)
    attention_terms = jnp.einsum(
        "wte,ec->wtc", heads_out, w_out, preferred_element_type=jnp.float32
    )
    attention_own = lax.psum_scatter(
        attention_terms.astype(jnp.bfloat16), "ch", scatter_dimension=2, tiled=True
    ).astype(jnp.float32)
    outcome = (window_own.astype(jnp.float32) + attention_own + b_out).astype(jnp.bfloat16)
    leaving = out_of_windows(outcome, local_h, steps_h, local_w, steps_w)
    returned = lax.all_to_all(
        lax.all_to_all(leaving, "gy", split_axis=1, concat_axis=0, tiled=True),
        "gx",
        split_axis=3,
        concat_axis=2,
        tiled=True,
    )
    return join_order(returned)


def solution(mesh):
    placed = (
        P(("grp", "gy"), "gx", None),
        P(None, "ch"),
        P("ch"),
        P(None, None, "ch"),
        P("ch"),
        P("ch", None),
        P(),
        P(),
        P(None, None, "ch"),
        P("ch", None),
        P("ch"),
    )
    return jax.shard_map(
        per_device,
        mesh=mesh,
        in_specs=placed,
        out_specs=P(("grp", "gy"), "gx", "ch"),
        check_vma=False,
    )
```

profile of v0, /device:TPU:0, one launch (start us, length us, event | category | flops | bytes accessed | tf_op | source)
XLA Modules:
  0.0 173.2 jit_solution(14447572569704020268)
XLA Ops:
  6.5 1.2 copy-done
  7.8 11.1 %fusion.3 = bf16[16,64,1024]{2,1,0:T(8,128)(2,1)S(1)} fusion(bf16[16,64,512]{2,1,0:T(8,128)(2,1)} %param.11, f32[1024]{0:T(1024)} %param.13, bf16[512,1024]{1,0:T(8,128)(2,1)S(1)} %copy-done), kind=kOutput, calls=%fused_computation.5 | convolution fusion | flops 1142947840 | bytes 4198400 | tf_op jit(solution)/shard_map/hwc,ce->hwe/dot_general | solution.py:28
  18.9 4.9 %collective-permute-start = (bf16[1,64,1024]{2,1,0:T(8,128)(2,1)S(1)}, bf16[1,64,1024]{2,1,0:T(8,128)(2,1)S(1)}, u32[]{:S(2)}, u32[]{:S(2)}) collective-permute-start(bf16[1,64,1024]{2,1,0:T(8,128)(2,1)S(1)} %get-tuple-element.9), channel_id=1, source_target_pairs={{0,4},{4,8},{8,12},{1,5},{5,9},{9,13},{2,6},{6,10},{10,14},{3,7},{... | collective-permute-start | bytes 393224 | tf_op jit(solution)/shard_map/ppermute | solution.py:15
  23.8 1.3 collective-permute-start.1
  25.1 1.4 collective-permute-done
  26.5 4.1 %collective-permute-done.1 = bf16[1,64,1024]{2,1,0:T(8,128)(2,1)S(1)} collective-permute-done((bf16[1,64,1024]{2,1,0:T(8,128)(2,1)S(1)}, bf16[1,64,1024]{2,1,0:T(8,128)(2,1)S(1)}, u32[]{:S(2)}, u32[]{:S(2)}) %collective-permute-start.1) | collective-permute-done | bytes 131104 | tf_op jit(solution)/shard_map/ppermute | solution.py:18
  30.7 0.1 pad_maximum_fusion.5
  30.8 0.0 copy-start.7
  30.8 0.0 copy-start.9
  30.8 3.5 %collective-permute-start.2 = (bf16[18,1,1024]{2,1,0:T(2,128)(2,1)S(1)}, bf16[18,1,1024]{2,1,0:T(2,128)(2,1)S(1)}, u32[]{:S(2)}, u32[]{:S(2)}) collective-permute-start(bf16[18,1,1024]{2,1,0:T(2,128)(2,1)S(1)} %get-tuple-element.7), channel_id=1, source_target_pairs={{0,2},{1,3},{4,6},{5,7},{8,10},{9,11},{12,14},{13,15},{16,18},{17,... | collective-permute-start | bytes 110600 | tf_op jit(solution)/shard_map/ppermute | solution.py:15
  34.3 1.3 collective-permute-start.3
  35.7 0.6 collective-permute-done.2
  36.3 4.3 %collective-permute-done.3 = bf16[18,1,1024]{2,1,0:T(2,128)(2,1)S(1)} collective-permute-done((bf16[18,1,1024]{2,1,0:T(2,128)(2,1)S(1)}, bf16[18,1,1024]{2,1,0:T(2,128)(2,1)S(1)}, u32[]{:S(2)}, u32[]{:S(2)}) %collective-permute-start.3) | collective-permute-done | bytes 36896 | tf_op jit(solution)/shard_map/ppermute | solution.py:18
  40.6 1.6 maximum_maximum_fusion
  42.2 0.0 copy-start.6
  42.2 0.0 copy-start.2
  42.2 16.1 %fusion.35 = bf16[16,64,512]{2,1,0:T(8,128)(2,1)} fusion(bf16[16,64,1024]{2,1,0:T(8,128)(2,1)S(1)} %fusion.3, bf16[18,65,1024]{2,1,0:T(8,128)(2,1)S(1)} %get-tuple-element.6, bf16[1,64,1024]{2,1,0:T(8,128)(2,1)S(1)} %collective-permute-done.1, bf16[18,65,1024]{2,1,0:T(8,128)(2,1)S(1)} %get-tuple-element.5, ...), kind=kOutput, calls=%fused_computation.62 | convolution fusion | flops 1172832256 | bytes 17080320 | tf_op jit(solution)/shard_map/hwe,ec->hwc/dot_general | solution.py:110
  58.3 0.0 reduce-scatter.3.cloned.1.call-update
  58.3 0.0 all-gather.2.cloned.1.call-start
  58.4 0.1 dynamic_slice.7
  58.4 7.9 %reduce-scatter.3.cloned.1.call-done = bf16[16,64,256]{2,1,0:T(8,128)(2,1)} async-done(((bf16[16,64,512]{2,1,0:T(8,128)(2,1)}), bf16[16,64,256]{2,1,0:T(8,128)(2,1)}) %reduce-scatter.3.cloned.1.call-update) | async-done | bytes 524304 | tf_op jit(solution)/shard_map/reduce_scatter | solution.py:111
  66.3 1.2 add_convert_fusion.1
  67.6 19.6 %all_to_all.69 = bf16[8,2,16,4,256]{4,2,3,1,0:T(8,128)(2,1)S(1)} all-to-all(bf16[8,2,16,4,256]{4,2,3,1,0:T(8,128)(2,1)S(1)} %bitcast.80), channel_id=1, replica_groups=mesh['grp'=2,'gy'=4,'gx'=2,'ch'=2] {'gy'}, dimensions={0} | all-to-all | bytes 1048576 | tf_op jit(solution)/shard_map/all_to_all | solution.py:119
  87.3 0.3 copy.52
  87.5 10.0 %all_to_all.70 = bf16[2,8,16,4,256]{4,3,1,0,2:T(4,128)(2,1)S(1)} all-to-all(bf16[2,8,16,4,256]{4,3,1,0,2:T(4,128)(2,1)S(1)} %copy.52), channel_id=1, replica_groups=mesh['grp'=2,'gy'=4,'gx'=2,'ch'=2] {'gx'}, dimensions={2} | all-to-all | bytes 1048576 | tf_op jit(solution)/shard_map/all_to_all | solution.py:118
  97.6 0.3 copy.79
  97.9 0.1 copy.54
  97.9 0.9 copy.55
  98.9 0.0 all-gather.2.cloned.1.call-update
  98.9 0.2 reduce-scatter.5.cloned.1.call-start
  99.1 7.3 %all-gather.2.cloned.1.call-done = bf16[16,64,512]{2,1,0:T(8,128)(2,1)} async-done(((bf16[16,64,256]{2,1,0:T(8,128)(2,1)}), bf16[16,64,512]{2,1,0:T(8,128)(2,1)}) %all-gather.2.cloned.1.call-update) | async-done | bytes 1048592 | tf_op jit(solution)/shard_map/all_gather | solution.py:126
  106.4 1.4 convert_reduce_fusion
  107.8 1.7 fusion.26
  109.6 2.3 %fusion.34 = bf16[3,16,64,256]{3,2,0,1:T(8,128)(2,1)S(1)} fusion(bf16[16,64,512]{2,1,0:T(8,128)(2,1)} %all-gather.2.cloned.1.call-done, f32[512]{0:T(512)S(1)} %copy-done.10, f32[16,64]{1,0:T(8,128)S(1)} %add_rsqrt_fusion, f32[16,64]{1,0:T(8,128)S(1)} %broadcast_multiply_fusion, bf16[512,3,256]{2,0,1:T(8,128)(2,1)S(1)} %copy-done.8), kind=kOutput, calls=%fused_computation.61 | convolution fusion | flops 808714240 | bytes 3418112 | tf_op jit(solution)/shard_map/wtc,cke->kwte/dot_general | solution.py:73
  111.9 0.2 fusion.82
  112.1 1.3 copy.57
  113.4 0.5 copy.58
  113.9 1.3 copy.56
  115.2 4.9 %fusion.83 = (f32[16,8,64]{2,1,0:T(8,128)S(1)}, f32[16,8,64,64]{2,3,1,0:T(8,128)}) fusion(bf16[16,64,8,32]{1,3,2,0:T(8,128)(2,1)} %bitcast.91, bf16[16,64,8,32]{1,3,2,0:T(8,128)(2,1)S(1)} %bitcast.92), kind=kOutput, calls=%fused_computation.126 | convolution fusion | flops 35127360 | bytes 3178496 | tf_op jit(solution)/shard_map/sub | solution.py:84
  120.2 3.2 %fusion.33 = bf16[16,8,32,64]{3,2,1,0:T(8,128)(2,1)S(1)} fusion(bf16[16,64,8,32]{1,3,2,0:T(8,128)(2,1)} %bitcast.93, f32[16,8,64,64]{2,3,1,0:T(8,128)} %get-tuple-element.24, f32[16,8,64]{2,1,0:T(8,128)S(1)} %get-tuple-element.23), kind=kOutput, calls=%fused_computation.59 | convolution fusion | flops 34865152 | bytes 3178496 | tf_op jit(solution)/shard_map/whqk,wkhd->wqhd/dot_general | solution.py:85
  123.4 1.4 convolution_convert_fusion.1
  124.9 0.0 reduce-scatter.5.cloned.1.call-update
  124.9 9.9 %reduce-scatter.5.cloned.1.call-done = bf16[16,64,256]{2,1,0:T(8,128)(2,1)} async-done(((bf16[16,64,512]{2,1,0:T(8,128)(2,1)}), bf16[16,64,256]{2,1,0:T(8,128)(2,1)}) %reduce-scatter.5.cloned.1.call-update) | async-done | bytes 524304 | tf_op jit(solution)/shard_map/reduce_scatter | solution.py:131
  134.8 1.2 add_convert_fusion
  136.0 19.6 %all_to_all.71 = bf16[2,8,8,8,256]{4,3,2,0,1:T(8,128)(2,1)S(1)} all-to-all(bf16[2,8,8,8,256]{4,3,2,0,1:T(8,128)(2,1)S(1)} %bitcast.85), channel_id=1, replica_groups=mesh['grp'=2,'gy'=4,'gx'=2,'ch'=2] {'gy'}, dimensions={1} | all-to-all | bytes 1048576 | tf_op jit(solution)/shard_map/all_to_all | solution.py:137
  155.7 0.1 copy.64
  155.8 10.0 %all_to_all.72 = bf16[8,2,8,8,256]{4,2,1,0,3:T(8,128)(2,1)S(1)} all-to-all(bf16[8,2,8,8,256]{4,2,1,0,3:T(8,128)(2,1)S(1)} %copy.64), channel_id=1, replica_groups=mesh['grp'=2,'gy'=4,'gx'=2,'ch'=2] {'gx'}, dimensions={3} | all-to-all | bytes 1048576 | tf_op jit(solution)/shard_map/all_to_all | solution.py:136
  165.9 0.8 copy.67
  (27 shorter events, 0.3 us)
Async XLA Ops:
  6.5 1.2 copy-start
  6.5 29.1 %copy-start.4 = (bf16[3,3,1024]{2,1,0:T(4,128)(2,1)S(1)}, bf16[3,3,1024]{2,1,0:T(4,128)(2,1)}, u32[]{:S(2)}) copy-start(bf16[3,3,1024]{2,1,0:T(4,128)(2,1)} %param.14) | copy-start | bytes 55300
  6.5 59.8 %reduce-scatter.3.cloned.1.call-start = ((), (), s32[]{:S(2)}) async-start(), calls=%async_computation.6 | async-start | bytes 1572864 | tf_op jit(solution)/shard_map/reduce_scatter | solution.py:111
  18.9 7.7 %collective-permute-start = (bf16[1,64,1024]{2,1,0:T(8,128)(2,1)S(1)}, bf16[1,64,1024]{2,1,0:T(8,128)(2,1)S(1)}, u32[]{:S(2)}, u32[]{:S(2)}) collective-permute-start(bf16[1,64,1024]{2,1,0:T(8,128)(2,1)S(1)} %get-tuple-element.9), channel_id=1, source_target_pairs={{0,4},{4,8},{8,12},{1,5},{5,9},{9,13},{2,6},{6,10},{10,14},{3,7},{... | collective-permute-start | bytes 393224 | tf_op jit(solution)/shard_map/ppermute | solution.py:15
  23.8 6.9 %collective-permute-start.1 = (bf16[1,64,1024]{2,1,0:T(8,128)(2,1)S(1)}, bf16[1,64,1024]{2,1,0:T(8,128)(2,1)S(1)}, u32[]{:S(2)}, u32[]{:S(2)}) collective-permute-start(bf16[1,64,1024]{2,1,0:T(8,128)(2,1)S(1)} %get-tuple-element.10), channel_id=1, source_target_pairs={{4,0},{8,4},{12,8},{5,1},{9,5},{13,9},{6,2},{10,6},{14,10},{7,3},{... | collective-permute-start | bytes 393224 | tf_op jit(solution)/shard_map/ppermute | solution.py:18
  30.8 11.4 %copy-start.7 = (bf16[1024,512]{1,0:T(8,128)(2,1)S(1)}, bf16[1024,512]{1,0:T(8,128)(2,1)}, u32[]{:S(2)}) copy-start(bf16[1024,512]{1,0:T(8,128)(2,1)} %param.16) | copy-start | bytes 3145732
  30.8 11.4 %copy-start.9 = (f32[1024]{0:T(1024)S(1)}, f32[1024]{0:T(1024)}, u32[]{:S(2)}) copy-start(f32[1024]{0:T(1024)} %param.15) | copy-start | bytes 12292
  30.8 5.5 %collective-permute-start.2 = (bf16[18,1,1024]{2,1,0:T(2,128)(2,1)S(1)}, bf16[18,1,1024]{2,1,0:T(2,128)(2,1)S(1)}, u32[]{:S(2)}, u32[]{:S(2)}) collective-permute-start(bf16[18,1,1024]{2,1,0:T(2,128)(2,1)S(1)} %get-tuple-element.7), channel_id=1, source_target_pairs={{0,2},{1,3},{4,6},{5,7},{8,10},{9,11},{12,14},{13,15},{16,18},{17,... | collective-permute-start | bytes 110600 | tf_op jit(solution)/shard_map/ppermute | solution.py:15
  34.3 6.2 %collective-permute-start.3 = (bf16[18,1,1024]{2,1,0:T(2,128)(2,1)S(1)}, bf16[18,1,1024]{2,1,0:T(2,128)(2,1)S(1)}, u32[]{:S(2)}, u32[]{:S(2)}) collective-permute-start(bf16[18,1,1024]{2,1,0:T(2,128)(2,1)S(1)} %get-tuple-element.8), channel_id=1, source_target_pairs={{2,0},{3,1},{6,4},{7,5},{10,8},{11,9},{14,12},{15,13},{18,16},{19,... | collective-permute-start | bytes 110600 | tf_op jit(solution)/shard_map/ppermute | solution.py:18
  42.2 16.2 %copy-start.6 = (f32[512]{0:T(512)S(1)}, f32[512]{0:T(512)}, u32[]{:S(2)}) copy-start(f32[512]{0:T(512)} %param.17) | copy-start | bytes 6148
  42.2 24.1 %copy-start.2 = (bf16[16,64,512]{2,1,0:T(8,128)(2,1)S(1)}, bf16[16,64,512]{2,1,0:T(8,128)(2,1)}, u32[]{:S(2)}) copy-start(bf16[16,64,512]{2,1,0:T(8,128)(2,1)} %param.11) | copy-start | bytes 3145732
  58.3 48.1 %all-gather.2.cloned.1.call-start = ((), (), s32[]{:S(2)}) async-start(), calls=%async_computation.7 | async-start | bytes 1572864 | tf_op jit(solution)/shard_map/all_gather | solution.py:126
  87.2 22.3 %copy-start.8 = (bf16[512,3,256]{2,0,1:T(8,128)(2,1)S(1)}, bf16[512,3,256]{2,0,1:T(8,128)(2,1)}, u32[]{:S(2)}) copy-start(bf16[512,3,256]{2,0,1:T(8,128)(2,1)} %param.19) | copy-start | bytes 2359300
  87.2 22.3 %copy-start.10 = (f32[512]{0:T(512)S(1)}, f32[512]{0:T(512)}, u32[]{:S(2)}) copy-start(f32[512]{0:T(512)} %param.18) | copy-start | bytes 6148
  98.9 35.9 %reduce-scatter.5.cloned.1.call-start = ((), (), s32[]{:S(2)}) async-start(), calls=%async_computation.8 | async-start | bytes 1572864 | tf_op jit(solution)/shard_map/reduce_scatter | solution.py:131
  120.1 3.3 %copy-start.3 = (bf16[256,512]{1,0:T(8,128)(2,1)S(1)}, bf16[256,512]{1,0:T(8,128)(2,1)}, u32[]{:S(2)}) copy-start(bf16[256,512]{1,0:T(8,128)(2,1)} %param.20) | copy-start | bytes 786436
  120.1 14.6 %copy-start.1 = (bf16[1,2,1,8,8,8,256]{6,5,4,3,1,2,0:T(8,128)(2,1)S(1)}, bf16[1,2,1,8,8,8,256]{6,5,4,3,1,2,0:T(8,128)(2,1)}, u32[]{:S(2)}) copy-start(bf16[1,2,1,8,8,8,256]{6,5,4,3,1,2,0:T(8,128)(2,1)} %copy.55) | copy-start | bytes 1572868
  120.2 14.6 %copy-start.5 = (f32[256]{0:T(256)S(1)}, f32[256]{0:T(256)}, u32[]{:S(2)}) copy-start(f32[256]{0:T(256)} %param.21) | copy-start | bytes 3076
Sparse Core Ops, SparseCore 0:
  58.4 7.8 reduce-scatter.2
  99.0 7.3 all-gather.1
  125.0 9.7 reduce-scatter.4
where the time goes:
time: 174 us; the launch traced here: 173 us
  blocking collectives  59.3 us (34%)
  matrix products  39.1 us (22%)
  waiting for transfers between devices  35.5 us (20%)
  between operations  13.4 us (8%)
  starting transfers between devices  11.3 us (6%)
  local copies, waits for them, and re-layouts  7.33 us (4%)
  other arithmetic  7.27 us (4%)
    all_to_all x1, blocking collectives, per_device(): lax.all_to_all(arranged, 'gy', split_axis=0, concat_axis=1, tiled=True)  19.6 us
    all_to_all x1, blocking collectives, per_device(): lax.all_to_all(leaving, 'gy', split_axis=1, concat_axis=0, tiled=True)  19.6 us
    dot_general x1, matrix products, per_device(): jnp.einsum('hwe,ec->hwc', depth, w_project, preferred_element_type=jnp.fl...  16.1 us
    dot_general x1, matrix products, expand_cells(): jnp.einsum('hwc,ce->hwe', source, w_expand, preferred_element_type=jnp.fl...  11.1 us
    all_to_all x1, blocking collectives, per_device(): lax.all_to_all(lax.all_to_all(arranged, 'gy', split_axis=0, concat_axis=1...  10 us
    all_to_all x1, blocking collectives, per_device(): lax.all_to_all(lax.all_to_all(leaving, 'gy', split_axis=1, concat_axis=0,...  10 us
    reduce_scatter x1, waiting for transfers between devices, per_device(): lax.psum_scatter(attention_terms.astype(jnp.bfloat16), 'ch', scatter_dime...  9.89 us
    ppermute x2, starting transfers between devices, extended(): lax.ppermute(lax.slice_in_dim(block, block.shape[dim] - width, None, axis...  8.47 us
  transfers between devices with their start and end apart: 7, of which 7 were waited for; matrix products, arithmetic and copies ran while one was open for 0% of the time, Pallas kernels for 0%

commit v1 on v0

--- a/solution.py
+++ b/solution.py
@@ -1,7 +1,16 @@
+import functools
+
 import jax
 import jax.numpy as jnp
+import numpy as np
 from jax import lax
+from jax.experimental import pallas as pl
+from jax.experimental.pallas import tpu as pltpu
 from jax.sharding import PartitionSpec as P
+
+SUBLANES = 8
+CHUNK = 256
+VMEM_BYTES = 48 * 2**20
 
 HEAD_DIM = 32
 GRID = 8
@@ -88,7 +97,7 @@
     return heads_out.reshape(window_count, tokens, own_width)
 
 
-def per_device(
+def general_device(
     cells, w_expand, b_expand, w_depth, b_depth, w_project, b_project, ln_gain, w_qkv, w_out, b_out
 ):
     tile_h, tile_w, width = cells.shape
@@ -143,6 +152,380 @@
     return join_order(returned)
 
 
+class Plan:
+    def __init__(self, cells, n_rows, n_cols, n_ch):
+        tile_h, tile_w, self.width = cells.shape
+        stride_h, stride_w = tile_h * n_rows // GRID, tile_w * n_cols // GRID
+        self.depth_h, self.depth_w = min(tile_h, stride_h), min(tile_w, stride_w)
+        self.outer_h, self.outer_w = tile_h // self.depth_h, tile_w // self.depth_w
+        self.n_rows, self.n_cols, self.n_ch = n_rows, n_cols, n_ch
+        self.fits = (
+            self.depth_h == stride_h
+            and self.depth_w == stride_w
+            and self.outer_h * self.outer_w == SUBLANES
+            and min(self.outer_h, self.outer_w) >= 2
+            and self.depth_h == n_rows * n_ch
+            and self.depth_w == n_cols * SUBLANES
+            and n_ch == 2
+            and n_rows * n_cols * SUBLANES == GRID * GRID
+            and self.width % CHUNK == 0
+        )
+
+    def order(self):
+        count = self.depth_w * SUBLANES
+        source = np.arange(count).reshape(self.outer_h, self.outer_w, self.depth_w)
+        source = source.transpose(2, 0, 1).reshape(count)
+        return np.eye(count, dtype=np.float32)[source]
+
+    def sides(self):
+        planes, rows = self.depth_h + 2, self.outer_h * self.depth_h + 2
+        left = np.zeros((planes, self.outer_h, self.outer_w, rows), np.float32)
+        right = np.zeros_like(left)
+        for plane in range(planes):
+            for i in range(self.outer_h):
+                left[plane, i, 0, i * self.depth_h + plane] = 1
+                right[plane, i, -1, i * self.depth_h + plane] = 1
+        return left.reshape(-1, rows), right.reshape(-1, rows)
+
+
+def gelu_erf(values):
+    return (0.5 * values) * (1.0 + lax.erf(values * 0.5**0.5))
+
+
+def expand_kernel(cells_ref, w_ref, b_ref, order_ref, out_ref, arranged_ref):
+    planes = cells_ref.shape[1]
+    count, width = arranged_ref.shape[1:]
+    for plane in range(planes):
+        block = cells_ref[:, plane].reshape(count, width)
+        arranged_ref[plane] = jnp.dot(
+            order_ref[...], block, preferred_element_type=jnp.float32
+        ).astype(jnp.bfloat16)
+    source = arranged_ref[...].reshape(planes * count, width)
+    for low in range(0, out_ref.shape[2], CHUNK):
+        part = slice(low, low + CHUNK)
+        pre = jnp.dot(source, w_ref[:, part], preferred_element_type=jnp.float32)
+        out_ref[:, :, part] = (
+            gelu_erf(pre + b_ref[:, part]).astype(jnp.bfloat16).reshape(planes, count, CHUNK)
+        )
+
+
+def expand(plan, cells, w_expand, b_expand, order):
+    planes = 2
+    count = plan.depth_w * SUBLANES
+    own = w_expand.shape[1]
+    shaped = cells.reshape(plan.outer_h, plan.depth_h, count // plan.outer_h, plan.width)
+    return pl.pallas_call(
+        expand_kernel,
+        grid=(plan.depth_h // planes,),
+        in_specs=[
+            pl.BlockSpec((plan.outer_h, planes) + shaped.shape[2:], lambda i: (0, i, 0, 0)),
+            pl.BlockSpec(w_expand.shape, lambda i: (0, 0)),
+            pl.BlockSpec(b_expand.shape, lambda i: (0, 0)),
+            pl.BlockSpec(order.shape, lambda i: (0, 0)),
+        ],
+        out_specs=[
+            pl.BlockSpec((planes, count, own), lambda i: (i, 0, 0)),
+            pl.BlockSpec((planes, count, plan.width), lambda i: (i, 0, 0)),
+        ],
+        out_shape=[
+            jax.ShapeDtypeStruct((plan.depth_h, count, own), jnp.bfloat16),
+            jax.ShapeDtypeStruct((plan.depth_h, count, plan.width), jnp.bfloat16),
+        ],
+        compiler_params=pltpu.CompilerParams(vmem_limit_bytes=VMEM_BYTES),
+        cost_estimate=pl.CostEstimate(
+            flops=2 * cells.size * own, bytes_accessed=8 * cells.size, transcendentals=0
+        ),
+        name="expand",
+    )(shaped, w_expand, b_expand, order)
+
+
+def depth_kernel(
+    plan, flag_ref, e_ref, x_ref, up_ref, down_ref, left_ref, right_ref, order_ref, left_at_ref,
+    right_at_ref, we_ref, be_ref, wd_ref, bd_ref, wp_ref, bp_ref, sib_ref, own_ref, held, deep,
+):
+    step = pl.program_id(0)
+    deep_h, deep_w, outer_w = plan.depth_h, plan.depth_w, plan.outer_w
+    count = deep_w * SUBLANES
+    chunk = e_ref.shape[2]
+    flags = [flag_ref[i].astype(jnp.float32) for i in range(1, 5)]
+    up, down, left, right = flags
+
+    def expanded(cells):
+        pre = jnp.dot(cells, we_ref[...], preferred_element_type=jnp.float32)
+        return gelu_erf(pre + be_ref[...])
+
+    row = lax.broadcasted_iota(jnp.int32, (1, SUBLANES, chunk), 1)
+    halo = jnp.concatenate([up_ref[...], down_ref[...]], axis=0)
+    spare = count - halo.shape[0]
+    if spare:
+        middle = jnp.zeros((spare, plan.width), halo.dtype)
+        halo = jnp.concatenate([up_ref[...], middle, down_ref[...]], axis=0)
+    halo = jnp.dot(order_ref[...], halo, preferred_element_type=jnp.float32).astype(jnp.bfloat16)
+    halo = expanded(halo).reshape(deep_w, SUBLANES, chunk)
+    halo = halo * jnp.where(row < outer_w, up, down)
+    side = jnp.dot(left_at_ref[...], left_ref[...], preferred_element_type=jnp.float32)
+    side = side + jnp.dot(right_at_ref[...], right_ref[...], preferred_element_type=jnp.float32)
+    side = expanded(side.astype(jnp.bfloat16)).reshape(deep_h + 2, SUBLANES, chunk)
+    side = side * jnp.where(row % outer_w == 0, left, right)
+    plane = lax.broadcasted_iota(jnp.int32, (deep_h + 2, SUBLANES, 1), 0)
+    at = lax.broadcasted_iota(jnp.int32, (deep_h + 2, SUBLANES, 1), 1)
+    side = side * jnp.where((plane == 0) & (at < outer_w), up, 1.0)
+    side = side * jnp.where((plane == deep_h + 1) & (at >= SUBLANES - outer_w), down, 1.0)
+
+    for a in range(deep_h):
+        values = e_ref[a].astype(jnp.float32).reshape(deep_w, SUBLANES, chunk)
+        held[a + 1, 1 : deep_w + 1] = values
+        if a == deep_h - 1:
+            held[0, 1 : deep_w + 1] = jnp.where(
+                row < outer_w, halo, pltpu.roll(values, outer_w, 1)
+            )
+        if a == 0:
+            held[deep_h + 1, 1 : deep_w + 1] = jnp.where(
+                row >= SUBLANES - outer_w, halo, pltpu.roll(values, SUBLANES - outer_w, 1)
+            )
+    held[:, 0] = jnp.where(row % outer_w == 0, side, pltpu.roll(held[:, deep_w], 1, 1))
+    held[:, deep_w + 1] = jnp.where(
+        row % outer_w == outer_w - 1, side, pltpu.roll(held[:, 1], SUBLANES - 1, 1)
+    )
+    for low in range(0, chunk, 128):
+        lanes = slice(low, low + 128)
+        for a in range(deep_h):
+            total = jnp.broadcast_to(bd_ref[:, lanes], (deep_w, SUBLANES, 128))
+            for di in range(3):
+                for dj in range(3):
+                    total = total + held[a + di, dj : dj + deep_w, :, lanes] * wd_ref[
+                        3 * di + dj : 3 * di + dj + 1, lanes
+                    ].astype(jnp.float32)
+            deep[step, a, :, lanes] = (
+                gelu_erf(total).astype(jnp.bfloat16).reshape(count, 128)
+            )
+
+    @pl.when(step == pl.num_programs(0) - 1)
+    def _():
+        core = flag_ref[0]
+
+        def projected(a):
+            total = jnp.zeros((count, plan.width), jnp.float32)
+            for piece in range(deep.shape[0]):
+                total = total + jnp.dot(
+                    deep[piece, a],
+                    wp_ref[piece * chunk : (piece + 1) * chunk],
+                    preferred_element_type=jnp.float32,
+                )
+            return total
+
+        for block in range(plan.n_rows):
+            sib_ref[block] = projected(2 * block + 1 - core).astype(jnp.bfloat16)
+        for block in range(plan.n_rows):
+            a = 2 * block + core
+            own_ref[block] = projected(a) + (x_ref[a].astype(jnp.float32) + bp_ref[...])
+
+
+def deepen(plan, flags, e, x, rows, cols, w_expand, b_expand, w_depth, b_depth, w_project, b_project, order):
+    own = w_expand.shape[1]
+    count = plan.depth_w * SUBLANES
+    steps = own // CHUNK
+    left_at, right_at = (jnp.asarray(m, jnp.bfloat16) for m in plan.sides())
+    whole = lambda v: pl.BlockSpec(v.shape, lambda i: (0,) * v.ndim)
+    columns = lambda v: pl.BlockSpec((v.shape[0], CHUNK), lambda i: (0, i))
+    up, down = rows
+    left, right = cols
+    operands = (
+        (flags, pl.BlockSpec(memory_space=pltpu.SMEM)),
+        (e, pl.BlockSpec(e.shape[:2] + (CHUNK,), lambda i: (0, 0, i))),
+        (x, whole(x)),
+        (up, whole(up)),
+        (down, whole(down)),
+        (left, whole(left)),
+        (right, whole(right)),
+        (order, whole(order)),
+        (left_at, whole(left_at)),
+        (right_at, whole(right_at)),
+        (w_expand, columns(w_expand)),
+        (b_expand, columns(b_expand)),
+        (w_depth, columns(w_depth)),
+        (b_depth, columns(b_depth)),
+        (w_project, whole(w_project)),
+        (b_project, whole(b_project)),
+    )
+    half = (plan.n_rows, count, plan.width)
+    return pl.pallas_call(
+        functools.partial(depth_kernel, plan),
+        grid=(steps,),
+        in_specs=[spec for _, spec in operands],
+        out_specs=[pl.BlockSpec(half, lambda i: (0, 0, 0))] * 2,
+        out_shape=[
+            jax.ShapeDtypeStruct(half, jnp.bfloat16),
+            jax.ShapeDtypeStruct(half, jnp.float32),
+        ],
+        scratch_shapes=[
+            pltpu.VMEM((plan.depth_h + 2, plan.depth_w + 2, SUBLANES, CHUNK), jnp.float32),
+            pltpu.VMEM((steps, plan.depth_h, count, CHUNK), jnp.bfloat16),
+        ],
+        compiler_params=pltpu.CompilerParams(vmem_limit_bytes=VMEM_BYTES),
+        cost_estimate=pl.CostEstimate(
+            flops=2 * x.size * own, bytes_accessed=2 * e.size, transcendentals=0
+        ),
+        name="deepen",
+    )(*[value for value, _ in operands])
+
+
+def attend_kernel(
+    plan, flag_ref, x_ref, gain_ref, wqkv_ref, wqkv_sib_ref, wo_ref, wo_sib_ref, bo_ref, bo_sib_ref,
+    out_ref, values, qkv, attended,
+):
+    sources, tokens, width = x_ref.shape
+    windows = tokens // SUBLANES
+    span = sources * SUBLANES
+    half = wo_ref.shape[0]
+    for source in range(sources):
+        values[:, source] = x_ref[source].astype(jnp.float32).reshape(windows, SUBLANES, width)
+    full = values[...].reshape(windows * span, width)
+    centred = full - jnp.mean(full, axis=-1, keepdims=True)
+    spread = jnp.mean(centred * centred, axis=-1, keepdims=True)
+    normed = (centred * lax.rsqrt(spread + 1e-05) * gain_ref[...]).astype(jnp.bfloat16)
+    for side, weight in enumerate((wqkv_ref, wqkv_sib_ref)):
+        for kind in range(3):
+            qkv[kind, :, side * half : (side + 1) * half] = jnp.dot(
+                normed, weight[:, kind * half : (kind + 1) * half], preferred_element_type=jnp.float32
+            ).astype(jnp.bfloat16)
+    heads = 128 // HEAD_DIM
+    lane = lax.broadcasted_iota(jnp.int32, (1, 128), 1) // HEAD_DIM
+    scale = HEAD_DIM ** (-0.5) * np.log2(np.e)
+    for window in range(windows):
+        rows = slice(window * span, (window + 1) * span)
+        for low in range(0, width, 128):
+            lanes = slice(low, low + 128)
+            query, keys, value = (qkv[kind, rows, lanes] for kind in range(3))
+            spread_query = jnp.concatenate(
+                [jnp.where(lane == h, query, jnp.zeros_like(query)) for h in range(heads)], axis=0
+            )
+            scores = lax.dot_general(
+                keys, spread_query, (((1,), (1,)), ((), ())), preferred_element_type=jnp.float32
+            )
+            top = jnp.max(scores, axis=0, keepdims=True)
+            powers = jnp.exp2((scores - top) * scale)
+            weights = powers * (1.0 / jnp.sum(powers, axis=0, keepdims=True))
+            mixed = lax.dot_general(
+                weights.astype(jnp.bfloat16), value, (((0,), (0,)), ((), ())),
+                preferred_element_type=jnp.float32,
+            )
+            chosen = mixed[:span]
+            for h in range(1, heads):
+                chosen = jnp.where(lane == h, mixed[h * span : (h + 1) * span], chosen)
+            attended[rows, lanes] = chosen.astype(jnp.bfloat16)
+    first = flag_ref[0] == 0
+    bias = jnp.concatenate(
+        [
+            jnp.where(first, bo_ref[...], bo_sib_ref[...]),
+            jnp.where(first, bo_sib_ref[...], bo_ref[...]),
+        ],
+        axis=1,
+    )
+    summed = jnp.dot(attended[:, :half], wo_ref[...], preferred_element_type=jnp.float32)
+    summed = summed + jnp.dot(attended[:, half:], wo_sib_ref[...], preferred_element_type=jnp.float32)
+    result = values[...] + (summed + bias).reshape(values.shape)
+    for target in range(sources):
+        part = result[:, target].reshape(tokens, width).astype(jnp.bfloat16)
+        for core in range(plan.n_ch):
+            out_ref[target, core] = part[:, core * half : (core + 1) * half]
+
+
+def attend_windows(plan, flags, arrived, ln_gain, w_qkv, w_qkv_sib, w_out, w_out_sib, b_out, b_out_sib):
+    sources, tokens, width = arrived.shape
+    windows = tokens // SUBLANES
+    half = w_out.shape[0]
+    operands = (arrived, ln_gain, w_qkv, w_qkv_sib, w_out, w_out_sib, b_out, b_out_sib)
+    return pl.pallas_call(
+        functools.partial(attend_kernel, plan),
+        in_specs=[pl.BlockSpec(memory_space=pltpu.SMEM)]
+        + [pl.BlockSpec(memory_space=pltpu.VMEM)] * len(operands),
+        out_specs=pl.BlockSpec(memory_space=pltpu.VMEM),
+        out_shape=jax.ShapeDtypeStruct((sources, plan.n_ch, tokens, half), jnp.bfloat16),
+        scratch_shapes=[
+            pltpu.VMEM((windows, sources, SUBLANES, width), jnp.float32),
+            pltpu.VMEM((3, sources * tokens, width), jnp.bfloat16),
+            pltpu.VMEM((sources * tokens, width), jnp.bfloat16),
+        ],
+        compiler_params=pltpu.CompilerParams(vmem_limit_bytes=VMEM_BYTES),
+        cost_estimate=pl.CostEstimate(
+            flops=8 * arrived.size * width, bytes_accessed=4 * arrived.size, transcendentals=0
+        ),
+        name="attend",
+    )(flags, *operands)
+
+
+def halo_rows(cells):
+    count = lax.axis_size("gy")
+    forward = [(i, i + 1) for i in range(count - 1)]
+    backward = [(target, source) for source, target in forward]
+    return lax.ppermute(cells[-1], "gy", forward), lax.ppermute(cells[0], "gy", backward)
+
+
+def halo_cols(cells, rows):
+    count = lax.axis_size("gx")
+    up, down = rows
+
+    def column(index):
+        parts = [up[None], cells, down[None]]
+        return jnp.concatenate(
+            [lax.dynamic_slice_in_dim(part, index, 1, axis=1)[:, 0] for part in parts], axis=0
+        )
+
+    last = cells.shape[1] - 1
+    if count == 2:
+        met = lax.ppermute(
+            column(jnp.where(lax.axis_index("gx") == 0, last, 0)), "gx", [(0, 1), (1, 0)]
+        )
+        return met, met
+    forward = [(i, i + 1) for i in range(count - 1)]
+    backward = [(target, source) for source, target in forward]
+    return lax.ppermute(column(last), "gx", forward), lax.ppermute(column(0), "gx", backward)
+
+
+def fast_device(
+    plan, cells, w_expand, b_expand, w_depth, b_depth, w_project, b_project, ln_gain, w_qkv, w_out, b_out
+):
+    n_rows, n_cols, n_ch = plan.n_rows, plan.n_cols, plan.n_ch
+    width = plan.width
+    own_y, own_x, own_c = (lax.axis_index(axis) for axis in ("gy", "gx", "ch"))
+    flags = jnp.stack(
+        [own_c, own_y > 0, own_y < n_rows - 1, own_x > 0, own_x < n_cols - 1]
+    ).astype(jnp.int32)
+    order = jnp.asarray(plan.order(), jnp.bfloat16)
+    swap = [(0, 1), (1, 0)]
+    rows = halo_rows(cells)
+    e, x = expand(plan, cells, w_expand, b_expand[None], order)
+    cols = halo_cols(cells, rows)
+    w_qkv = w_qkv.reshape(width, -1)
+    w_qkv_sib, w_out_sib, b_out_sib = (
+        lax.ppermute(value, "ch", swap) for value in (w_qkv, w_out, b_out[None])
+    )
+    sib, own = deepen(
+        plan, flags, e, x, rows, cols, w_expand, b_expand[None], w_depth.reshape(9, -1), b_depth[None],
+        w_project, b_project[None], order,
+    )
+    mixed = (own + lax.ppermute(sib, "ch", swap).astype(jnp.float32)).astype(jnp.bfloat16)
+    mixed = mixed.reshape(n_rows * n_cols, -1, width)
+    arrived = lax.all_to_all(mixed, ("gy", "gx"), 0, 0, tiled=True)
+    leaving = attend_windows(
+        plan, flags, arrived, ln_gain[None], w_qkv, w_qkv_sib, w_out, w_out_sib, b_out[None], b_out_sib
+    )
+    leaving = leaving.reshape((n_rows * n_cols * n_ch,) + leaving.shape[2:])
+    returned = lax.all_to_all(leaving, ("gy", "gx", "ch"), 0, 0, tiled=True)
+    returned = returned.reshape(
+        n_rows, n_cols, n_ch, SUBLANES, plan.outer_h, plan.outer_w, width // n_ch
+    )
+    return returned.transpose(4, 0, 2, 5, 1, 3, 6).reshape(cells.shape[0], cells.shape[1], -1)
+
+
+def per_device(cells, *rest):
+    plan = Plan(cells, *(lax.axis_size(axis) for axis in ("gy", "gx", "ch")))
+    if plan.fits:
+        return fast_device(plan, cells, *rest)
+    return general_device(cells, *rest)
+
+
 def solution(mesh):
     placed = (
         P(("grp", "gy"), "gx", None),

time: 174 us -> 73.9 us (0.42)
  blocking collectives: 59.3 us -> 18 us
  matrix products: 39.1 us -> 0 us
  waiting for transfers between devices: 35.5 us -> 16.3 us
  Pallas kernels: 0 us -> 13.7 us
  between operations: 13.4 us -> 0.27 us
  other arithmetic: 7.27 us -> 0.97 us
  starting transfers between devices: 11.3 us -> 15.4 us
    all_to_all x4 -> x1, blocking collectives: 59.3 us -> 18 us  [fast_device(): returned = lax.all_to_all(leaving, ('gy', 'gx', 'ch'), 0, 0, tiled=True)]
    dot_general x5 -> x0, matrix products: 34.1 us -> none  [the longest x1 16.1 us: per_device(): jnp.einsum('hwe,ec->hwc', depth, w_project, preferred_element_type=jnp.fl...]
    reduce_scatter x2 -> x0, waiting for transfers between devices: 17.8 us -> none  [the longest x1 9.89 us: per_device(): lax.psum_scatter(attention_terms.astype(jnp.bfloat16), 'ch', scatter_dime...]
    pallas_call x0 -> x3, Pallas kernels: none -> 13.7 us  [the longest x1 7.42 us: deepen(): pl.pallas_call(functools.partial(depth_kernel, plan), grid=(steps,), in_s...]
    all_to_all x0 -> x1, waiting for transfers between devices: none -> 11.5 us  [fast_device(): arrived = lax.all_to_all(mixed, ('gy', 'gx'), 0, 0, tiled=True)]
    all_gather x1 -> x0, waiting for transfers between devices: 7.28 us -> none  [per_device(): window_full = lax.all_gather(window_own, 'ch', axis=2, tiled=True)]
    all_to_all x0 -> x1, starting transfers between devices: none -> 5.8 us  [fast_device(): arrived = lax.all_to_all(mixed, ('gy', 'gx'), 0, 0, tiled=True)]
    ppermute x4 -> x7, waiting for transfers between devices: 10.5 us -> 4.77 us  [the longest x3 2.06 us: fast_device(): lax.ppermute(value, 'ch', swap)]
  transfers between devices with their start and end apart: 7 -> 8, of which waited for: 7 -> 4; matrix products, arithmetic and copies ran while one was open for 0% -> 2% of each run, Pallas kernels for 0% -> 4%
where the time goes in v1:
time: 73.9 us; the launch traced here: 73.4 us
  blocking collectives  18 us (24%)
  waiting for transfers between devices  16.3 us (22%)
  starting transfers between devices  15.4 us (21%)
  Pallas kernels  13.7 us (19%)
  local copies, waits for them, and re-layouts  8.84 us (12%)
  other arithmetic  0.97 us (1%)
    all_to_all x1, blocking collectives, fast_device(): returned = lax.all_to_all(leaving, ('gy', 'gx', 'ch'), 0, 0, tiled=True)  18 us
    all_to_all x1, waiting for transfers between devices, fast_device(): arrived = lax.all_to_all(mixed, ('gy', 'gx'), 0, 0, tiled=True)  11.5 us
    pallas_call x1, Pallas kernels, deepen(): pl.pallas_call(functools.partial(depth_kernel, plan), grid=(steps,), in_s...  7.42 us
    all_to_all x1, starting transfers between devices, fast_device(): arrived = lax.all_to_all(mixed, ('gy', 'gx'), 0, 0, tiled=True)  5.8 us
    unnamed x38, local copies, waits for them, and re-layouts  5.58 us
    ppermute x1, starting transfers between devices, halo_rows(): lax.ppermute(cells[-1], 'gy', forward)  5.56 us
    pallas_call x1, Pallas kernels, attend_windows(): pl.pallas_call(functools.partial(attend_kernel, plan), in_specs=[pl.Block...  3.56 us
    pallas_call x1, Pallas kernels, expand(): pl.pallas_call(expand_kernel, grid=(plan.depth_h // planes,), in_specs=[p...  2.67 us
  transfers between devices with their start and end apart: 8, of which 4 were waited for; matrix products, arithmetic and copies ran while one was open for 2% of the time, Pallas kernels for 4%

profile of v1, /device:TPU:0, one launch (start us, length us, event | category | flops | bytes accessed | tf_op | source)
XLA Modules:
  0.0 73.4 jit_solution(17718020495017718549)
XLA Ops:
  0.0 0.9 %slice_bitcast_fusion = (bf16[64,512]{1,0:T(8,128)(2,1)S(1)}, bf16[64,512]{1,0:T(8,128)(2,1)S(1)}) fusion(bf16[16,64,512]{2,1,0:T(8,128)(2,1)} %param.14), kind=kLoop, calls=%fused_computation.1 | loop fusion | bytes 262144 | tf_op jit(solution)/shard_map/squeeze | solution.py:462
  0.9 0.0 copy-start.17
  0.9 1.3 %collective-permute-start.1 = (bf16[64,512]{1,0:T(8,128)(2,1)S(1)}, bf16[64,512]{1,0:T(8,128)(2,1)S(1)}, u32[]{:S(2)}, u32[]{:S(2)}) collective-permute-start(bf16[64,512]{1,0:T(8,128)(2,1)S(1)} %get-tuple-element.13), channel_id=1, source_target_pairs={{4,0},{8,4},{12,8},{5,1},{9,5},{13,9},{6,2},{10,6},{14,10},{7,3},{... | collective-permute-start | bytes 196616 | tf_op jit(solution)/shard_map/ppermute | solution.py:462
  2.2 5.6 %collective-permute-start = (bf16[64,512]{1,0:T(8,128)(2,1)S(1)}, bf16[64,512]{1,0:T(8,128)(2,1)S(1)}, u32[]{:S(2)}, u32[]{:S(2)}) collective-permute-start(bf16[64,512]{1,0:T(8,128)(2,1)S(1)} %get-tuple-element.14), channel_id=1, source_target_pairs={{0,4},{4,8},{8,12},{1,5},{5,9},{9,13},{2,6},{6,10},{10,14},{3,7},{... | collective-permute-start | bytes 196616 | tf_op jit(solution)/shard_map/ppermute | solution.py:462
  7.8 0.9 %constant_dynamic-slice_fusion.1 = bf16[16,1,512]{2,1,0:T(2,128)(2,1)S(1)} fusion(bf16[16,64,512]{2,1,0:T(8,128)(2,1)} %param.14, s32[]{:T(128)S(6)} %select_n.4), kind=kLoop, calls=%fused_computation.6 | loop fusion | bytes 32772 | tf_op jit(solution)/shard_map/dynamic_slice | solution.py:472
  8.7 0.0 copy-start.5
  8.7 0.0 copy-start.7
  8.7 0.0 copy-start.8
  8.8 0.0 copy-start.10
  8.8 0.0 copy-start.11
  8.8 0.0 copy-start.12
  8.8 0.0 collective-permute-done.1.down_ref
  8.8 0.8 %collective-permute-done.up_ref = bf16[64,512]{1,0:T(8,128)(2,1)S(1)} collective-permute-done((bf16[64,512]{1,0:T(8,128)(2,1)S(1)}, bf16[64,512]{1,0:T(8,128)(2,1)S(1)}, u32[]{:S(2)}, u32[]{:S(2)}) %collective-permute-start) | collective-permute-done | bytes 65568 | tf_op jit(solution)/shard_map/ppermute | solution.py:462
  9.7 2.0 %collective-permute-start.2 = (bf16[18,512]{1,0:T(8,128)(2,1)S(1)}, bf16[18,512]{1,0:T(8,128)(2,1)S(1)}, u32[]{:S(2)}, u32[]{:S(2)}) collective-permute-start(bf16[18,512]{1,0:T(8,128)(2,1)S(1)} %pad_maximum_fusion), channel_id=1, source_target_pairs={{0,2},{2,0},{1,3},{3,1},{4,6},{6,4},{5,7},{7,5},{8,10},{10,8},{9,1... | collective-permute-start | bytes 55304 | tf_op jit(solution)/shard_map/ppermute | solution.py:477
  11.7 1.2 %copy-done.1 = bf16[512,1024]{1,0:T(8,128)(2,1)S(1)} copy-done((bf16[512,1024]{1,0:T(8,128)(2,1)S(1)}, bf16[512,1024]{1,0:T(8,128)(2,1)}, u32[]{:S(2)}) %copy-start.1) | copy-done | bytes 1048600
  12.9 0.8 %copy-done.4 = bf16[128,128]{1,0:T(8,128)(2,1)S(1)} copy-done((bf16[128,128]{1,0:T(8,128)(2,1)S(1)}, bf16[128,128]{1,0:T(8,128)(2,1)}, u32[]{:S(2)}) %copy-start.4) | copy-done | bytes 32792
  13.7 1.2 %copy-done.6 = bf16[16,64,512]{2,1,0:T(8,128)(2,1)S(1)} copy-done((bf16[16,64,512]{2,1,0:T(8,128)(2,1)S(1)}, bf16[16,64,512]{2,1,0:T(8,128)(2,1)}, u32[]{:S(2)}) %copy-start.6) | copy-done | bytes 1048600
  14.9 0.7 copy-done.9
  15.6 2.7 %expand.1 = (bf16[8,128,1024]{2,1,0:T(8,128)(2,1)S(1)}, bf16[8,128,512]{2,1,0:T(8,128)(2,1)S(1)}) custom-call(bf16[2,8,64,512]{3,2,1,0:T(8,128)(2,1)S(1)} %bitcast.25, bf16[512,1024]{1,0:T(8,128)(2,1)S(1)} %copy-done.1, f32[1,1024]{1,0:T(1,128)S(1)} %bitcast.26, bf16[128,128]{1,0:T(8,128)(2,1)S(1)} %copy-done.4), custom_call_target="tpu_custom_call" | custom-call | flops 1073741824 | bytes 4194304 | tf_op jit(solution)/shard_map/expand/pallas_call | solution.py:217
  18.3 0.0 copy-start
  18.3 1.3 %copy-done = bf16[8,128,1024]{2,1,0:T(8,128)(2,1)} copy-done((bf16[8,128,1024]{2,1,0:T(8,128)(2,1)}, bf16[8,128,1024]{2,1,0:T(8,128)(2,1)S(1)}, u32[]{:S(2)}) %copy-start) | copy-done | bytes 2097176
  19.6 0.1 stack.39.flag_ref
  19.7 0.0 collective-permute-done.2.left_ref.right_ref
  19.7 0.0 copy-done.8
  19.7 0.0 copy-done.10
  19.7 0.0 copy-done.11
  19.8 0.0 copy-done.12
  19.8 0.0 copy-done.2
  19.8 0.0 copy-done.3
  19.8 7.4 %deepen.1 = (bf16[4,128,512]{2,1,0:T(8,128)(2,1)S(1)}, f32[4,128,512]{2,1,0:T(8,128)S(1)}) custom-call(s32[5]{0:T(128)S(1)} %stack.39.flag_ref, bf16[8,128,1024]{2,1,0:T(8,128)(2,1)} %copy-done, bf16[8,128,512]{2,1,0:T(8,128)(2,1)S(1)} %get-tuple-element.10.x_ref, bf16[64,512]{1,0:T(8,128)(2,1)S(1)} %collective-permute-done.up_ref, ...), custom_call_target="tpu_custom_call" | custom-call | flops 1073741824 | bytes 2097152 | tf_op jit(solution)/shard_map/deepen/pallas_call | solution.py:352
  27.2 0.0 copy-start.16
  27.2 0.1 collective-permute-start.3
  27.3 1.9 %collective-permute-done.3 = bf16[4,128,512]{2,1,0:T(8,128)(2,1)S(1)} collective-permute-done((bf16[4,128,512]{2,1,0:T(8,128)(2,1)S(1)}, bf16[4,128,512]{2,1,0:T(8,128)(2,1)S(1)}, u32[]{:S(2)}, u32[]{:S(2)}) %collective-permute-start.3) | collective-permute-done | bytes 524320 | tf_op jit(solution)/shard_map/ppermute | solution.py:508
  29.2 1.0 %add_convert_fusion = bf16[4,128,512]{2,1,0:T(8,128)(2,1)} fusion(f32[4,128,512]{2,1,0:T(8,128)S(1)} %get-tuple-element.11, bf16[4,128,512]{2,1,0:T(8,128)(2,1)S(1)} %collective-permute-done.3), kind=kLoop, calls=%fused_computation | loop fusion | flops 786432 | bytes 2097152 | tf_op jit(solution)/shard_map/convert_element_type | solution.py:508
  30.2 5.8 %all-to-all-start = ((bf16[8,64,512]{2,1,0:T(8,128)(2,1)}), bf16[8,64,512]{2,1,0:T(8,128)(2,1)S(1)}, u32[]{:S(2)}, u32[]{:S(2)}) async-start(bf16[8,64,512]{2,1,0:T(8,128)(2,1)} %bitcast.12), calls=%async_computation | async-start | bytes 1048576 | tf_op jit(solution)/shard_map/all_to_all | solution.py:510
  36.0 0.3 copy.18
  36.3 0.3 copy.20.wqkv_ref
  36.5 0.1 collective-permute-start.4
  36.6 0.5 collective-permute-start.5
  37.1 0.1 collective-permute-start.6
  37.2 2.1 %collective-permute-done.6.bo_sib_ref = f32[1,256]{1,0:T(1,128)S(1)} collective-permute-done((f32[1,256]{1,0:T(1,128)S(1)}, f32[1,256]{1,0:T(1,128)S(1)}, u32[]{:S(2)}, u32[]{:S(2)}) %collective-permute-start.6) | collective-permute-done | bytes 1056 | tf_op jit(solution)/shard_map/ppermute | solution.py:502
  39.3 0.0 collective-permute-done.5.wo_sib_ref
  39.3 0.0 collective-permute-done.4.wqkv_sib_ref
  39.3 11.5 %all-to-all-done.x_ref = bf16[8,64,512]{2,1,0:T(8,128)(2,1)S(1)} async-done(((bf16[8,64,512]{2,1,0:T(8,128)(2,1)}), bf16[8,64,512]{2,1,0:T(8,128)(2,1)S(1)}, u32[]{:S(2)}, u32[]{:S(2)}) %all-to-all-start) | async-done | bytes 524320 | tf_op jit(solution)/shard_map/all_to_all | solution.py:510
  50.8 3.6 %attend.1 = bf16[8,2,64,256]{3,2,1,0:T(8,128)(2,1)S(1)} custom-call(s32[5]{0:T(128)S(1)} %stack.39.flag_ref, bf16[8,64,512]{2,1,0:T(8,128)(2,1)S(1)} %all-to-all-done.x_ref, f32[1,512]{1,0:T(1,128)S(1)} %bitcast.30, bf16[512,768]{1,0:T(8,128)(2,1)S(1)} %copy.20.wqkv_ref, bf16[512,768]{1,0:T(8,128)(2,1)S(1)} %collective-permute-done.4.wqkv_sib_ref, ...), custom_call_target="tpu_custom_call" | custom-call | flops 1073741824 | bytes 1048576 | tf_op jit(solution)/shard_map/attend/pallas_call | solution.py:439
  54.3 18.0 %all_to_all.10 = bf16[16,64,256]{2,1,0:T(8,128)(2,1)S(1)} all-to-all(bf16[16,64,256]{2,1,0:T(8,128)(2,1)S(1)} %bitcast.24), channel_id=1, replica_groups=mesh['grp'=2,'gy'=4,'gx'=2,'ch'=2] {'gy','gx','ch'}, dimensions={0} | all-to-all | bytes 1048576 | tf_op jit(solution)/shard_map/all_to_all | solution.py:515
  72.3 0.1 reshape.30
  72.5 0.9 %copy.21 = bf16[4,2,2,8,2,4,256]{6,3,1,5,2,0,4:T(8,128)(2,1)} copy(bf16[4,2,2,8,2,4,256]{6,5,4,3,2,1,0:T(4,128)(2,1)S(1)} %reshape.30) | data formatting | bytes 1048576 | tf_op jit(solution)/shard_map/reshape | solution.py:516
  (21 shorter events, 0.1 us)
Async XLA Ops:
  0.9 18.7 %copy-start.17 = (bf16[3,3,1024]{2,1,0:T(4,128)(2,1)S(1)}, bf16[3,3,1024]{2,1,0:T(4,128)(2,1)}, u32[]{:S(2)}) copy-start(bf16[3,3,1024]{2,1,0:T(4,128)(2,1)} %param.17) | copy-start | bytes 55300
  0.9 7.9 %collective-permute-start.1 = (bf16[64,512]{1,0:T(8,128)(2,1)S(1)}, bf16[64,512]{1,0:T(8,128)(2,1)S(1)}, u32[]{:S(2)}, u32[]{:S(2)}) collective-permute-start(bf16[64,512]{1,0:T(8,128)(2,1)S(1)} %get-tuple-element.13), channel_id=1, source_target_pairs={{4,0},{8,4},{12,8},{5,1},{9,5},{13,9},{6,2},{10,6},{14,10},{7,3},{... | collective-permute-start | bytes 196616 | tf_op jit(solution)/shard_map/ppermute | solution.py:462
  2.2 7.5 %collective-permute-start = (bf16[64,512]{1,0:T(8,128)(2,1)S(1)}, bf16[64,512]{1,0:T(8,128)(2,1)S(1)}, u32[]{:S(2)}, u32[]{:S(2)}) collective-permute-start(bf16[64,512]{1,0:T(8,128)(2,1)S(1)} %get-tuple-element.14), channel_id=1, source_target_pairs={{0,4},{4,8},{8,12},{1,5},{5,9},{9,13},{2,6},{6,10},{10,14},{3,7},{... | collective-permute-start | bytes 196616 | tf_op jit(solution)/shard_map/ppermute | solution.py:462
  8.7 11.0 %copy-start.5 = (bf16[128,128]{1,0:T(8,128)(2,1)S(1)}, bf16[128,128]{1,0:T(8,128)(2,1)}, u32[]{:S(2)}) copy-start(bf16[128,128]{1,0:T(8,128)(2,1)} %constant.27.clone.order_ref) | copy-start | bytes 98308
  8.7 11.0 %copy-start.7 = (bf16[80,18]{1,0:T(8,128)(2,1)S(1)}, bf16[80,18]{1,0:T(8,128)(2,1)}, u32[]{:S(2)}) copy-start(bf16[80,18]{1,0:T(8,128)(2,1)} %constant.28.clone.left_at_ref) | copy-start | bytes 8644
  8.7 11.0 %copy-start.8 = (bf16[80,18]{1,0:T(8,128)(2,1)S(1)}, bf16[80,18]{1,0:T(8,128)(2,1)}, u32[]{:S(2)}) copy-start(bf16[80,18]{1,0:T(8,128)(2,1)} %constant.29.clone.right_at_ref) | copy-start | bytes 8644
  8.8 11.0 %copy-start.10 = (f32[1024]{0:T(1024)S(1)}, f32[1024]{0:T(1024)}, u32[]{:S(2)}) copy-start(f32[1024]{0:T(1024)} %param.16) | copy-start | bytes 12292
  8.8 11.0 %copy-start.11 = (f32[1024]{0:T(1024)S(1)}, f32[1024]{0:T(1024)}, u32[]{:S(2)}) copy-start(f32[1024]{0:T(1024)} %param.18) | copy-start | bytes 12292
  8.8 11.0 %copy-start.12 = (f32[512]{0:T(512)S(1)}, f32[512]{0:T(512)}, u32[]{:S(2)}) copy-start(f32[512]{0:T(512)} %param.20) | copy-start | bytes 6148
  9.7 10.0 %collective-permute-start.2 = (bf16[18,512]{1,0:T(8,128)(2,1)S(1)}, bf16[18,512]{1,0:T(8,128)(2,1)S(1)}, u32[]{:S(2)}, u32[]{:S(2)}) collective-permute-start(bf16[18,512]{1,0:T(8,128)(2,1)S(1)} %pad_maximum_fusion), channel_id=1, source_target_pairs={{0,2},{2,0},{1,3},{3,1},{4,6},{6,4},{5,7},{7,5},{8,10},{10,8},{9,1... | collective-permute-start | bytes 55304 | tf_op jit(solution)/shard_map/ppermute | solution.py:477
  11.7 1.2 %copy-start.1 = (bf16[512,1024]{1,0:T(8,128)(2,1)S(1)}, bf16[512,1024]{1,0:T(8,128)(2,1)}, u32[]{:S(2)}) copy-start(bf16[512,1024]{1,0:T(8,128)(2,1)} %we_ref.1) | copy-start | bytes 3145732
  12.9 0.8 %copy-start.4 = (bf16[128,128]{1,0:T(8,128)(2,1)S(1)}, bf16[128,128]{1,0:T(8,128)(2,1)}, u32[]{:S(2)}) copy-start(bf16[128,128]{1,0:T(8,128)(2,1)} %constant.27.clone.order_ref) | copy-start | bytes 98308
  13.7 1.2 %copy-start.6 = (bf16[16,64,512]{2,1,0:T(8,128)(2,1)S(1)}, bf16[16,64,512]{2,1,0:T(8,128)(2,1)}, u32[]{:S(2)}) copy-start(bf16[16,64,512]{2,1,0:T(8,128)(2,1)} %param.14) | copy-start | bytes 3145732
  14.9 0.7 copy-start.9
  15.6 4.2 %copy-start.2 = (bf16[512,1024]{1,0:T(8,128)(2,1)S(1)}, bf16[512,1024]{1,0:T(8,128)(2,1)}, u32[]{:S(2)}) copy-start(bf16[512,1024]{1,0:T(8,128)(2,1)} %we_ref.1) | copy-start | bytes 3145732
  15.6 4.2 %copy-start.3 = (bf16[1024,512]{1,0:T(8,128)(2,1)S(1)}, bf16[1024,512]{1,0:T(8,128)(2,1)}, u32[]{:S(2)}) copy-start(bf16[1024,512]{1,0:T(8,128)(2,1)} %wp_ref.1) | copy-start | bytes 3145732
  18.3 1.3 %copy-start = (bf16[8,128,1024]{2,1,0:T(8,128)(2,1)}, bf16[8,128,1024]{2,1,0:T(8,128)(2,1)S(1)}, u32[]{:S(2)}) copy-start(bf16[8,128,1024]{2,1,0:T(8,128)(2,1)S(1)} %get-tuple-element.9.e_ref) | copy-start | bytes 6291460
  27.2 8.8 %copy-start.16 = (bf16[512,3,256]{2,0,1:T(8,128)(2,1)S(1)}, bf16[512,3,256]{2,0,1:T(8,128)(2,1)}, u32[]{:S(2)}) copy-start(bf16[512,3,256]{2,0,1:T(8,128)(2,1)} %param.22) | copy-start | bytes 2359300
  27.2 2.0 %collective-permute-start.3 = (bf16[4,128,512]{2,1,0:T(8,128)(2,1)S(1)}, bf16[4,128,512]{2,1,0:T(8,128)(2,1)S(1)}, u32[]{:S(2)}, u32[]{:S(2)}) collective-permute-start(bf16[4,128,512]{2,1,0:T(8,128)(2,1)S(1)} %get-tuple-element.12), channel_id=1, source_target_pairs={{0,1},{1,0},{2,3},{3,2},{4,5},{5,4},{6,7},{7,6},{8,9},{9,8},{10,11... | collective-permute-start | bytes 1572872 | tf_op jit(solution)/shard_map/ppermute | solution.py:508
  30.2 6.5 %copy-start.13 = (bf16[256,512]{1,0:T(8,128)(2,1)S(1)}, bf16[256,512]{1,0:T(8,128)(2,1)}, u32[]{:S(2)}) copy-start(bf16[256,512]{1,0:T(8,128)(2,1)} %wo_ref.1) | copy-start | bytes 786436
  30.2 7.0 %copy-start.15 = (f32[256]{0:T(256)S(1)}, f32[256]{0:T(256)}, u32[]{:S(2)}) copy-start(f32[256]{0:T(256)} %param.24) | copy-start | bytes 3076
  30.2 20.6 %copy-start.14 = (f32[512]{0:T(512)S(1)}, f32[512]{0:T(512)}, u32[]{:S(2)}) copy-start(f32[512]{0:T(512)} %param.21) | copy-start | bytes 6148
  30.2 20.6 %all-to-all-start = ((bf16[8,64,512]{2,1,0:T(8,128)(2,1)}), bf16[8,64,512]{2,1,0:T(8,128)(2,1)S(1)}, u32[]{:S(2)}, u32[]{:S(2)}) async-start(bf16[8,64,512]{2,1,0:T(8,128)(2,1)} %bitcast.12), calls=%async_computation | async-start | bytes 1048576 | tf_op jit(solution)/shard_map/all_to_all | solution.py:510
  36.5 2.7 %collective-permute-start.4 = (bf16[512,768]{1,0:T(8,128)(2,1)S(1)}, bf16[512,768]{1,0:T(8,128)(2,1)S(1)}, u32[]{:S(2)}, u32[]{:S(2)}) collective-permute-start(bf16[512,768]{1,0:T(8,128)(2,1)S(1)} %copy.20.wqkv_ref), channel_id=1, source_target_pairs={{0,1},{1,0},{2,3},{3,2},{4,5},{5,4},{6,7},{7,6},{8,9},{9,8},{10,11... | collective-permute-start | bytes 2359304 | tf_op jit(solution)/shard_map/ppermute | solution.py:502
  36.6 2.6 %collective-permute-start.5 = (bf16[256,512]{1,0:T(8,128)(2,1)S(1)}, bf16[256,512]{1,0:T(8,128)(2,1)S(1)}, u32[]{:S(2)}, u32[]{:S(2)}) collective-permute-start(bf16[256,512]{1,0:T(8,128)(2,1)S(1)} %copy-done.13), channel_id=1, source_target_pairs={{0,1},{1,0},{2,3},{3,2},{4,5},{5,4},{6,7},{7,6},{8,9},{9,8},{10,11... | collective-permute-start | bytes 786440 | tf_op jit(solution)/shard_map/ppermute | solution.py:502
  37.1 2.1 %collective-permute-start.6 = (f32[1,256]{1,0:T(1,128)S(1)}, f32[1,256]{1,0:T(1,128)S(1)}, u32[]{:S(2)}, u32[]{:S(2)}) collective-permute-start(f32[1,256]{1,0:T(1,128)S(1)} %bitcast.31), channel_id=1, source_target_pairs={{0,1},{1,0},{2,3},{3,2},{4,5},{5,4},{6,7},{7,6},{8,9},{9,8},{10,11... | collective-permute-start | bytes 3080 | tf_op jit(solution)/shard_map/ppermute | solution.py:502

commit v2 on v0

--- a/solution.py
+++ b/solution.py
@@ -1,7 +1,18 @@
+import functools
+
 import jax
 import jax.numpy as jnp
+import numpy as np
 from jax import lax
+from jax.experimental import pallas as pl
+from jax.experimental.pallas import tpu as pltpu
 from jax.sharding import PartitionSpec as P
+
+SUBLANES = 8
+CHUNK = 512
+VMEM_BYTES = 24 * 2**20
+EDGES_VMEM_BYTES = 61 * 2**20
+B_EXPAND, B_DEPTH, B_OUT, B_PROJECT, GAIN = (slice(row, row + 1) for row in range(9, 14))
 
 HEAD_DIM = 32
 GRID = 8
@@ -88,7 +99,7 @@
     return heads_out.reshape(window_count, tokens, own_width)
 
 
-def per_device(
+def general_device(
     cells, w_expand, b_expand, w_depth, b_depth, w_project, b_project, ln_gain, w_qkv, w_out, b_out
 ):
     tile_h, tile_w, width = cells.shape
@@ -143,6 +154,469 @@
     return join_order(returned)
 
 
+class Plan:
+    def __init__(self, cells, n_rows, n_cols, n_ch):
+        tile_h, tile_w, self.width = cells.shape
+        stride_h, stride_w = tile_h * n_rows // GRID, tile_w * n_cols // GRID
+        self.depth_h, self.depth_w = min(tile_h, stride_h), min(tile_w, stride_w)
+        self.outer_h, self.outer_w = tile_h // self.depth_h, tile_w // self.depth_w
+        self.n_rows, self.n_cols, self.n_ch = n_rows, n_cols, n_ch
+        self.span_w = self.depth_w // n_ch
+        self.half_h = self.depth_h // 2
+        self.fits = (
+            (n_rows, n_cols, n_ch) == (4, 2, 2)
+            and self.depth_h == stride_h
+            and self.depth_w == stride_w
+            and self.outer_h * self.outer_w == SUBLANES
+            and min(self.outer_h, self.outer_w) >= 2
+            and self.depth_h % n_rows == 0
+            and self.span_w % (2 * n_cols) == 0
+            and self.width % CHUNK == 0
+        )
+
+    def columns(self, shape, core):
+        token = lax.broadcasted_iota(jnp.int32, shape, 0)
+        slot, j = token // SUBLANES, token % self.outer_w
+        return token, j * self.depth_w + core * self.span_w + slot - 1
+
+    def order(self, core):
+        wide = self.outer_w * self.depth_w
+        shape = ((self.span_w + 2) * SUBLANES, self.outer_h * wide)
+        token, column = self.columns(shape, core)
+        place = token // self.outer_w % self.outer_h * wide + column
+        inside = (column >= 0) & (column < wide)
+        return one_hot(jnp.where(inside, place, -1))
+
+    def row_order(self, core):
+        shape = ((self.span_w + 2) * SUBLANES, self.outer_w * self.depth_w)
+        return one_hot(self.columns(shape, core)[1])
+
+    def column_order(self, part):
+        shape = ((self.half_h + 2) * SUBLANES, self.outer_h * self.depth_h + 2)
+        token = lax.broadcasted_iota(jnp.int32, shape, 0)
+        i, plane = token // self.outer_w % self.outer_h, token // SUBLANES
+        return one_hot(i * self.depth_h + part * self.half_h + plane)
+
+
+def one_hot(place):
+    return (lax.broadcasted_iota(jnp.int32, place.shape, 1) == place).astype(jnp.bfloat16)
+
+
+def gelu_erf(values):
+    return (0.5 * values) * (1.0 + lax.erf(values * 0.5**0.5))
+
+
+def in_vmem(count):
+    return [pl.BlockSpec(memory_space=pltpu.VMEM)] * count
+
+
+def grow(plan, source_ref, weight, small, e_ref):
+    slots = plan.span_w + 2
+    for low_a in range(0, plan.depth_h, plan.half_h):
+        planes = slice(low_a, low_a + plan.half_h)
+        source = source_ref[planes].reshape(-1, plan.width)
+        for low in range(0, weight.shape[1], CHUNK):
+            part = slice(low, low + CHUNK)
+            pre = jnp.dot(source, weight[:, part], preferred_element_type=jnp.float32)
+            e_ref[planes, :, part] = (
+                gelu_erf(pre + small[B_EXPAND, part])
+                .astype(jnp.bfloat16)
+                .reshape(plan.half_h, slots * SUBLANES, CHUNK)
+            )
+
+
+def expand_first_kernel(plan, flag_ref, cells_ref, w_ref, small_ref, e_ref, x_ref, ordered_ref):
+    order = plan.order(flag_ref[0])
+    for a in range(plan.depth_h):
+        block = cells_ref[:, a].reshape(-1, plan.width)
+        picked = jnp.dot(order, block, preferred_element_type=jnp.float32)
+        ordered_ref[a] = picked.astype(jnp.bfloat16)
+        x_ref[a] = picked[SUBLANES:-SUBLANES].astype(jnp.bfloat16)
+    grow(plan, ordered_ref, w_ref, small_ref, e_ref)
+
+
+def expand_first(plan, flags, cells, weight, small):
+    shaped = cells.reshape(plan.outer_h, plan.depth_h, -1, plan.width)
+    rows = (plan.span_w + 2) * SUBLANES
+    return pl.pallas_call(
+        functools.partial(expand_first_kernel, plan),
+        in_specs=[pl.BlockSpec(memory_space=pltpu.SMEM)] + in_vmem(3),
+        out_specs=in_vmem(3),
+        out_shape=[
+            jax.ShapeDtypeStruct((plan.depth_h, rows, weight.shape[1]), jnp.bfloat16),
+            jax.ShapeDtypeStruct((plan.depth_h, plan.span_w * SUBLANES, plan.width), jnp.bfloat16),
+            jax.ShapeDtypeStruct((plan.depth_h, rows, plan.width), jnp.bfloat16),
+        ],
+        compiler_params=pltpu.CompilerParams(vmem_limit_bytes=VMEM_BYTES),
+        cost_estimate=pl.CostEstimate(
+            flops=8 * cells.size * weight.shape[1], bytes_accessed=8 * cells.size, transcendentals=0
+        ),
+        name="expand_first",
+    )(flags, shaped, weight, small)
+
+
+def expand_second_kernel(plan, ordered_ref, w_ref, small_ref, *refs):
+    count = (len(refs) - 2) // 2
+    others, (e_ref, *kept), sems = refs[:count], refs[count:-1], refs[-1]
+    copies = [
+        pltpu.make_async_copy(*pair, sems.at[i]) for i, pair in enumerate(zip((w_ref, *others), kept))
+    ]
+    for copy in copies:
+        copy.start()
+    grow(plan, ordered_ref, w_ref, small_ref, e_ref)
+    for copy in copies:
+        copy.wait()
+
+
+def expand_second(plan, ordered, weight, small, others):
+    kept = weight, *others
+    return pl.pallas_call(
+        functools.partial(expand_second_kernel, plan),
+        in_specs=in_vmem(3) + [pl.BlockSpec(memory_space=pl.ANY)] * len(others),
+        out_specs=in_vmem(1 + len(kept)),
+        out_shape=[
+            jax.ShapeDtypeStruct((*ordered.shape[:2], weight.shape[1]), jnp.bfloat16),
+            *(jax.ShapeDtypeStruct(v.shape, v.dtype) for v in kept),
+        ],
+        scratch_shapes=[pltpu.SemaphoreType.DMA((len(kept),))],
+        compiler_params=pltpu.CompilerParams(vmem_limit_bytes=VMEM_BYTES),
+        cost_estimate=pl.CostEstimate(
+            flops=2 * ordered.size * weight.shape[1], bytes_accessed=4 * ordered.size, transcendentals=0
+        ),
+        name="expand_second",
+    )(ordered, weight, small, *others)
+
+
+def deepen_kernel(
+    plan, targets, flag_ref, e_own_ref, e_sib_ref, x_ref, up_ref, down_ref, beside_ref, we_ref, we_sib_ref,
+    small_ref, small_sib_ref, wp_ref, wp_sib_ref, *rest,
+):
+    *outs, held, deep, mixed = rest[-len(targets) - 3 :]
+    core, up, down, left, right, own_y, own_x = (flag_ref[i] for i in range(7))
+    far = targets[0][0] // 2
+    part = (own_y // 2) ^ far
+    base = part * plan.half_h
+    planes, slots, outer_w = plan.half_h + 2, plan.span_w + 2, plan.outer_w
+    own = we_ref.shape[1]
+    row = lax.broadcasted_iota(jnp.int32, (1, SUBLANES, CHUNK), 1)
+    plane = lax.broadcasted_iota(jnp.int32, (planes, SUBLANES, CHUNK), 0)
+    at = lax.broadcasted_iota(jnp.int32, (planes, SUBLANES, CHUNK), 1)
+    first = part == 0
+
+    edge = jnp.where(first, up, down).astype(jnp.float32)
+    beside = jnp.where(core == 0, left, right).astype(jnp.float32)
+    side_mask = beside * jnp.where(
+        (plane == part * (planes - 1)) & (at // outer_w == part * (plan.outer_h - 1)), edge, 1.0
+    )
+    low_rows = jnp.where(first, outer_w, 0)
+    high_rows = outer_w - low_rows
+    at_side = row % outer_w == core * (outer_w - 1)
+    halo_cells = jnp.where(first, up_ref[...], down_ref[...])
+    halo_cells = jnp.dot(
+        plan.row_order(core), halo_cells, preferred_element_type=jnp.float32
+    ).astype(jnp.bfloat16)
+    side_cells = jnp.dot(
+        plan.column_order(part), beside_ref[...], preferred_element_type=jnp.float32
+    ).astype(jnp.bfloat16)
+    outside = jnp.concatenate([halo_cells, side_cells], axis=0)
+    before = lax.rem(base + plan.depth_h - 1, plan.depth_h)
+    after = lax.rem(base + plan.half_h, plan.depth_h)
+
+    sides = (e_own_ref, we_ref, small_ref), (e_sib_ref, we_sib_ref, small_sib_ref)
+    for side, (e_ref, we, small) in enumerate(sides):
+        for low in range(0, own, CHUNK):
+            lanes = slice(low, low + CHUNK)
+            pre = jnp.dot(outside, we[:, lanes], preferred_element_type=jnp.float32)
+            grown = gelu_erf(pre + small[B_EXPAND, lanes])
+            halo = grown[: slots * SUBLANES].reshape(slots, SUBLANES, CHUNK) * edge
+            beside_cells = grown[slots * SUBLANES :].reshape(planes, SUBLANES, CHUNK) * side_mask
+
+            def plane_of(index):
+                return e_ref[index, :, lanes].astype(jnp.float32).reshape(slots, SUBLANES, CHUNK)
+
+            for p in range(1, planes - 1):
+                held[p] = plane_of(base + p - 1)
+            values = plane_of(before)
+            held[0] = jnp.where(row < low_rows, halo, pltpu.roll(values, low_rows, 1))
+            values = plane_of(after)
+            held[planes - 1] = jnp.where(
+                row >= SUBLANES - high_rows,
+                halo,
+                pltpu.roll(values, lax.rem(SUBLANES - high_rows, SUBLANES), 1),
+            )
+            slot = core * (slots - 1)
+            held[:, slot] = jnp.where(at_side, beside_cells, held[:, slot])
+            for lane in range(0, CHUNK, 128):
+                here = slice(lane, lane + 128)
+                now = slice(low + lane, low + lane + 128)
+                for a in range(plan.half_h):
+                    total = jnp.broadcast_to(
+                        small[B_DEPTH, now], (plan.span_w, SUBLANES, 128)
+                    )
+                    for di in range(3):
+                        for dj in range(3):
+                            tap = small[3 * di + dj : 3 * di + dj + 1, now]
+                            total = total + held[a + di, dj : dj + plan.span_w, :, here] * tap
+                    deep[a, :, side * own + low + lane : side * own + low + lane + 128] = (
+                        gelu_erf(total).astype(jnp.bfloat16).reshape(-1, 128)
+                    )
+    source = deep[...].reshape(-1, 2 * own)
+    total = jnp.dot(source[:, :own], wp_ref[...], preferred_element_type=jnp.float32)
+    total = total + jnp.dot(source[:, own:], wp_sib_ref[...], preferred_element_type=jnp.float32)
+    residual = x_ref[pl.ds(base, plan.half_h)].astype(jnp.float32) + small_ref[B_PROJECT, : plan.width]
+    mixed[...] = (total.reshape(residual.shape) + residual).reshape(mixed.shape)
+    planes_each = plan.depth_h // plan.n_rows
+    rows = plan.span_w // plan.n_cols * SUBLANES
+    for out, (dy, dx) in zip(outs, targets):
+        block = (own_y ^ dy) & 1
+        column = own_x ^ dx
+        for k in range(planes_each):
+            out[k * rows : (k + 1) * rows] = mixed[block * planes_each + k, column].astype(jnp.bfloat16)
+
+
+def deepen(plan, targets, flags, e, x, rows, cols, weights, after):
+    own = weights[0].shape[1]
+    planes, slots = plan.half_h + 2, plan.span_w + 2
+    tokens = plan.span_w * SUBLANES
+    message = (plan.depth_h // plan.n_rows * (tokens // plan.n_cols), plan.width)
+    operands = (*e, x, *rows, cols, *weights)
+    return pl.pallas_call(
+        functools.partial(deepen_kernel, plan, targets),
+        in_specs=[pl.BlockSpec(memory_space=pltpu.SMEM)]
+        + in_vmem(len(operands))
+        + [pl.BlockSpec(memory_space=pl.ANY)] * len(after),
+        out_specs=in_vmem(len(targets)),
+        out_shape=[jax.ShapeDtypeStruct(message, jnp.bfloat16)] * len(targets),
+        scratch_shapes=[
+            pltpu.VMEM((planes, slots, SUBLANES, CHUNK), jnp.float32),
+            pltpu.VMEM((plan.half_h, tokens, 2 * own), jnp.bfloat16),
+            pltpu.VMEM((plan.half_h, plan.n_cols, tokens // plan.n_cols, plan.width), jnp.float32),
+        ],
+        compiler_params=pltpu.CompilerParams(vmem_limit_bytes=VMEM_BYTES),
+        cost_estimate=pl.CostEstimate(
+            flops=2 * x.size * own, bytes_accessed=4 * e[0].size, transcendentals=0
+        ),
+        name="deepen",
+    )(flags, *operands, *after)
+
+
+def attend_kernel(
+    plan, targets, flag_ref, wqkv_ref, wqkv_sib_ref, wo_ref, wo_sib_ref, small_ref, small_sib_ref, *rest
+):
+    sources = len(targets)
+    xs, (out_ref, values, qkv, attended) = rest[:sources], rest[sources:]
+    tokens, width = xs[0].shape
+    windows = tokens // SUBLANES
+    span = sources * SUBLANES
+    half = wo_ref.shape[0]
+    for source in range(sources):
+        values[:, source] = xs[source][...].astype(jnp.float32).reshape(windows, SUBLANES, width)
+    full = values[...].reshape(windows * span, width)
+    centred = full - jnp.mean(full, axis=-1, keepdims=True)
+    spread = jnp.mean(centred * centred, axis=-1, keepdims=True)
+    normed = (centred * lax.rsqrt(spread + 1e-05) * small_ref[GAIN, :width]).astype(jnp.bfloat16)
+    for side, weight in enumerate((wqkv_ref, wqkv_sib_ref)):
+        for kind in range(3):
+            qkv[kind, :, side * half : (side + 1) * half] = jnp.dot(
+                normed, weight[kind], preferred_element_type=jnp.float32
+            ).astype(jnp.bfloat16)
+    heads = 128 // HEAD_DIM
+    lane = lax.broadcasted_iota(jnp.int32, (1, 128), 1) // HEAD_DIM
+    scale = HEAD_DIM ** (-0.5) * np.log2(np.e)
+    for window in range(windows):
+        rows = slice(window * span, (window + 1) * span)
+        for low in range(0, width, 128):
+            lanes = slice(low, low + 128)
+            query, keys, value = (qkv[kind, rows, lanes] for kind in range(3))
+            spread_query = jnp.concatenate(
+                [jnp.where(lane == h, query, jnp.zeros_like(query)) for h in range(heads)], axis=0
+            )
+            scores = lax.dot_general(
+                keys, spread_query, (((1,), (1,)), ((), ())), preferred_element_type=jnp.float32
+            )
+            top = jnp.max(scores, axis=0, keepdims=True)
+            powers = jnp.exp2((scores - top) * scale)
+            weights = powers * (1.0 / jnp.sum(powers, axis=0, keepdims=True))
+            mixed = lax.dot_general(
+                weights.astype(jnp.bfloat16), value, (((0,), (0,)), ((), ())),
+                preferred_element_type=jnp.float32,
+            )
+            chosen = mixed[:span]
+            for h in range(1, heads):
+                chosen = jnp.where(lane == h, mixed[h * span : (h + 1) * span], chosen)
+            attended[rows, lanes] = chosen.astype(jnp.bfloat16)
+    first = flag_ref[0] == 0
+    bias = jnp.concatenate(
+        [
+            jnp.where(first, small_ref[B_OUT, :half], small_sib_ref[B_OUT, :half]),
+            jnp.where(first, small_sib_ref[B_OUT, :half], small_ref[B_OUT, :half]),
+        ],
+        axis=1,
+    )
+    summed = jnp.dot(attended[:, :half], wo_ref[...], preferred_element_type=jnp.float32)
+    summed = summed + jnp.dot(attended[:, half:], wo_sib_ref[...], preferred_element_type=jnp.float32)
+    result = values[...] + (summed + bias).reshape(values.shape)
+    for source, (dy, dx) in enumerate(targets):
+        part = result[:, source].reshape(tokens, width).astype(jnp.bfloat16)
+        target = (flag_ref[5] ^ dy) * plan.n_cols + (flag_ref[6] ^ dx)
+        for core in range(plan.n_ch):
+            out_ref[target, core] = part[:, core * half : (core + 1) * half]
+
+
+def attend_windows(plan, targets, flags, arrived, weights):
+    tokens, width = arrived[0].shape
+    sources = len(targets)
+    windows = tokens // SUBLANES
+    half = width // plan.n_ch
+    operands = (*weights, *arrived)
+    return pl.pallas_call(
+        functools.partial(attend_kernel, plan, targets),
+        in_specs=[pl.BlockSpec(memory_space=pltpu.SMEM)] + in_vmem(len(operands)),
+        out_specs=pl.BlockSpec(memory_space=pltpu.VMEM),
+        out_shape=jax.ShapeDtypeStruct((sources, plan.n_ch, tokens, half), jnp.bfloat16),
+        scratch_shapes=[
+            pltpu.VMEM((windows, sources, SUBLANES, width), jnp.float32),
+            pltpu.VMEM((3, sources * tokens, width), jnp.bfloat16),
+            pltpu.VMEM((sources * tokens, width), jnp.bfloat16),
+        ],
+        compiler_params=pltpu.CompilerParams(vmem_limit_bytes=VMEM_BYTES),
+        cost_estimate=pl.CostEstimate(
+            flops=8 * sources * tokens * width * width, bytes_accessed=4 * width * width, transcendentals=0
+        ),
+        name="attend",
+    )(flags, *operands)
+
+
+def edges_kernel(group, column_ref, cells_hbm, taps_hbm, *refs):
+    count = (len(refs) - 6) // 2
+    vectors_hbm, (top_ref, bottom_ref, side_ref, small_ref, held, taps), (*vectors, sems) = (
+        refs[:count], refs[count : count + 6], refs[count + 6 :]
+    )
+    rows, width = cells_hbm.shape[0], cells_hbm.shape[2]
+    column = column_ref[0]
+    start = pl.multiple_of(column // group * group, group)
+    pairs = [
+        (cells_hbm.at[0], top_ref),
+        (cells_hbm.at[rows - 1], bottom_ref),
+        (cells_hbm.at[:, pl.ds(start, group)], held),
+        (taps_hbm, taps),
+        *zip(vectors_hbm, vectors),
+    ]
+    copies = [pltpu.make_async_copy(*pair, sems.at[i]) for i, pair in enumerate(pairs)]
+    for copy in copies:
+        copy.start()
+    shape = (rows, rows * group)
+    pick = one_hot(lax.broadcasted_iota(jnp.int32, shape, 0) * group + (column - start))
+    small_ref[...] = jnp.zeros_like(small_ref)
+    for copy in copies:
+        copy.wait()
+    side_ref[...] = jnp.dot(
+        pick, held[...].reshape(rows * group, width), preferred_element_type=jnp.float32
+    ).astype(jnp.bfloat16)
+    for i in range(3):
+        small_ref[3 * i : 3 * i + 3] = taps[i].astype(jnp.float32)
+    for i, vector in enumerate(vectors):
+        small_ref[9 + i : 10 + i, : vector.shape[1]] = vector[...]
+
+
+def edges(cells, column, w_depth, vectors):
+    rows, cols, width = cells.shape
+    group = 2 * SUBLANES
+    operands = (cells, w_depth, *vectors)
+    return pl.pallas_call(
+        functools.partial(edges_kernel, group),
+        in_specs=[pl.BlockSpec(memory_space=pltpu.SMEM)]
+        + [pl.BlockSpec(memory_space=pltpu.HBM)] * len(operands),
+        out_specs=in_vmem(4),
+        out_shape=[jax.ShapeDtypeStruct((count, width), cells.dtype) for count in (cols, cols, rows)]
+        + [jax.ShapeDtypeStruct((group, w_depth.shape[2]), jnp.float32)],
+        scratch_shapes=[
+            pltpu.VMEM((rows, group, width), cells.dtype),
+            *(pltpu.VMEM(v.shape, v.dtype) for v in operands[1:]),
+            pltpu.SemaphoreType.DMA((len(operands) + 2,)),
+        ],
+        compiler_params=pltpu.CompilerParams(vmem_limit_bytes=EDGES_VMEM_BYTES),
+        name="edges",
+    )(column[None], *operands)
+
+
+def halo_rows(top, bottom):
+    count = lax.axis_size("gy")
+    forward = [(i, i + 1) for i in range(count - 1)]
+    backward = [(target, source) for source, target in forward]
+    return lax.ppermute(bottom, "gy", forward), lax.ppermute(top, "gy", backward)
+
+
+def halo_column(column, rows, index):
+    above, below = (lax.dynamic_slice_in_dim(row, index, 1, axis=0) for row in rows)
+    return lax.ppermute(jnp.concatenate([above, column, below], axis=0), "gx", [(0, 1), (1, 0)])
+
+
+def send_to(value, dy, dx):
+    n_rows, n_cols = lax.axis_size("gy"), lax.axis_size("gx")
+    pairs = [
+        (y * n_cols + x, (y ^ dy) * n_cols + (x ^ dx)) for y in range(n_rows) for x in range(n_cols)
+    ]
+    return lax.ppermute(value, ("gy", "gx"), pairs)
+
+
+def fast_device(
+    plan, cells, w_expand, b_expand, w_depth, b_depth, w_project, b_project, ln_gain, w_qkv, w_out, b_out
+):
+    n_rows, n_cols, n_ch = plan.n_rows, plan.n_cols, plan.n_ch
+    width = plan.width
+    own_y, own_x, own_c = (lax.axis_index(axis) for axis in ("gy", "gx", "ch"))
+    flags = jnp.stack(
+        [own_c, own_y > 0, own_y < n_rows - 1, own_x > 0, own_x < n_cols - 1, own_y, own_x]
+    ).astype(jnp.int32)
+    index = jnp.where(own_x == 0, cells.shape[1] - 1, 0)
+    vectors = tuple(v[None] for v in (b_expand, b_depth, b_out, b_project, ln_gain))
+    top, bottom, column, small = edges(cells, index, w_depth, vectors)
+    top, w_expand, w_project = lax.optimization_barrier((top, w_expand, w_project))
+    rows = halo_rows(top, bottom)
+
+    def both(value):
+        return value, lax.ppermute(value, "ch", [(0, 1), (1, 0)])
+
+    w_expand, w_project, small = both(w_expand), both(w_project), both(small)
+    flags, w_project_sib = lax.optimization_barrier((flags, w_project[1]))
+    e_sib, x, ordered = expand_first(plan, flags, cells, w_expand[1], small[1])
+    e_own, *kept = expand_second(
+        plan, ordered, w_expand[0], small[0], (w_project[0], w_qkv.transpose(1, 0, 2), w_out)
+    )
+    *rows, x, e_own = lax.optimization_barrier((*rows, x, e_own))
+    e = e_own, e_sib
+    cols = halo_column(column, rows, index)
+    cols, w_qkv, w_out = lax.optimization_barrier((cols, *kept[2:]))
+    w_qkv, w_out = both(w_qkv), both(w_out)
+    weights = (kept[0], w_expand[1], *small, kept[1], w_project_sib)
+    far = [(dy, dx) for dy in (2, 3) for dx in (0, 1)]
+    near = [(1, 0), (1, 1), (0, 1), (0, 0)]
+    early = deepen(plan, far, flags, e, x, rows, cols, weights, ())
+    *early, w_qkv_sib, w_out_sib = lax.optimization_barrier((*early, w_qkv[1], w_out[1]))
+    w_qkv, w_out = (w_qkv[0], w_qkv_sib), (w_out[0], w_out_sib)
+    arrived = [send_to(value, *target) for value, target in zip(early, far)]
+    late = deepen(plan, near, flags, e, x, rows, cols, weights, early)
+    *late, arrived[0] = lax.optimization_barrier((*late, arrived[0]))
+    arrived = [send_to(value, *target) for value, target in zip(late[:-1], near)] + [late[-1], *arrived]
+    leaving = attend_windows(
+        plan, near + far, flags, arrived, (*w_qkv, *w_out, *small)
+    )
+    leaving = leaving.reshape((n_rows * n_cols * n_ch,) + leaving.shape[2:])
+    returned = lax.all_to_all(leaving, ("gy", "gx", "ch"), 0, 0, tiled=True)
+    returned = returned.reshape(
+        n_rows, n_cols, n_ch, plan.depth_h // n_rows, plan.span_w // n_cols, plan.outer_h, plan.outer_w, -1
+    )
+    return returned.transpose(5, 0, 3, 6, 2, 1, 4, 7).reshape(cells.shape[0], cells.shape[1], -1)
+
+
+def per_device(cells, *rest):
+    plan = Plan(cells, *(lax.axis_size(axis) for axis in ("gy", "gx", "ch")))
+    if plan.fits:
+        return fast_device(plan, cells, *rest)
+    return general_device(cells, *rest)
+
+
 def solution(mesh):
     placed = (
         P(("grp", "gy"), "gx", None),

time: 174 us -> 65.8 us (0.38)
  blocking collectives: 59.3 us -> 19.5 us
  matrix products: 39.1 us -> 0 us
  waiting for transfers between devices: 35.5 us -> 6.47 us
  Pallas kernels: 0 us -> 16 us
  between operations: 13.4 us -> 0.24 us
  starting transfers between devices: 11.3 us -> 20.7 us
  other arithmetic: 7.27 us -> 0.02 us
  local copies, waits for them, and re-layouts: 7.33 us -> 2.65 us
    all_to_all x4 -> x1, blocking collectives: 59.3 us -> 19.5 us  [fast_device(): returned = lax.all_to_all(leaving, ('gy', 'gx', 'ch'), 0, 0, tiled=True)]
    dot_general x5 -> x0, matrix products: 34.1 us -> none  [the longest x1 16.1 us: per_device(): jnp.einsum('hwe,ec->hwc', depth, w_project, preferred_element_type=jnp.fl...]
    reduce_scatter x2 -> x0, waiting for transfers between devices: 17.8 us -> none  [the longest x1 9.89 us: per_device(): lax.psum_scatter(attention_terms.astype(jnp.bfloat16), 'ch', scatter_dime...]
    pallas_call x0 -> x6, Pallas kernels: none -> 16 us  [the longest x2 7.36 us: deepen(): pl.pallas_call(functools.partial(deepen_kernel, plan, targets), in_specs=...]
    ppermute x4 -> x15, starting transfers between devices: 11.1 us -> 20.7 us  [the longest x7 11.7 us: send_to(): return lax.ppermute(value, ('gy', 'gx'), pairs)]
    all_gather x1 -> x0, waiting for transfers between devices: 7.28 us -> none  [per_device(): window_full = lax.all_gather(window_own, 'ch', axis=2, tiled=True)]
    sub x1 -> x0, matrix products: 4.92 us -> none  [attend(): weights = jax.nn.softmax(scores, axis=-1).astype(jnp.bfloat16)]
    ppermute x4 -> x15, waiting for transfers between devices: 10.5 us -> 6.47 us  [the longest x7 3.71 us: send_to(): return lax.ppermute(value, ('gy', 'gx'), pairs)]
  transfers between devices with their start and end apart: 7 -> 15, of which waited for: 7 -> 5; matrix products, arithmetic and copies ran while one was open for 0% -> 0% of each run, Pallas kernels for 0% -> 16%
where the time goes in v2:
time: 65.8 us; the launch traced here: 65.6 us
  starting transfers between devices  20.7 us (31%)
  blocking collectives  19.5 us (30%)
  Pallas kernels  16 us (24%)
  waiting for transfers between devices  6.47 us (10%)
  local copies, waits for them, and re-layouts  2.65 us (4%)
    all_to_all x1, blocking collectives, fast_device(): returned = lax.all_to_all(leaving, ('gy', 'gx', 'ch'), 0, 0, tiled=True)  19.5 us
    ppermute x7, starting transfers between devices, send_to(): return lax.ppermute(value, ('gy', 'gx'), pairs)  11.7 us
    pallas_call x2, Pallas kernels, deepen(): pl.pallas_call(functools.partial(deepen_kernel, plan, targets), in_specs=...  7.36 us
    ppermute x1, starting transfers between devices, halo_rows(): lax.ppermute(bottom, 'gy', forward)  4.55 us
    ppermute x7, waiting for transfers between devices, send_to(): return lax.ppermute(value, ('gy', 'gx'), pairs)  3.71 us
    pallas_call x1, Pallas kernels, attend_windows(): pl.pallas_call(functools.partial(attend_kernel, plan, targets), in_specs=...  3.59 us
    ppermute x1, waiting for transfers between devices, halo_column(): lax.ppermute(jnp.concatenate([above, column, below], axis=0), 'gx', [(0,...  2.34 us
    pallas_call x1, Pallas kernels, edges(): pl.pallas_call(functools.partial(edges_kernel, group), in_specs=[pl.Block...  1.88 us
  transfers between devices with their start and end apart: 15, of which 5 were waited for; matrix products, arithmetic and copies ran while one was open for 0% of the time, Pallas kernels for 16%

profile of v2, /device:TPU:0, one launch (start us, length us, event | category | flops | bytes accessed | tf_op | source)
XLA Modules:
  0.0 65.6 jit_solution(77602725099147442)
XLA Ops:
  0.0 1.9 %edges.1 = (bf16[64,512]{1,0:T(8,128)(2,1)}, bf16[64,512]{1,0:T(8,128)(2,1)}, bf16[16,512]{1,0:T(8,128)(2,1)}, f32[16,1024]{1,0:T(8,128)}) custom-call(s32[1]{0:T(128)} %bitcast.7.column_ref, bf16[16,64,512]{2,1,0:T(8,128)(2,1)} %cells_hbm.1, bf16[3,3,1024]{2,1,0:T(4,128)(2,1)} %taps_hbm.1, f32[1,1024]{1,0:T(1,128)} %bitcast.23, f32[1,1024]{1,0:T(1,128)} %bitcast.24, ...), custom_call_target="tpu_custom_call" | custom-call | tf_op jit(solution)/shard_map/edges/pallas_call | solution.py:526
  1.9 0.5 collective-permute-start
  2.4 0.1 collective-permute-start.3
  2.5 0.4 collective-permute-start.4
  2.9 4.5 %collective-permute-start.1 = (bf16[64,512]{1,0:T(8,128)(2,1)}, bf16[64,512]{1,0:T(8,128)(2,1)S(1)}, u32[]{:S(2)}, u32[]{:S(2)}) collective-permute-start(bf16[64,512]{1,0:T(8,128)(2,1)} %get-tuple-element.51), channel_id=1, source_target_pairs={{0,4},{4,8},{8,12},{1,5},{5,9},{9,13},{2,6},{6,10},{10,14},{3,7},{... | collective-permute-start | bytes 196616 | tf_op jit(solution)/shard_map/ppermute | solution.py:547
  7.5 1.3 %collective-permute-start.2 = (bf16[64,512]{1,0:T(8,128)(2,1)}, bf16[64,512]{1,0:T(8,128)(2,1)S(1)}, u32[]{:S(2)}, u32[]{:S(2)}) collective-permute-start(bf16[64,512]{1,0:T(8,128)(2,1)} %get-tuple-element.52), channel_id=1, source_target_pairs={{4,0},{8,4},{12,8},{5,1},{9,5},{13,9},{6,2},{10,6},{14,10},{7,3},{... | collective-permute-start | bytes 196616 | tf_op jit(solution)/shard_map/ppermute | solution.py:547
  8.8 0.1 stack.47.flag_ref
  8.9 0.0 collective-permute-done.wp_sib_ref
  8.9 0.0 collective-permute-done.4.small_ref.small_sib_ref
  8.9 0.0 collective-permute-done.3.w_ref.we_sib_ref
  8.9 0.0 copy-start
  8.9 1.2 %copy-done = bf16[16,64,512]{2,1,0:T(8,128)(2,1)S(1)} copy-done((bf16[16,64,512]{2,1,0:T(8,128)(2,1)S(1)}, bf16[16,64,512]{2,1,0:T(8,128)(2,1)}, u32[]{:S(2)}) %copy-start) | copy-done | bytes 1048600
  10.1 0.0 copy-start.5
  10.1 1.8 %expand_first.1 = (bf16[8,80,1024]{2,1,0:T(8,128)(2,1)S(1)}, bf16[8,64,512]{2,1,0:T(8,128)(2,1)S(1)}, bf16[8,80,512]{2,1,0:T(8,128)(2,1)S(1)}) custom-call(s32[7]{0:T(128)S(1)} %stack.47.flag_ref, bf16[2,8,64,512]{3,2,1,0:T(8,128)(2,1)S(1)} %bitcast.19, bf16[512,1024]{1,0:T(8,128)(2,1)S(1)} %collective-permute-done.3.w_ref.we_sib_ref, ...), custom_call_target="tpu_custom_call" | custom-call | flops 4294967296 | bytes 4194304 | tf_op jit(solution)/shard_map/expand_first/pallas_call | solution.py:241
  12.0 0.0 copy-done.1
  12.0 0.0 copy-done.2
  12.0 0.0 copy-done.3
  12.0 0.0 copy-done.4
  12.0 1.4 %expand_second.1 = (bf16[8,80,1024]{2,1,0:T(8,128)(2,1)S(1)}, bf16[512,1024]{1,0:T(8,128)(2,1)S(1)}, bf16[1024,512]{1,0:T(8,128)(2,1)S(1)}, bf16[3,512,256]{2,1,0:T(8,128)(2,1)S(1)}, bf16[256,512]{1,0:T(8,128)(2,1)S(1)}) custom-call(bf16[8,80,512]{2,1,0:T(8,128)(2,1)S(1)} %get-tuple-element.56.ordered_ref, bf16[512,1024]{1,0:T(8,128)(2,1)S(1)} %copy-done.1, ...), custom_call_target="tpu_custom_call" | custom-call | flops 671088640 | bytes 1310720 | tf_op jit(solution)/shard_map/expand_second/pallas_call | solution.py:273
  13.4 0.0 collective-permute-done.1.up_ref
  13.4 0.4 collective-permute-done.2.down_ref
  13.9 1.6 %collective-permute-start.5 = (bf16[18,512]{1,0:T(8,128)(2,1)S(1)}, bf16[18,512]{1,0:T(8,128)(2,1)S(1)}, u32[]{:S(2)}, u32[]{:S(2)}) collective-permute-start(bf16[18,512]{1,0:T(8,128)(2,1)S(1)} %pad_maximum_fusion), channel_id=1, source_target_pairs={{0,2},{2,0},{1,3},{3,1},{4,6},{6,4},{5,7},{7,5},{8,10},{10,8},{9,1... | collective-permute-start | bytes 55304 | tf_op jit(solution)/shard_map/ppermute | solution.py:552
  15.4 2.3 %collective-permute-done.5.beside_ref = bf16[18,512]{1,0:T(8,128)(2,1)S(1)} collective-permute-done((bf16[18,512]{1,0:T(8,128)(2,1)S(1)}, bf16[18,512]{1,0:T(8,128)(2,1)S(1)}, u32[]{:S(2)}, u32[]{:S(2)}) %collective-permute-start.5) | collective-permute-done | bytes 18464 | tf_op jit(solution)/shard_map/ppermute | solution.py:552
  17.8 0.0 collective-permute-start.6
  17.8 0.5 collective-permute-start.7
  18.3 3.7 %deepen.2 = (bf16[64,512]{1,0:T(8,128)(2,1)S(1)}, bf16[64,512]{1,0:T(8,128)(2,1)S(1)}, bf16[64,512]{1,0:T(8,128)(2,1)S(1)}, bf16[64,512]{1,0:T(8,128)(2,1)S(1)}) custom-call(s32[7]{0:T(128)S(1)} %stack.47.flag_ref, bf16[8,80,1024]{2,1,0:T(8,128)(2,1)S(1)} %get-tuple-element.64.e_own_ref, bf16[8,80,1024]{2,1,0:T(8,128)(2,1)S(1)} %get-tuple-element.65.e_sib_ref, ...), custom_call_target="tpu_custom_call" | custom-call | flops 536870912 | bytes 2621440 | tf_op jit(solution)/shard_map/deepen/pallas_call | solution.py:383
  22.0 0.0 collective-permute-done.7.wo_sib_ref
  22.0 0.0 collective-permute-done.6.wqkv_sib_ref
  22.0 3.3 %collective-permute-start.8 = (bf16[64,512]{1,0:T(8,128)(2,1)S(1)}, bf16[64,512]{1,0:T(8,128)(2,1)S(1)}, u32[]{:S(2)}, u32[]{:S(2)}) collective-permute-start(bf16[64,512]{1,0:T(8,128)(2,1)S(1)} %get-tuple-element.78.rest_0_), channel_id=1, source_target_pairs={{0,8},{2,10},{4,12},{6,14},{8,0},{10,2},{12,4},{14,6},{1,9},{3,11}... | collective-permute-start | bytes 196616 | tf_op jit(solution)/shard_map/ppermute | solution.py:560
  25.3 1.0 %collective-permute-start.12 = (bf16[64,512]{1,0:T(8,128)(2,1)S(1)}, bf16[64,512]{1,0:T(8,128)(2,1)S(1)}, u32[]{:S(2)}, u32[]{:S(2)}) collective-permute-start(bf16[64,512]{1,0:T(8,128)(2,1)S(1)} %get-tuple-element.79.rest_1_), channel_id=1, source_target_pairs={{0,10},{2,8},{4,14},{6,12},{8,2},{10,0},{12,6},{14,4},{1,11},{3,9}... | collective-permute-start | bytes 196616 | tf_op jit(solution)/shard_map/ppermute | solution.py:560
  26.3 3.9 %collective-permute-start.13 = (bf16[64,512]{1,0:T(8,128)(2,1)S(1)}, bf16[64,512]{1,0:T(8,128)(2,1)S(1)}, u32[]{:S(2)}, u32[]{:S(2)}) collective-permute-start(bf16[64,512]{1,0:T(8,128)(2,1)S(1)} %get-tuple-element.80.rest_2_), channel_id=1, source_target_pairs={{0,12},{2,14},{4,8},{6,10},{8,4},{10,6},{12,0},{14,2},{1,13},{3,15... | collective-permute-start | bytes 196616 | tf_op jit(solution)/shard_map/ppermute | solution.py:560
  30.2 0.0 collective-permute-start.14
  30.2 3.7 %deepen.3 = (bf16[64,512]{1,0:T(8,128)(2,1)S(1)}, bf16[64,512]{1,0:T(8,128)(2,1)S(1)}, bf16[64,512]{1,0:T(8,128)(2,1)S(1)}, bf16[64,512]{1,0:T(8,128)(2,1)S(1)}) custom-call(s32[7]{0:T(128)S(1)} %stack.47.flag_ref, bf16[8,80,1024]{2,1,0:T(8,128)(2,1)S(1)} %get-tuple-element.64.e_own_ref, bf16[8,80,1024]{2,1,0:T(8,128)(2,1)S(1)} %get-tuple-element.65.e_sib_ref, ...), custom_call_target="tpu_custom_call" | custom-call | flops 536870912 | bytes 2621440 | tf_op jit(solution)/shard_map/deepen/pallas_call | solution.py:383
  33.9 0.0 collective-permute-done.8.rest_4_
  33.9 0.1 collective-permute-start.9
  34.0 2.9 %collective-permute-start.10 = (bf16[64,512]{1,0:T(8,128)(2,1)S(1)}, bf16[64,512]{1,0:T(8,128)(2,1)S(1)}, u32[]{:S(2)}, u32[]{:S(2)}) collective-permute-start(bf16[64,512]{1,0:T(8,128)(2,1)S(1)} %get-tuple-element.87), channel_id=1, source_target_pairs={{0,6},{2,4},{4,2},{6,0},{8,14},{10,12},{12,10},{14,8},{1,7},{3,5},... | collective-permute-start | bytes 196616 | tf_op jit(solution)/shard_map/ppermute | solution.py:560
  36.9 0.0 collective-permute-done.12.rest_5_
  36.9 0.6 collective-permute-start.11
  37.4 0.0 collective-permute-done.13.rest_6_
  37.5 0.0 collective-permute-done.14.rest_7_
  37.5 1.0 %collective-permute-done.9.rest_0_ = bf16[64,512]{1,0:T(8,128)(2,1)S(1)} collective-permute-done((bf16[64,512]{1,0:T(8,128)(2,1)S(1)}, bf16[64,512]{1,0:T(8,128)(2,1)S(1)}, u32[]{:S(2)}, u32[]{:S(2)}) %collective-permute-start.9) | collective-permute-done | bytes 65568 | tf_op jit(solution)/shard_map/ppermute | solution.py:560
  38.5 1.6 %collective-permute-done.10.rest_1_ = bf16[64,512]{1,0:T(8,128)(2,1)S(1)} collective-permute-done((bf16[64,512]{1,0:T(8,128)(2,1)S(1)}, bf16[64,512]{1,0:T(8,128)(2,1)S(1)}, u32[]{:S(2)}, u32[]{:S(2)}) %collective-permute-start.10) | collective-permute-done | bytes 65568 | tf_op jit(solution)/shard_map/ppermute | solution.py:560
  40.1 1.1 %collective-permute-done.11.rest_2_ = bf16[64,512]{1,0:T(8,128)(2,1)S(1)} collective-permute-done((bf16[64,512]{1,0:T(8,128)(2,1)S(1)}, bf16[64,512]{1,0:T(8,128)(2,1)S(1)}, u32[]{:S(2)}, u32[]{:S(2)}) %collective-permute-start.11) | collective-permute-done | bytes 65568 | tf_op jit(solution)/shard_map/ppermute | solution.py:560
  41.2 3.6 %attend.1 = bf16[8,2,64,256]{3,2,1,0:T(8,128)(2,1)S(1)} custom-call(s32[7]{0:T(128)S(1)} %stack.47.flag_ref, bf16[3,512,256]{2,1,0:T(8,128)(2,1)S(1)} %get-tuple-element.63.wqkv_ref, bf16[3,512,256]{2,1,0:T(8,128)(2,1)S(1)} %collective-permute-done.6.wqkv_sib_ref, bf16[256,512]{1,0:T(8,128)(2,1)S(1)} %get-tuple-element.75.wo_ref, ...), custom_call_target="tpu_custom_call" | custom-call | flops 1073741824 | bytes 1048576 | tf_op jit(solution)/shard_map/attend/pallas_call | solution.py:472
  44.8 19.5 %all_to_all.5 = bf16[16,64,256]{2,1,0:T(8,128)(2,1)S(1)} all-to-all(bf16[16,64,256]{2,1,0:T(8,128)(2,1)S(1)} %bitcast.21), channel_id=1, replica_groups=mesh['grp'=2,'gy'=4,'gx'=2,'ch'=2] {'gy','gx','ch'}, dimensions={0} | all-to-all | bytes 1048576 | tf_op jit(solution)/shard_map/all_to_all | solution.py:606
  64.2 0.1 reshape.14
  64.4 0.3 copy.14
  64.6 0.9 %reshape.15 = bf16[16,64,256]{2,1,0:T(8,128)(2,1)} reshape(bf16[2,4,2,4,2,2,4,256]{7,6,5,4,3,2,1,0:T(4,128)(2,1)S(1)} %bitcast.22) | data formatting | bytes 1048576 | tf_op jit(solution)/shard_map/reshape | solution.py:610
  (9 shorter events, 0.0 us)
Async XLA Ops:
  1.9 7.0 %collective-permute-start = (bf16[1024,512]{1,0:T(8,128)(2,1)}, bf16[1024,512]{1,0:T(8,128)(2,1)S(1)}, u32[]{:S(2)}, u32[]{:S(2)}) collective-permute-start(bf16[1024,512]{1,0:T(8,128)(2,1)} %refs_0_), channel_id=1, source_target_pairs={{0,1},{1,0},{2,3},{3,2},{4,5},{5,4},{6,7},{7,6},{8,9},{9,8},{10,11... | collective-permute-start | bytes 3145736 | tf_op jit(solution)/shard_map/ppermute | solution.py:579
  2.4 6.5 %collective-permute-start.3 = (bf16[512,1024]{1,0:T(8,128)(2,1)}, bf16[512,1024]{1,0:T(8,128)(2,1)S(1)}, u32[]{:S(2)}, u32[]{:S(2)}) collective-permute-start(bf16[512,1024]{1,0:T(8,128)(2,1)} %w_ref), channel_id=1, source_target_pairs={{0,1},{1,0},{2,3},{3,2},{4,5},{5,4},{6,7},{7,6},{8,9},{9,8},{10,11... | collective-permute-start | bytes 3145736 | tf_op jit(solution)/shard_map/ppermute | solution.py:579
  2.5 6.4 %collective-permute-start.4 = (f32[16,1024]{1,0:T(8,128)}, f32[16,1024]{1,0:T(8,128)S(1)}, u32[]{:S(2)}, u32[]{:S(2)}) collective-permute-start(f32[16,1024]{1,0:T(8,128)} %get-tuple-element.54.small_ref), channel_id=1, source_target_pairs={{0,1},{1,0},{2,3},{3,2},{4,5},{5,4},{6,7},{7,6},{8,9},{9,8},{10,11... | collective-permute-start | bytes 196616 | tf_op jit(solution)/shard_map/ppermute | solution.py:579
  2.9 10.5 %collective-permute-start.1 = (bf16[64,512]{1,0:T(8,128)(2,1)}, bf16[64,512]{1,0:T(8,128)(2,1)S(1)}, u32[]{:S(2)}, u32[]{:S(2)}) collective-permute-start(bf16[64,512]{1,0:T(8,128)(2,1)} %get-tuple-element.51), channel_id=1, source_target_pairs={{0,4},{4,8},{8,12},{1,5},{5,9},{9,13},{2,6},{6,10},{10,14},{3,7},{... | collective-permute-start | bytes 196616 | tf_op jit(solution)/shard_map/ppermute | solution.py:547
  7.5 6.4 %collective-permute-start.2 = (bf16[64,512]{1,0:T(8,128)(2,1)}, bf16[64,512]{1,0:T(8,128)(2,1)S(1)}, u32[]{:S(2)}, u32[]{:S(2)}) collective-permute-start(bf16[64,512]{1,0:T(8,128)(2,1)} %get-tuple-element.52), channel_id=1, source_target_pairs={{4,0},{8,4},{12,8},{5,1},{9,5},{13,9},{6,2},{10,6},{14,10},{7,3},{... | collective-permute-start | bytes 196616 | tf_op jit(solution)/shard_map/ppermute | solution.py:547
  8.9 1.2 %copy-start = (bf16[16,64,512]{2,1,0:T(8,128)(2,1)S(1)}, bf16[16,64,512]{2,1,0:T(8,128)(2,1)}, u32[]{:S(2)}) copy-start(bf16[16,64,512]{2,1,0:T(8,128)(2,1)} %cells_hbm.1) | copy-start | bytes 3145732
  10.1 1.9 %copy-start.1 = (bf16[512,1024]{1,0:T(8,128)(2,1)S(1)}, bf16[512,1024]{1,0:T(8,128)(2,1)}, u32[]{:S(2)}) copy-start(bf16[512,1024]{1,0:T(8,128)(2,1)} %w_ref) | copy-start | bytes 3145732
  10.1 1.9 %copy-start.2 = (bf16[1024,512]{1,0:T(8,128)(2,1)S(1)}, bf16[1024,512]{1,0:T(8,128)(2,1)}, u32[]{:S(2)}) copy-start(bf16[1024,512]{1,0:T(8,128)(2,1)} %refs_0_) | copy-start | bytes 3145732
  10.1 1.9 %copy-start.3 = (bf16[512,3,256]{2,0,1:T(8,128)(2,1)S(1)}, bf16[512,3,256]{2,0,1:T(8,128)(2,1)}, u32[]{:S(2)}) copy-start(bf16[512,3,256]{2,0,1:T(8,128)(2,1)} %param.19) | copy-start | bytes 2359300
  10.1 1.9 %copy-start.4 = (f32[16,1024]{1,0:T(8,128)S(1)}, f32[16,1024]{1,0:T(8,128)}, u32[]{:S(2)}) copy-start(f32[16,1024]{1,0:T(8,128)} %get-tuple-element.54.small_ref) | copy-start | bytes 196612
  10.1 1.9 %copy-start.5 = (bf16[256,512]{1,0:T(8,128)(2,1)S(1)}, bf16[256,512]{1,0:T(8,128)(2,1)}, u32[]{:S(2)}) copy-start(bf16[256,512]{1,0:T(8,128)(2,1)} %refs_2_.1) | copy-start | bytes 786436
  12.0 1.8 %copy-start.6 = (bf16[16,512]{1,0:T(8,128)(2,1)S(1)}, bf16[16,512]{1,0:T(8,128)(2,1)}, u32[]{:S(2)}) copy-start(bf16[16,512]{1,0:T(8,128)(2,1)} %get-tuple-element.59) | copy-start | bytes 49156
  13.9 3.9 %collective-permute-start.5 = (bf16[18,512]{1,0:T(8,128)(2,1)S(1)}, bf16[18,512]{1,0:T(8,128)(2,1)S(1)}, u32[]{:S(2)}, u32[]{:S(2)}) collective-permute-start(bf16[18,512]{1,0:T(8,128)(2,1)S(1)} %pad_maximum_fusion), channel_id=1, source_target_pairs={{0,2},{2,0},{1,3},{3,1},{4,6},{6,4},{5,7},{7,5},{8,10},{10,8},{9,1... | collective-permute-start | bytes 55304 | tf_op jit(solution)/shard_map/ppermute | solution.py:552
  17.8 4.2 %collective-permute-start.6 = (bf16[3,512,256]{2,1,0:T(8,128)(2,1)S(1)}, bf16[3,512,256]{2,1,0:T(8,128)(2,1)S(1)}, u32[]{:S(2)}, u32[]{:S(2)}) collective-permute-start(bf16[3,512,256]{2,1,0:T(8,128)(2,1)S(1)} %get-tuple-element.63.wqkv_ref), channel_id=1, source_target_pairs={{0,1},{1,0},{2,3},{3,2},{4,5},{5,4},{6,7},{7,6},{8,9},{9,8},{10,11... | collective-permute-start | bytes 2359304 | tf_op jit(solution)/shard_map/ppermute | solution.py:579
  17.8 4.2 %collective-permute-start.7 = (bf16[256,512]{1,0:T(8,128)(2,1)S(1)}, bf16[256,512]{1,0:T(8,128)(2,1)S(1)}, u32[]{:S(2)}, u32[]{:S(2)}) collective-permute-start(bf16[256,512]{1,0:T(8,128)(2,1)S(1)} %get-tuple-element.75.wo_ref), channel_id=1, source_target_pairs={{0,1},{1,0},{2,3},{3,2},{4,5},{5,4},{6,7},{7,6},{8,9},{9,8},{10,11... | collective-permute-start | bytes 786440 | tf_op jit(solution)/shard_map/ppermute | solution.py:579
  22.0 11.9 %collective-permute-start.8 = (bf16[64,512]{1,0:T(8,128)(2,1)S(1)}, bf16[64,512]{1,0:T(8,128)(2,1)S(1)}, u32[]{:S(2)}, u32[]{:S(2)}) collective-permute-start(bf16[64,512]{1,0:T(8,128)(2,1)S(1)} %get-tuple-element.78.rest_0_), channel_id=1, source_target_pairs={{0,8},{2,10},{4,12},{6,14},{8,0},{10,2},{12,4},{14,6},{1,9},{3,11}... | collective-permute-start | bytes 196616 | tf_op jit(solution)/shard_map/ppermute | solution.py:560
  25.3 11.6 %collective-permute-start.12 = (bf16[64,512]{1,0:T(8,128)(2,1)S(1)}, bf16[64,512]{1,0:T(8,128)(2,1)S(1)}, u32[]{:S(2)}, u32[]{:S(2)}) collective-permute-start(bf16[64,512]{1,0:T(8,128)(2,1)S(1)} %get-tuple-element.79.rest_1_), channel_id=1, source_target_pairs={{0,10},{2,8},{4,14},{6,12},{8,2},{10,0},{12,6},{14,4},{1,11},{3,9}... | collective-permute-start | bytes 196616 | tf_op jit(solution)/shard_map/ppermute | solution.py:560
  26.3 11.1 %collective-permute-start.13 = (bf16[64,512]{1,0:T(8,128)(2,1)S(1)}, bf16[64,512]{1,0:T(8,128)(2,1)S(1)}, u32[]{:S(2)}, u32[]{:S(2)}) collective-permute-start(bf16[64,512]{1,0:T(8,128)(2,1)S(1)} %get-tuple-element.80.rest_2_), channel_id=1, source_target_pairs={{0,12},{2,14},{4,8},{6,10},{8,4},{10,6},{12,0},{14,2},{1,13},{3,15... | collective-permute-start | bytes 196616 | tf_op jit(solution)/shard_map/ppermute | solution.py:560
  30.2 7.3 %collective-permute-start.14 = (bf16[64,512]{1,0:T(8,128)(2,1)S(1)}, bf16[64,512]{1,0:T(8,128)(2,1)S(1)}, u32[]{:S(2)}, u32[]{:S(2)}) collective-permute-start(bf16[64,512]{1,0:T(8,128)(2,1)S(1)} %get-tuple-element.81.rest_3_), channel_id=1, source_target_pairs={{0,14},{2,12},{4,10},{6,8},{8,6},{10,4},{12,2},{14,0},{1,15},{3,13... | collective-permute-start | bytes 196616 | tf_op jit(solution)/shard_map/ppermute | solution.py:560
  33.9 4.6 %collective-permute-start.9 = (bf16[64,512]{1,0:T(8,128)(2,1)S(1)}, bf16[64,512]{1,0:T(8,128)(2,1)S(1)}, u32[]{:S(2)}, u32[]{:S(2)}) collective-permute-start(bf16[64,512]{1,0:T(8,128)(2,1)S(1)} %get-tuple-element.86), channel_id=1, source_target_pairs={{0,4},{2,6},{4,0},{6,2},{8,12},{10,14},{12,8},{14,10},{1,5},{3,7},... | collective-permute-start | bytes 196616 | tf_op jit(solution)/shard_map/ppermute | solution.py:560
  34.0 6.1 %collective-permute-start.10 = (bf16[64,512]{1,0:T(8,128)(2,1)S(1)}, bf16[64,512]{1,0:T(8,128)(2,1)S(1)}, u32[]{:S(2)}, u32[]{:S(2)}) collective-permute-start(bf16[64,512]{1,0:T(8,128)(2,1)S(1)} %get-tuple-element.87), channel_id=1, source_target_pairs={{0,6},{2,4},{4,2},{6,0},{8,14},{10,12},{12,10},{14,8},{1,7},{3,5},... | collective-permute-start | bytes 196616 | tf_op jit(solution)/shard_map/ppermute | solution.py:560
  36.9 4.3 %collective-permute-start.11 = (bf16[64,512]{1,0:T(8,128)(2,1)S(1)}, bf16[64,512]{1,0:T(8,128)(2,1)S(1)}, u32[]{:S(2)}, u32[]{:S(2)}) collective-permute-start(bf16[64,512]{1,0:T(8,128)(2,1)S(1)} %get-tuple-element.88), channel_id=1, source_target_pairs={{0,2},{2,0},{4,6},{6,4},{8,10},{10,8},{12,14},{14,12},{1,3},{3,1},... | collective-permute-start | bytes 196616 | tf_op jit(solution)/shard_map/ppermute | solution.py:560

commit v3 on v2

--- a/solution.py
+++ b/solution.py
@@ -191,11 +191,10 @@
         shape = ((self.span_w + 2) * SUBLANES, self.outer_w * self.depth_w)
         return one_hot(self.columns(shape, core)[1])
 
-    def column_order(self, part):
-        shape = ((self.half_h + 2) * SUBLANES, self.outer_h * self.depth_h + 2)
+    def column_order(self):
+        shape = ((self.depth_h + 2) * SUBLANES, self.outer_h * self.depth_h + 2)
         token = lax.broadcasted_iota(jnp.int32, shape, 0)
-        i, plane = token // self.outer_w % self.outer_h, token // SUBLANES
-        return one_hot(i * self.depth_h + part * self.half_h + plane)
+        return one_hot(token // self.outer_w % self.outer_h * self.depth_h + token // SUBLANES)
 
 
 def one_hot(place):
@@ -287,114 +286,141 @@
     )(ordered, weight, small, *others)
 
 
-def deepen_kernel(
-    plan, targets, flag_ref, e_own_ref, e_sib_ref, x_ref, up_ref, down_ref, beside_ref, we_ref, we_sib_ref,
-    small_ref, small_sib_ref, wp_ref, wp_sib_ref, *rest,
-):
-    *outs, held, deep, mixed = rest[-len(targets) - 3 :]
-    core, up, down, left, right, own_y, own_x = (flag_ref[i] for i in range(7))
-    far = targets[0][0] // 2
-    part = (own_y // 2) ^ far
-    base = part * plan.half_h
-    planes, slots, outer_w = plan.half_h + 2, plan.span_w + 2, plan.outer_w
-    own = we_ref.shape[1]
-    row = lax.broadcasted_iota(jnp.int32, (1, SUBLANES, CHUNK), 1)
-    plane = lax.broadcasted_iota(jnp.int32, (planes, SUBLANES, CHUNK), 0)
-    at = lax.broadcasted_iota(jnp.int32, (planes, SUBLANES, CHUNK), 1)
-    first = part == 0
-
-    edge = jnp.where(first, up, down).astype(jnp.float32)
+def outside_kernel_part(plan, flag_ref, one_ref, other_ref, beside_ref, sides, halo_ref, beside_out_ref):
+    core, up, down, left, right = (flag_ref[i] for i in range(5))
+    planes, slots, outer_w = plan.depth_h + 2, plan.span_w + 2, plan.outer_w
+    order = plan.row_order(core)
+    even = flag_ref[5] % 2 == 0
+    rows = jnp.where(even, other_ref[...], one_ref[...]), jnp.where(even, one_ref[...], other_ref[...])
+    cells = [jnp.dot(order, row, preferred_element_type=jnp.float32) for row in rows]
+    cells.append(jnp.dot(plan.column_order(), beside_ref[...], preferred_element_type=jnp.float32))
+    cells = jnp.concatenate([value.astype(jnp.bfloat16) for value in cells], axis=0)
+    up, down = up.astype(jnp.float32), down.astype(jnp.float32)
     beside = jnp.where(core == 0, left, right).astype(jnp.float32)
-    side_mask = beside * jnp.where(
-        (plane == part * (planes - 1)) & (at // outer_w == part * (plan.outer_h - 1)), edge, 1.0
-    )
-    low_rows = jnp.where(first, outer_w, 0)
-    high_rows = outer_w - low_rows
-    at_side = row % outer_w == core * (outer_w - 1)
-    halo_cells = jnp.where(first, up_ref[...], down_ref[...])
-    halo_cells = jnp.dot(
-        plan.row_order(core), halo_cells, preferred_element_type=jnp.float32
-    ).astype(jnp.bfloat16)
-    side_cells = jnp.dot(
-        plan.column_order(part), beside_ref[...], preferred_element_type=jnp.float32
-    ).astype(jnp.bfloat16)
-    outside = jnp.concatenate([halo_cells, side_cells], axis=0)
-    before = lax.rem(base + plan.depth_h - 1, plan.depth_h)
-    after = lax.rem(base + plan.half_h, plan.depth_h)
-
-    sides = (e_own_ref, we_ref, small_ref), (e_sib_ref, we_sib_ref, small_sib_ref)
-    for side, (e_ref, we, small) in enumerate(sides):
+    token = lax.broadcasted_iota(jnp.int32, (cells.shape[0], 1), 0) - 2 * slots * SUBLANES
+    plane, i = token // SUBLANES, token // outer_w % plan.outer_h
+    mask = jnp.where(token < -slots * SUBLANES, up, jnp.where(token < 0, down, beside))
+    mask = mask * jnp.where((token >= 0) & (plane == 0) & (i == 0), up, 1.0)
+    mask = mask * jnp.where((plane == planes - 1) & (i == plan.outer_h - 1), down, 1.0)
+    for side, (weight, small) in enumerate(sides):
+        own = weight.shape[1]
         for low in range(0, own, CHUNK):
             lanes = slice(low, low + CHUNK)
-            pre = jnp.dot(outside, we[:, lanes], preferred_element_type=jnp.float32)
-            grown = gelu_erf(pre + small[B_EXPAND, lanes])
-            halo = grown[: slots * SUBLANES].reshape(slots, SUBLANES, CHUNK) * edge
-            beside_cells = grown[slots * SUBLANES :].reshape(planes, SUBLANES, CHUNK) * side_mask
-
-            def plane_of(index):
-                return e_ref[index, :, lanes].astype(jnp.float32).reshape(slots, SUBLANES, CHUNK)
-
-            for p in range(1, planes - 1):
-                held[p] = plane_of(base + p - 1)
-            values = plane_of(before)
-            held[0] = jnp.where(row < low_rows, halo, pltpu.roll(values, low_rows, 1))
-            values = plane_of(after)
-            held[planes - 1] = jnp.where(
-                row >= SUBLANES - high_rows,
-                halo,
-                pltpu.roll(values, lax.rem(SUBLANES - high_rows, SUBLANES), 1),
-            )
-            slot = core * (slots - 1)
-            held[:, slot] = jnp.where(at_side, beside_cells, held[:, slot])
-            for lane in range(0, CHUNK, 128):
-                here = slice(lane, lane + 128)
-                now = slice(low + lane, low + lane + 128)
-                for a in range(plan.half_h):
-                    total = jnp.broadcast_to(
-                        small[B_DEPTH, now], (plan.span_w, SUBLANES, 128)
-                    )
-                    for di in range(3):
-                        for dj in range(3):
-                            tap = small[3 * di + dj : 3 * di + dj + 1, now]
-                            total = total + held[a + di, dj : dj + plan.span_w, :, here] * tap
-                    deep[a, :, side * own + low + lane : side * own + low + lane + 128] = (
-                        gelu_erf(total).astype(jnp.bfloat16).reshape(-1, 128)
-                    )
-    source = deep[...].reshape(-1, 2 * own)
-    total = jnp.dot(source[:, :own], wp_ref[...], preferred_element_type=jnp.float32)
-    total = total + jnp.dot(source[:, own:], wp_sib_ref[...], preferred_element_type=jnp.float32)
-    residual = x_ref[pl.ds(base, plan.half_h)].astype(jnp.float32) + small_ref[B_PROJECT, : plan.width]
+            there = slice(side * own + low, side * own + low + CHUNK)
+            pre = jnp.dot(cells, weight[:, lanes], preferred_element_type=jnp.float32)
+            grown = (gelu_erf(pre + small[B_EXPAND, lanes]) * mask).astype(jnp.bfloat16)
+            halo_ref[0, :, there] = grown[: slots * SUBLANES]
+            halo_ref[1, :, there] = grown[slots * SUBLANES : 2 * slots * SUBLANES]
+            beside_out_ref[:, :, there] = grown[2 * slots * SUBLANES :].reshape(planes, SUBLANES, CHUNK)
+
+
+def deepen_kernel(plan, targets, first, *refs):
+    flag_ref, e_own_ref, e_sib_ref, x_ref, *refs = refs
+    small_ref, small_sib_ref, wp_ref, wp_sib_ref, *refs = refs
+    *refs, deep, mixed = refs
+    if first:
+        one_ref, other_ref, beside_ref, we_ref, we_sib_ref, *outs, halo_ref, sides_ref = refs
+        weights = (we_ref, small_ref), (we_sib_ref, small_sib_ref)
+        outside_kernel_part(plan, flag_ref, one_ref, other_ref, beside_ref, weights, halo_ref, sides_ref)
+    else:
+        halo_ref, sides_ref, *refs = refs
+        outs = refs[-len(targets) :]
+    core, own_y, own_x = flag_ref[0], flag_ref[5], flag_ref[6]
+    each = plan.depth_h // plan.n_rows
+    blocks = len({dy for dy, _ in targets})
+    count, slots, outer_w = blocks * each, plan.span_w + 2, plan.outer_w
+    base = (own_y ^ targets[0][0]) // blocks * count
+    low_rows = jnp.where(base == 0, outer_w, 0)
+    high_rows = jnp.where(base + count == plan.depth_h, outer_w, 0)
+    row = lax.broadcasted_iota(jnp.int32, (1, SUBLANES, 128), 1)
+    from_low, from_high = row < low_rows, row >= SUBLANES - high_rows
+    at_left = row % outer_w == jnp.where(core == 0, 0, -1)
+    at_right = row % outer_w == jnp.where(core == 0, -1, outer_w - 1)
+    before = lax.rem(base + plan.depth_h - 1, plan.depth_h)
+    after = lax.rem(base + count, plan.depth_h)
+
+    own = wp_ref.shape[0]
+    total = None
+    for side, (e_ref, wp, small) in enumerate(
+        ((e_own_ref, wp_ref, small_ref), (e_sib_ref, wp_sib_ref, small_sib_ref))
+    ):
+        for low in range(0, own, 128):
+            now, there = slice(low, low + 128), slice(side * own + low, side * own + low + 128)
+            taps = [small[tap : tap + 1, now] for tap in range(9)]
+            bias = small[B_DEPTH, now]
+
+            def shaped(values):
+                return values.astype(jnp.float32).reshape(slots, SUBLANES, 128)
+
+            def plane_of(p):
+                values = shaped(e_ref[before if p == 0 else after if p == count + 1 else base + p - 1, :, now])
+                if p == 0:
+                    rolled = pltpu.roll(values, low_rows, 1)
+                    values = jnp.where(from_low, shaped(halo_ref[0, :, there]), rolled)
+                if p == count + 1:
+                    rolled = pltpu.roll(values, lax.rem(SUBLANES - high_rows, SUBLANES), 1)
+                    values = jnp.where(from_high, shaped(halo_ref[1, :, there]), rolled)
+                met = sides_ref[base + p, :, there].astype(jnp.float32)[None]
+                return jnp.concatenate(
+                    [
+                        jnp.where(at_left, met, values[:1]),
+                        values[1:-1],
+                        jnp.where(at_right, met, values[-1:]),
+                    ],
+                    axis=0,
+                )
+
+            window = [plane_of(0), plane_of(1)]
+            for a in range(count):
+                window.append(plane_of(a + 2))
+                summed = jnp.broadcast_to(bias, (plan.span_w, SUBLANES, 128))
+                for di in range(3):
+                    for dj in range(3):
+                        summed = summed + window[a + di][dj : dj + plan.span_w] * taps[3 * di + dj]
+                deep[a, :, there] = gelu_erf(summed).astype(jnp.bfloat16).reshape(-1, 128)
+            if (low + 128) % CHUNK == 0:
+                rows = slice(low + 128 - CHUNK, low + 128)
+                source = deep[:, :, side * own + rows.start : side * own + rows.stop]
+                term = jnp.dot(
+                    source.reshape(-1, CHUNK), wp[rows], preferred_element_type=jnp.float32
+                )
+                total = term if total is None else total + term
+    residual = x_ref[pl.ds(base, count)].astype(jnp.float32) + small_ref[B_PROJECT, : plan.width]
     mixed[...] = (total.reshape(residual.shape) + residual).reshape(mixed.shape)
-    planes_each = plan.depth_h // plan.n_rows
     rows = plan.span_w // plan.n_cols * SUBLANES
     for out, (dy, dx) in zip(outs, targets):
-        block = (own_y ^ dy) & 1
+        block = (own_y ^ dy) % blocks
         column = own_x ^ dx
-        for k in range(planes_each):
-            out[k * rows : (k + 1) * rows] = mixed[block * planes_each + k, column].astype(jnp.bfloat16)
-
-
-def deepen(plan, targets, flags, e, x, rows, cols, weights, after):
-    own = weights[0].shape[1]
-    planes, slots = plan.half_h + 2, plan.span_w + 2
+        for k in range(each):
+            out[k * rows : (k + 1) * rows] = mixed[block * each + k, column].astype(jnp.bfloat16)
+
+
+def deepen(plan, targets, flags, e, x, small, w_project, outside, first, after=()):
+    own = w_project[0].shape[0]
     tokens = plan.span_w * SUBLANES
-    message = (plan.depth_h // plan.n_rows * (tokens // plan.n_cols), plan.width)
-    operands = (*e, x, *rows, cols, *weights)
+    each = plan.depth_h // plan.n_rows
+    count = len({dy for dy, _ in targets}) * each
+    message = (each * (tokens // plan.n_cols), plan.width)
+    operands = (*e, x, *small, *w_project, *outside)
+    out_shape = [jax.ShapeDtypeStruct(message, jnp.bfloat16)] * len(targets)
+    if first:
+        slots = (plan.span_w + 2) * SUBLANES
+        out_shape.append(jax.ShapeDtypeStruct((2, slots, 2 * own), jnp.bfloat16))
+        out_shape.append(jax.ShapeDtypeStruct((plan.depth_h + 2, SUBLANES, 2 * own), jnp.bfloat16))
     return pl.pallas_call(
-        functools.partial(deepen_kernel, plan, targets),
+        functools.partial(deepen_kernel, plan, targets, first),
         in_specs=[pl.BlockSpec(memory_space=pltpu.SMEM)]
         + in_vmem(len(operands))
         + [pl.BlockSpec(memory_space=pl.ANY)] * len(after),
-        out_specs=in_vmem(len(targets)),
-        out_shape=[jax.ShapeDtypeStruct(message, jnp.bfloat16)] * len(targets),
+        out_specs=in_vmem(len(out_shape)),
+        out_shape=out_shape,
         scratch_shapes=[
-            pltpu.VMEM((planes, slots, SUBLANES, CHUNK), jnp.float32),
-            pltpu.VMEM((plan.half_h, tokens, 2 * own), jnp.bfloat16),
-            pltpu.VMEM((plan.half_h, plan.n_cols, tokens // plan.n_cols, plan.width), jnp.float32),
+            pltpu.VMEM((count, tokens, 2 * own), jnp.bfloat16),
+            pltpu.VMEM((count, plan.n_cols, tokens // plan.n_cols, plan.width), jnp.float32),
         ],
         compiler_params=pltpu.CompilerParams(vmem_limit_bytes=VMEM_BYTES),
         cost_estimate=pl.CostEstimate(
-            flops=2 * x.size * own, bytes_accessed=4 * e[0].size, transcendentals=0
+            flops=count * tokens * 4 * own * plan.width, bytes_accessed=4 * e[0].size, transcendentals=0
         ),
         name="deepen",
     )(flags, *operands, *after)
@@ -487,17 +513,17 @@
     )(flags, *operands)
 
 
-def edges_kernel(group, column_ref, cells_hbm, taps_hbm, *refs):
+def edges_kernel(group, column_ref, row_ref, cells_hbm, taps_hbm, *refs):
     count = (len(refs) - 6) // 2
-    vectors_hbm, (top_ref, bottom_ref, side_ref, small_ref, held, taps), (*vectors, sems) = (
+    vectors_hbm, (one_ref, other_ref, side_ref, small_ref, held, taps), (*vectors, sems) = (
         refs[:count], refs[count : count + 6], refs[count + 6 :]
     )
     rows, width = cells_hbm.shape[0], cells_hbm.shape[2]
-    column = column_ref[0]
+    column, one = column_ref[0], row_ref[0]
     start = pl.multiple_of(column // group * group, group)
     pairs = [
-        (cells_hbm.at[0], top_ref),
-        (cells_hbm.at[rows - 1], bottom_ref),
+        (cells_hbm.at[one], one_ref),
+        (cells_hbm.at[rows - 1 - one], other_ref),
         (cells_hbm.at[:, pl.ds(start, group)], held),
         (taps_hbm, taps),
         *zip(vectors_hbm, vectors),
@@ -519,13 +545,13 @@
         small_ref[9 + i : 10 + i, : vector.shape[1]] = vector[...]
 
 
-def edges(cells, column, w_depth, vectors):
+def edges(cells, column, row, w_depth, vectors):
     rows, cols, width = cells.shape
     group = 2 * SUBLANES
     operands = (cells, w_depth, *vectors)
     return pl.pallas_call(
         functools.partial(edges_kernel, group),
-        in_specs=[pl.BlockSpec(memory_space=pltpu.SMEM)]
+        in_specs=[pl.BlockSpec(memory_space=pltpu.SMEM)] * 2
         + [pl.BlockSpec(memory_space=pltpu.HBM)] * len(operands),
         out_specs=in_vmem(4),
         out_shape=[jax.ShapeDtypeStruct((count, width), cells.dtype) for count in (cols, cols, rows)]
@@ -537,19 +563,55 @@
         ],
         compiler_params=pltpu.CompilerParams(vmem_limit_bytes=EDGES_VMEM_BYTES),
         name="edges",
-    )(column[None], *operands)
-
-
-def halo_rows(top, bottom):
+    )(column[None], row[None], *operands)
+
+
+def lay_out_kernel(plan, arrived_ref, out_ref):
+    each, run = plan.depth_h // plan.n_rows, plan.span_w // plan.n_cols
+    columns, tokens = plan.outer_w * plan.depth_w, run * SUBLANES
+    peers = plan.n_ch * plan.n_cols
+    row = lax.broadcasted_iota(jnp.int32, (plan.outer_h * columns, peers * tokens), 0)
+    i, j, b = row // columns, row % columns // plan.depth_w, row % plan.depth_w
+    core, column, slot = b // plan.span_w, b % plan.span_w // run, b % run
+    order = one_hot(
+        (column * plan.n_ch + core) * tokens + slot * SUBLANES + i * plan.outer_w + j
+    )
+    for block in range(plan.n_rows):
+        for k in range(each):
+            source = arrived_ref[block * peers : (block + 1) * peers, k * tokens : (k + 1) * tokens]
+            placed = jnp.dot(
+                order, source.reshape(peers * tokens, -1), preferred_element_type=jnp.float32
+            ).astype(jnp.bfloat16)
+            out_ref[:, block * each + k] = placed.reshape(plan.outer_h, columns, -1)
+
+
+def lay_out(plan, arrived):
+    columns = plan.outer_w * plan.depth_w
+    return pl.pallas_call(
+        functools.partial(lay_out_kernel, plan),
+        in_specs=in_vmem(1),
+        out_specs=pl.BlockSpec(memory_space=pltpu.VMEM),
+        out_shape=jax.ShapeDtypeStruct(
+            (plan.outer_h, plan.depth_h, columns, arrived.shape[2]), jnp.bfloat16
+        ),
+        compiler_params=pltpu.CompilerParams(vmem_limit_bytes=VMEM_BYTES),
+        name="lay_out",
+    )(arrived)
+
+
+def swap_rows(one, other):
     count = lax.axis_size("gy")
-    forward = [(i, i + 1) for i in range(count - 1)]
-    backward = [(target, source) for source, target in forward]
-    return lax.ppermute(bottom, "gy", forward), lax.ppermute(top, "gy", backward)
-
-
-def halo_column(column, rows, index):
-    above, below = (lax.dynamic_slice_in_dim(row, index, 1, axis=0) for row in rows)
-    return lax.ppermute(jnp.concatenate([above, column, below], axis=0), "gx", [(0, 1), (1, 0)])
+    sets = [[(i, i + 1) for i in range(low, count - 1, 2)] for low in (0, 1)]
+    return [
+        lax.ppermute(value, "gy", pairs + [(target, source) for source, target in pairs])
+        for value, pairs in zip((one, other), sets)
+    ]
+
+
+def halo_column(column, rows, index, even):
+    one, other = (lax.dynamic_slice_in_dim(row, index, 1, axis=0) for row in rows)
+    parts = [jnp.where(even, other, one), column, jnp.where(even, one, other)]
+    return lax.ppermute(jnp.concatenate(parts, axis=0), "gx", [(0, 1), (1, 0)])
 
 
 def send_to(value, dy, dx):
@@ -571,9 +633,12 @@
     ).astype(jnp.int32)
     index = jnp.where(own_x == 0, cells.shape[1] - 1, 0)
     vectors = tuple(v[None] for v in (b_expand, b_depth, b_out, b_project, ln_gain))
-    top, bottom, column, small = edges(cells, index, w_depth, vectors)
-    top, w_expand, w_project = lax.optimization_barrier((top, w_expand, w_project))
-    rows = halo_rows(top, bottom)
+    even = own_y % 2 == 0
+    one, other, column, small = edges(
+        cells, index, jnp.where(even, cells.shape[0] - 1, 0), w_depth, vectors
+    )
+    one, w_expand, w_project = lax.optimization_barrier((one, w_expand, w_project))
+    rows = swap_rows(one, other)
 
     def both(value):
         return value, lax.ppermute(value, "ch", [(0, 1), (1, 0)])
@@ -584,30 +649,35 @@
     e_own, *kept = expand_second(
         plan, ordered, w_expand[0], small[0], (w_project[0], w_qkv.transpose(1, 0, 2), w_out)
     )
-    *rows, x, e_own = lax.optimization_barrier((*rows, x, e_own))
+    *rows, x = lax.optimization_barrier((*rows, x))
     e = e_own, e_sib
-    cols = halo_column(column, rows, index)
+    cols = halo_column(column, rows, index, even)
     cols, w_qkv, w_out = lax.optimization_barrier((cols, *kept[2:]))
     w_qkv, w_out = both(w_qkv), both(w_out)
-    weights = (kept[0], w_expand[1], *small, kept[1], w_project_sib)
+    w_project = kept[1], w_project_sib
     far = [(dy, dx) for dy in (2, 3) for dx in (0, 1)]
-    near = [(1, 0), (1, 1), (0, 1), (0, 0)]
-    early = deepen(plan, far, flags, e, x, rows, cols, weights, ())
-    *early, w_qkv_sib, w_out_sib = lax.optimization_barrier((*early, w_qkv[1], w_out[1]))
+    near = [(1, 1), (1, 0), (0, 1), (0, 0)]
+    outside = (*rows, cols, kept[0], w_expand[1])
+    *sent, halo, sides = deepen(plan, far, flags, e, x, small, w_project, outside, True)
+    *sent, w_qkv_sib, w_out_sib = lax.optimization_barrier((*sent, w_qkv[1], w_out[1]))
     w_qkv, w_out = (w_qkv[0], w_qkv_sib), (w_out[0], w_out_sib)
-    arrived = [send_to(value, *target) for value, target in zip(early, far)]
-    late = deepen(plan, near, flags, e, x, rows, cols, weights, early)
-    *late, arrived[0] = lax.optimization_barrier((*late, arrived[0]))
-    arrived = [send_to(value, *target) for value, target in zip(late[:-1], near)] + [late[-1], *arrived]
+    arrived = [send_to(value, *target) for value, target in zip(sent, far)]
+    for targets, places in ((near, (0,)),):
+        sent = deepen(plan, targets, flags, e, x, small, w_project, (halo, sides), False, sent)
+        held = [arrived[place] for place in places]
+        sent = lax.optimization_barrier((*sent, *held))
+        sent, held = sent[: len(targets)], sent[len(targets) :]
+        for place, value in zip(places, held):
+            arrived[place] = value
+        arrived += [
+            value if target == (0, 0) else send_to(value, *target) for value, target in zip(sent, targets)
+        ]
     leaving = attend_windows(
-        plan, near + far, flags, arrived, (*w_qkv, *w_out, *small)
+        plan, far + near, flags, arrived, (*w_qkv, *w_out, *small)
     )
     leaving = leaving.reshape((n_rows * n_cols * n_ch,) + leaving.shape[2:])
     returned = lax.all_to_all(leaving, ("gy", "gx", "ch"), 0, 0, tiled=True)
-    returned = returned.reshape(
-        n_rows, n_cols, n_ch, plan.depth_h // n_rows, plan.span_w // n_cols, plan.outer_h, plan.outer_w, -1
-    )
-    return returned.transpose(5, 0, 3, 6, 2, 1, 4, 7).reshape(cells.shape[0], cells.shape[1], -1)
+    return lay_out(plan, returned).reshape(cells.shape[0], cells.shape[1], -1)
 
 
 def per_device(cells, *rest):

time: 65.8 us -> 62.3 us (0.947)
  waiting for transfers between devices: 6.47 us -> 4.31 us
  local copies, waits for them, and re-layouts: 2.65 us -> 1.34 us
  Pallas kernels: 16 us -> 16.8 us
    ppermute x3, waiting for transfers between devices: 2.75 us -> 0.41 us  [the longest x1 0.4 us: halo_column(): return lax.ppermute(jnp.concatenate(parts, axis=0), 'gx', [(0, 1), (1, 0)])]
    reshape x3 -> x0, local copies, waits for them, and re-layouts: 1.31 us -> none  [the longest x1 0.92 us: fast_device(): returned.transpose(5, 0, 3, 6, 2, 1, 4, 7)]
    ppermute x3, starting transfers between devices: 7.39 us -> 6.22 us  [the longest x2 3.3 us: swap_rows(): lax.ppermute(value, 'gy', pairs + [(target, source) for source, target in...]
    pallas_call x2 -> x3, Pallas kernels: 7.36 us -> 8.12 us  [the longest x2 7.02 us: deepen(): pl.pallas_call(functools.partial(deepen_kernel, plan, targets, first), in...]
    ppermute x7, starting transfers between devices: 11.7 us -> 12.5 us  [send_to(): return lax.ppermute(value, ('gy', 'gx'), pairs)]
  transfers between devices with their start and end apart: 15 -> 15, of which waited for: 5 -> 5; matrix products, arithmetic and copies ran while one was open for 0% -> 0% of each run, Pallas kernels for 16% -> 17%
where the time goes in v3:
time: 62.3 us; the launch traced here: 62.1 us
  starting transfers between devices  20.2 us (32%)
  blocking collectives  19.2 us (31%)
  Pallas kernels  16.8 us (27%)
  waiting for transfers between devices  4.31 us (7%)
  local copies, waits for them, and re-layouts  1.34 us (2%)
    all_to_all x1, blocking collectives, fast_device(): returned = lax.all_to_all(leaving, ('gy', 'gx', 'ch'), 0, 0, tiled=True)  19.2 us
    ppermute x7, starting transfers between devices, send_to(): return lax.ppermute(value, ('gy', 'gx'), pairs)  12.5 us
    pallas_call x2, Pallas kernels, deepen(): pl.pallas_call(functools.partial(deepen_kernel, plan, targets, first), in...  7.02 us
    ppermute x7, waiting for transfers between devices, send_to(): return lax.ppermute(value, ('gy', 'gx'), pairs)  3.73 us
    pallas_call x1, Pallas kernels, attend_windows(): pl.pallas_call(functools.partial(attend_kernel, plan, targets), in_specs=...  3.6 us
    ppermute x2, starting transfers between devices, swap_rows(): lax.ppermute(value, 'gy', pairs + [(target, source) for source, target in...  3.3 us
    ppermute x1, starting transfers between devices, halo_column(): return lax.ppermute(jnp.concatenate(parts, axis=0), 'gx', [(0, 1), (1, 0)])  2.92 us
    pallas_call x1, Pallas kernels, edges(): pl.pallas_call(functools.partial(edges_kernel, group), in_specs=[pl.Block...  1.88 us
  transfers between devices with their start and end apart: 15, of which 5 were waited for; matrix products, arithmetic and copies ran while one was open for 0% of the time, Pallas kernels for 17%

profile of v3, /device:TPU:0, one launch (start us, length us, event | category | flops | bytes accessed | tf_op | source)
XLA Modules:
  0.0 62.1 jit_solution(5970110044341150195)
XLA Ops:
  0.0 1.9 %edges.1 = (bf16[64,512]{1,0:T(8,128)(2,1)}, bf16[64,512]{1,0:T(8,128)(2,1)}, bf16[16,512]{1,0:T(8,128)(2,1)}, f32[16,1024]{1,0:T(8,128)}) custom-call(s32[1]{0:T(128)} %bitcast.7.column_ref, s32[1]{0:T(128)} %bitcast.8.row_ref, bf16[16,64,512]{2,1,0:T(8,128)(2,1)} %cells_hbm.1, bf16[3,3,1024]{2,1,0:T(4,128)(2,1)} %taps_hbm.1, f32[1,1024]{1,0:T(1,128)} %bitcast.21, ...), custom_call_target="tpu_custom_call" | custom-call | tf_op jit(solution)/shard_map/edges/pallas_call | solution.py:552
  1.9 0.5 collective-permute-start
  2.4 0.1 collective-permute-start.3
  2.5 0.4 collective-permute-start.4
  2.9 2.7 %collective-permute-start.1 = (bf16[64,512]{1,0:T(8,128)(2,1)}, bf16[64,512]{1,0:T(8,128)(2,1)S(1)}, u32[]{:S(2)}, u32[]{:S(2)}) collective-permute-start(bf16[64,512]{1,0:T(8,128)(2,1)} %get-tuple-element.52), channel_id=1, source_target_pairs={{0,4},{8,12},{4,0},{12,8},{1,5},{9,13},{5,1},{13,9},{2,6},{10,14},... | collective-permute-start | bytes 196616 | tf_op jit(solution)/shard_map/ppermute | solution.py:606
  5.6 0.7 %collective-permute-start.2 = (bf16[64,512]{1,0:T(8,128)(2,1)}, bf16[64,512]{1,0:T(8,128)(2,1)S(1)}, u32[]{:S(2)}, u32[]{:S(2)}) collective-permute-start(bf16[64,512]{1,0:T(8,128)(2,1)} %get-tuple-element.53), channel_id=1, source_target_pairs={{4,8},{8,4},{5,9},{9,5},{6,10},{10,6},{7,11},{11,7},{20,24},{24,20... | collective-permute-start | bytes 196616 | tf_op jit(solution)/shard_map/ppermute | solution.py:606
  6.2 0.1 stack.47.flag_ref.refs_0_
  6.3 0.0 collective-permute-done.refs_7_
  6.3 0.2 collective-permute-done.4.small_ref.refs_5_.small_sib_ref
  6.5 0.0 collective-permute-done.3.w_ref.refs_12_
  6.5 1.2 %copy-done = bf16[16,64,512]{2,1,0:T(8,128)(2,1)S(1)} copy-done((bf16[16,64,512]{2,1,0:T(8,128)(2,1)S(1)}, bf16[16,64,512]{2,1,0:T(8,128)(2,1)}, u32[]{:S(2)}) %copy-start) | copy-done | bytes 1048600
  7.7 0.0 copy-start.4
  7.7 0.0 copy-start.5
  7.8 1.9 %expand_first.1 = (bf16[8,80,1024]{2,1,0:T(8,128)(2,1)S(1)}, bf16[8,64,512]{2,1,0:T(8,128)(2,1)S(1)}, bf16[8,80,512]{2,1,0:T(8,128)(2,1)S(1)}) custom-call(s32[7]{0:T(128)S(1)} %stack.47.flag_ref.refs_0_, bf16[2,8,64,512]{3,2,1,0:T(8,128)(2,1)S(1)} %bitcast.18, bf16[512,1024]{1,0:T(8,128)(2,1)S(1)} %collective-permute-done.3.w_ref.refs_12_, ...), custom_call_target="tpu_custom_call" | custom-call | flops 4294967296 | bytes 4194304 | tf_op jit(solution)/shard_map/expand_first/pallas_call | solution.py:240
  9.6 0.0 collective-permute-done.1.refs_8_
  9.6 0.0 collective-permute-done.2.refs_9_
  9.7 0.0 copy-done.6
  9.7 2.9 %collective-permute-start.5 = (bf16[18,512]{1,0:T(8,128)(2,1)S(1)}, bf16[18,512]{1,0:T(8,128)(2,1)S(1)}, u32[]{:S(2)}, u32[]{:S(2)}) collective-permute-start(bf16[18,512]{1,0:T(8,128)(2,1)S(1)} %pad_maximum_fusion), channel_id=1, source_target_pairs={{0,2},{2,0},{1,3},{3,1},{4,6},{6,4},{5,7},{7,5},{8,10},{10,8},{9,1... | collective-permute-start | bytes 55304 | tf_op jit(solution)/shard_map/ppermute | solution.py:614
  12.6 0.0 copy-done.1
  12.6 0.0 copy-done.2
  12.6 0.0 copy-done.3
  12.6 0.0 copy-done.4
  12.6 0.0 copy-done.5
  12.6 1.4 %expand_second.1 = (bf16[8,80,1024]{2,1,0:T(8,128)(2,1)S(1)}, bf16[512,1024]{1,0:T(8,128)(2,1)S(1)}, bf16[1024,512]{1,0:T(8,128)(2,1)S(1)}, bf16[3,512,256]{2,1,0:T(8,128)(2,1)S(1)}, bf16[256,512]{1,0:T(8,128)(2,1)S(1)}) custom-call(bf16[8,80,512]{2,1,0:T(8,128)(2,1)S(1)} %get-tuple-element.60.ordered_ref, bf16[512,1024]{1,0:T(8,128)(2,1)S(1)} %copy-done.1, ...), custom_call_target="tpu_custom_call" | custom-call | flops 671088640 | bytes 1310720 | tf_op jit(solution)/shard_map/expand_second/pallas_call | solution.py:272
  14.0 0.4 collective-permute-done.5.refs_10_
  14.4 0.0 collective-permute-start.6
  14.4 0.5 collective-permute-start.7
  14.9 4.0 %deepen.2 = (bf16[64,512]{1,0:T(8,128)(2,1)S(1)}, bf16[64,512]{1,0:T(8,128)(2,1)S(1)}, bf16[64,512]{1,0:T(8,128)(2,1)S(1)}, bf16[64,512]{1,0:T(8,128)(2,1)S(1)},...) custom-call(s32[7]{0:T(128)S(1)} %stack.47.flag_ref.refs_0_, ...), custom_call_target="tpu_custom_call" | custom-call | flops 536870912 | bytes 2621440 | tf_op jit(solution)/shard_map/deepen/pallas_call | solution.py:410
  19.0 0.0 collective-permute-done.7.wo_sib_ref
  19.0 0.0 collective-permute-done.6.wqkv_sib_ref
  19.0 4.1 %collective-permute-start.8 = (bf16[64,512]{1,0:T(8,128)(2,1)S(1)}, bf16[64,512]{1,0:T(8,128)(2,1)S(1)}, u32[]{:S(2)}, u32[]{:S(2)}) collective-permute-start(bf16[64,512]{1,0:T(8,128)(2,1)S(1)} %get-tuple-element.80.refs_10_), channel_id=1, source_target_pairs={{0,8},{2,10},{4,12},{6,14},{8,0},{10,2},{12,4},{14,6},{1,9},{3,11}... | collective-permute-start | bytes 196616 | tf_op jit(solution)/shard_map/ppermute | solution.py:622
  23.1 1.0 %collective-permute-start.9 = (bf16[64,512]{1,0:T(8,128)(2,1)S(1)}, bf16[64,512]{1,0:T(8,128)(2,1)S(1)}, u32[]{:S(2)}, u32[]{:S(2)}) collective-permute-start(bf16[64,512]{1,0:T(8,128)(2,1)S(1)} %get-tuple-element.81.refs_11_), channel_id=1, source_target_pairs={{0,10},{2,8},{4,14},{6,12},{8,2},{10,0},{12,6},{14,4},{1,11},{3,9}... | collective-permute-start | bytes 196616 | tf_op jit(solution)/shard_map/ppermute | solution.py:622
  24.1 3.0 %collective-permute-start.10 = (bf16[64,512]{1,0:T(8,128)(2,1)S(1)}, bf16[64,512]{1,0:T(8,128)(2,1)S(1)}, u32[]{:S(2)}, u32[]{:S(2)}) collective-permute-start(bf16[64,512]{1,0:T(8,128)(2,1)S(1)} %get-tuple-element.82.refs_12_), channel_id=1, source_target_pairs={{0,12},{2,14},{4,8},{6,10},{8,4},{10,6},{12,0},{14,2},{1,13},{3,15... | collective-permute-start | bytes 196616 | tf_op jit(solution)/shard_map/ppermute | solution.py:622
  27.0 0.8 %collective-permute-start.11 = (bf16[64,512]{1,0:T(8,128)(2,1)S(1)}, bf16[64,512]{1,0:T(8,128)(2,1)S(1)}, u32[]{:S(2)}, u32[]{:S(2)}) collective-permute-start(bf16[64,512]{1,0:T(8,128)(2,1)S(1)} %get-tuple-element.83.refs_13_), channel_id=1, source_target_pairs={{0,14},{2,12},{4,10},{6,8},{8,6},{10,4},{12,2},{14,0},{1,15},{3,13... | collective-permute-start | bytes 196616 | tf_op jit(solution)/shard_map/ppermute | solution.py:622
  27.9 3.0 %deepen.3 = (bf16[64,512]{1,0:T(8,128)(2,1)S(1)}, bf16[64,512]{1,0:T(8,128)(2,1)S(1)}, bf16[64,512]{1,0:T(8,128)(2,1)S(1)}, bf16[64,512]{1,0:T(8,128)(2,1)S(1)}) custom-call(s32[7]{0:T(128)S(1)} %stack.47.flag_ref.refs_0_, bf16[8,80,1024]{2,1,0:T(8,128)(2,1)S(1)} %get-tuple-element.64.refs_1_, bf16[8,80,1024]{2,1,0:T(8,128)(2,1)S(1)} %get-tuple-element.65.refs_2_, ...), custom_call_target="tpu_custom_call" | custom-call | flops 536870912 | bytes 2621440 | tf_op jit(solution)/shard_map/deepen/pallas_call | solution.py:410
  30.9 0.0 collective-permute-done.8.rest_0_
  30.9 1.5 %collective-permute-start.12 = (bf16[64,512]{1,0:T(8,128)(2,1)S(1)}, bf16[64,512]{1,0:T(8,128)(2,1)S(1)}, u32[]{:S(2)}, u32[]{:S(2)}) collective-permute-start(bf16[64,512]{1,0:T(8,128)(2,1)S(1)} %get-tuple-element.89), channel_id=1, source_target_pairs={{0,6},{2,4},{4,2},{6,0},{8,14},{10,12},{12,10},{14,8},{1,7},{3,5},... | collective-permute-start | bytes 196616 | tf_op jit(solution)/shard_map/ppermute | solution.py:622
  32.4 1.5 %collective-permute-start.13 = (bf16[64,512]{1,0:T(8,128)(2,1)S(1)}, bf16[64,512]{1,0:T(8,128)(2,1)S(1)}, u32[]{:S(2)}, u32[]{:S(2)}) collective-permute-start(bf16[64,512]{1,0:T(8,128)(2,1)S(1)} %get-tuple-element.90), channel_id=1, source_target_pairs={{0,4},{2,6},{4,0},{6,2},{8,12},{10,14},{12,8},{14,10},{1,5},{3,7},... | collective-permute-start | bytes 196616 | tf_op jit(solution)/shard_map/ppermute | solution.py:622
  33.9 0.0 collective-permute-done.9.rest_1_
  33.9 0.5 collective-permute-start.14
  34.5 0.0 collective-permute-done.10.rest_2_
  34.5 0.0 collective-permute-done.11.rest_3_
  34.5 1.9 %collective-permute-done.12.rest_4_ = bf16[64,512]{1,0:T(8,128)(2,1)S(1)} collective-permute-done((bf16[64,512]{1,0:T(8,128)(2,1)S(1)}, bf16[64,512]{1,0:T(8,128)(2,1)S(1)}, u32[]{:S(2)}, u32[]{:S(2)}) %collective-permute-start.12) | collective-permute-done | bytes 65568 | tf_op jit(solution)/shard_map/ppermute | solution.py:622
  36.3 0.5 collective-permute-done.13.rest_5_
  36.9 1.3 %collective-permute-done.14.rest_6_ = bf16[64,512]{1,0:T(8,128)(2,1)S(1)} collective-permute-done((bf16[64,512]{1,0:T(8,128)(2,1)S(1)}, bf16[64,512]{1,0:T(8,128)(2,1)S(1)}, u32[]{:S(2)}, u32[]{:S(2)}) %collective-permute-start.14) | collective-permute-done | bytes 65568 | tf_op jit(solution)/shard_map/ppermute | solution.py:622
  38.2 3.6 %attend.1 = bf16[8,2,64,256]{3,2,1,0:T(8,128)(2,1)S(1)} custom-call(s32[7]{0:T(128)S(1)} %stack.47.flag_ref.refs_0_, bf16[3,512,256]{2,1,0:T(8,128)(2,1)S(1)} %get-tuple-element.63.wqkv_ref, bf16[3,512,256]{2,1,0:T(8,128)(2,1)S(1)} %collective-permute-done.6.wqkv_sib_ref, bf16[256,512]{1,0:T(8,128)(2,1)S(1)} %get-tuple-element.75.wo_ref, ...), custom_call_target="tpu_custom_call" | custom-call | flops 1073741824 | bytes 1048576 | tf_op jit(solution)/shard_map/attend/pallas_call | solution.py:498
  41.8 19.2 %all_to_all.5.arrived_ref = bf16[16,64,256]{2,1,0:T(8,128)(2,1)S(1)} all-to-all(bf16[16,64,256]{2,1,0:T(8,128)(2,1)S(1)} %bitcast.20), channel_id=1, replica_groups=mesh['grp'=2,'gy'=4,'gx'=2,'ch'=2] {'gy','gx','ch'}, dimensions={0} | all-to-all | bytes 1048576 | tf_op jit(solution)/shard_map/all_to_all | solution.py:679
  61.0 1.1 %lay_out.1 = bf16[2,8,64,256]{3,2,1,0:T(8,128)(2,1)} custom-call(bf16[16,64,256]{2,1,0:T(8,128)(2,1)S(1)} %all_to_all.5.arrived_ref), custom_call_target="tpu_custom_call" | custom-call | tf_op jit(solution)/shard_map/lay_out/pallas_call | solution.py:590
  (7 shorter events, 0.0 us)
Async XLA Ops:
  1.9 4.4 %collective-permute-start = (bf16[1024,512]{1,0:T(8,128)(2,1)}, bf16[1024,512]{1,0:T(8,128)(2,1)S(1)}, u32[]{:S(2)}, u32[]{:S(2)}) collective-permute-start(bf16[1024,512]{1,0:T(8,128)(2,1)} %refs_0_), channel_id=1, source_target_pairs={{0,1},{1,0},{2,3},{3,2},{4,5},{5,4},{6,7},{7,6},{8,9},{9,8},{10,11... | collective-permute-start | bytes 3145736 | tf_op jit(solution)/shard_map/ppermute | solution.py:644
  2.4 4.1 %collective-permute-start.3 = (bf16[512,1024]{1,0:T(8,128)(2,1)}, bf16[512,1024]{1,0:T(8,128)(2,1)S(1)}, u32[]{:S(2)}, u32[]{:S(2)}) collective-permute-start(bf16[512,1024]{1,0:T(8,128)(2,1)} %w_ref), channel_id=1, source_target_pairs={{0,1},{1,0},{2,3},{3,2},{4,5},{5,4},{6,7},{7,6},{8,9},{9,8},{10,11... | collective-permute-start | bytes 3145736 | tf_op jit(solution)/shard_map/ppermute | solution.py:644
  2.5 4.0 %collective-permute-start.4 = (f32[16,1024]{1,0:T(8,128)}, f32[16,1024]{1,0:T(8,128)S(1)}, u32[]{:S(2)}, u32[]{:S(2)}) collective-permute-start(f32[16,1024]{1,0:T(8,128)} %get-tuple-element.55.small_ref.refs_4_), channel_id=1, source_target_pairs={{0,1},{1,0},{2,3},{3,2},{4,5},{5,4},{6,7},{7,6},{8,9},{9,8},{10,11... | collective-permute-start | bytes 196616 | tf_op jit(solution)/shard_map/ppermute | solution.py:644
  2.9 6.7 %collective-permute-start.1 = (bf16[64,512]{1,0:T(8,128)(2,1)}, bf16[64,512]{1,0:T(8,128)(2,1)S(1)}, u32[]{:S(2)}, u32[]{:S(2)}) collective-permute-start(bf16[64,512]{1,0:T(8,128)(2,1)} %get-tuple-element.52), channel_id=1, source_target_pairs={{0,4},{8,12},{4,0},{12,8},{1,5},{9,13},{5,1},{13,9},{2,6},{10,14},... | collective-permute-start | bytes 196616 | tf_op jit(solution)/shard_map/ppermute | solution.py:606
  5.6 4.1 %collective-permute-start.2 = (bf16[64,512]{1,0:T(8,128)(2,1)}, bf16[64,512]{1,0:T(8,128)(2,1)S(1)}, u32[]{:S(2)}, u32[]{:S(2)}) collective-permute-start(bf16[64,512]{1,0:T(8,128)(2,1)} %get-tuple-element.53), channel_id=1, source_target_pairs={{4,8},{8,4},{5,9},{9,5},{6,10},{10,6},{7,11},{11,7},{20,24},{24,20... | collective-permute-start | bytes 196616 | tf_op jit(solution)/shard_map/ppermute | solution.py:606
  6.5 1.2 %copy-start = (bf16[16,64,512]{2,1,0:T(8,128)(2,1)S(1)}, bf16[16,64,512]{2,1,0:T(8,128)(2,1)}, u32[]{:S(2)}) copy-start(bf16[16,64,512]{2,1,0:T(8,128)(2,1)} %cells_hbm.1) | copy-start | bytes 3145732
  7.7 1.9 %copy-start.6 = (bf16[16,512]{1,0:T(8,128)(2,1)S(1)}, bf16[16,512]{1,0:T(8,128)(2,1)}, u32[]{:S(2)}) copy-start(bf16[16,512]{1,0:T(8,128)(2,1)} %get-tuple-element.59) | copy-start | bytes 49156
  7.7 4.9 %copy-start.1 = (bf16[512,1024]{1,0:T(8,128)(2,1)S(1)}, bf16[512,1024]{1,0:T(8,128)(2,1)}, u32[]{:S(2)}) copy-start(bf16[512,1024]{1,0:T(8,128)(2,1)} %w_ref) | copy-start | bytes 3145732
  7.7 4.9 %copy-start.2 = (bf16[1024,512]{1,0:T(8,128)(2,1)S(1)}, bf16[1024,512]{1,0:T(8,128)(2,1)}, u32[]{:S(2)}) copy-start(bf16[1024,512]{1,0:T(8,128)(2,1)} %refs_0_) | copy-start | bytes 3145732
  7.7 4.9 %copy-start.3 = (bf16[512,3,256]{2,0,1:T(8,128)(2,1)S(1)}, bf16[512,3,256]{2,0,1:T(8,128)(2,1)}, u32[]{:S(2)}) copy-start(bf16[512,3,256]{2,0,1:T(8,128)(2,1)} %param.19) | copy-start | bytes 2359300
  7.7 4.9 %copy-start.4 = (f32[16,1024]{1,0:T(8,128)S(1)}, f32[16,1024]{1,0:T(8,128)}, u32[]{:S(2)}) copy-start(f32[16,1024]{1,0:T(8,128)} %get-tuple-element.55.small_ref.refs_4_) | copy-start | bytes 196612
  7.7 4.9 %copy-start.5 = (bf16[256,512]{1,0:T(8,128)(2,1)S(1)}, bf16[256,512]{1,0:T(8,128)(2,1)}, u32[]{:S(2)}) copy-start(bf16[256,512]{1,0:T(8,128)(2,1)} %refs_2_.1) | copy-start | bytes 786436
  9.7 4.7 %collective-permute-start.5 = (bf16[18,512]{1,0:T(8,128)(2,1)S(1)}, bf16[18,512]{1,0:T(8,128)(2,1)S(1)}, u32[]{:S(2)}, u32[]{:S(2)}) collective-permute-start(bf16[18,512]{1,0:T(8,128)(2,1)S(1)} %pad_maximum_fusion), channel_id=1, source_target_pairs={{0,2},{2,0},{1,3},{3,1},{4,6},{6,4},{5,7},{7,5},{8,10},{10,8},{9,1... | collective-permute-start | bytes 55304 | tf_op jit(solution)/shard_map/ppermute | solution.py:614
  14.4 4.6 %collective-permute-start.6 = (bf16[3,512,256]{2,1,0:T(8,128)(2,1)S(1)}, bf16[3,512,256]{2,1,0:T(8,128)(2,1)S(1)}, u32[]{:S(2)}, u32[]{:S(2)}) collective-permute-start(bf16[3,512,256]{2,1,0:T(8,128)(2,1)S(1)} %get-tuple-element.63.wqkv_ref), channel_id=1, source_target_pairs={{0,1},{1,0},{2,3},{3,2},{4,5},{5,4},{6,7},{7,6},{8,9},{9,8},{10,11... | collective-permute-start | bytes 2359304 | tf_op jit(solution)/shard_map/ppermute | solution.py:644
  14.4 4.5 %collective-permute-start.7 = (bf16[256,512]{1,0:T(8,128)(2,1)S(1)}, bf16[256,512]{1,0:T(8,128)(2,1)S(1)}, u32[]{:S(2)}, u32[]{:S(2)}) collective-permute-start(bf16[256,512]{1,0:T(8,128)(2,1)S(1)} %get-tuple-element.75.wo_ref), channel_id=1, source_target_pairs={{0,1},{1,0},{2,3},{3,2},{4,5},{5,4},{6,7},{7,6},{8,9},{9,8},{10,11... | collective-permute-start | bytes 786440 | tf_op jit(solution)/shard_map/ppermute | solution.py:644
  19.0 11.9 %collective-permute-start.8 = (bf16[64,512]{1,0:T(8,128)(2,1)S(1)}, bf16[64,512]{1,0:T(8,128)(2,1)S(1)}, u32[]{:S(2)}, u32[]{:S(2)}) collective-permute-start(bf16[64,512]{1,0:T(8,128)(2,1)S(1)} %get-tuple-element.80.refs_10_), channel_id=1, source_target_pairs={{0,8},{2,10},{4,12},{6,14},{8,0},{10,2},{12,4},{14,6},{1,9},{3,11}... | collective-permute-start | bytes 196616 | tf_op jit(solution)/shard_map/ppermute | solution.py:622
  23.1 10.8 %collective-permute-start.9 = (bf16[64,512]{1,0:T(8,128)(2,1)S(1)}, bf16[64,512]{1,0:T(8,128)(2,1)S(1)}, u32[]{:S(2)}, u32[]{:S(2)}) collective-permute-start(bf16[64,512]{1,0:T(8,128)(2,1)S(1)} %get-tuple-element.81.refs_11_), channel_id=1, source_target_pairs={{0,10},{2,8},{4,14},{6,12},{8,2},{10,0},{12,6},{14,4},{1,11},{3,9}... | collective-permute-start | bytes 196616 | tf_op jit(solution)/shard_map/ppermute | solution.py:622
  24.1 10.4 %collective-permute-start.10 = (bf16[64,512]{1,0:T(8,128)(2,1)S(1)}, bf16[64,512]{1,0:T(8,128)(2,1)S(1)}, u32[]{:S(2)}, u32[]{:S(2)}) collective-permute-start(bf16[64,512]{1,0:T(8,128)(2,1)S(1)} %get-tuple-element.82.refs_12_), channel_id=1, source_target_pairs={{0,12},{2,14},{4,8},{6,10},{8,4},{10,6},{12,0},{14,2},{1,13},{3,15... | collective-permute-start | bytes 196616 | tf_op jit(solution)/shard_map/ppermute | solution.py:622
  27.0 7.4 %collective-permute-start.11 = (bf16[64,512]{1,0:T(8,128)(2,1)S(1)}, bf16[64,512]{1,0:T(8,128)(2,1)S(1)}, u32[]{:S(2)}, u32[]{:S(2)}) collective-permute-start(bf16[64,512]{1,0:T(8,128)(2,1)S(1)} %get-tuple-element.83.refs_13_), channel_id=1, source_target_pairs={{0,14},{2,12},{4,10},{6,8},{8,6},{10,4},{12,2},{14,0},{1,15},{3,13... | collective-permute-start | bytes 196616 | tf_op jit(solution)/shard_map/ppermute | solution.py:622
  30.9 5.4 %collective-permute-start.12 = (bf16[64,512]{1,0:T(8,128)(2,1)S(1)}, bf16[64,512]{1,0:T(8,128)(2,1)S(1)}, u32[]{:S(2)}, u32[]{:S(2)}) collective-permute-start(bf16[64,512]{1,0:T(8,128)(2,1)S(1)} %get-tuple-element.89), channel_id=1, source_target_pairs={{0,6},{2,4},{4,2},{6,0},{8,14},{10,12},{12,10},{14,8},{1,7},{3,5},... | collective-permute-start | bytes 196616 | tf_op jit(solution)/shard_map/ppermute | solution.py:622
  32.4 4.4 %collective-permute-start.13 = (bf16[64,512]{1,0:T(8,128)(2,1)S(1)}, bf16[64,512]{1,0:T(8,128)(2,1)S(1)}, u32[]{:S(2)}, u32[]{:S(2)}) collective-permute-start(bf16[64,512]{1,0:T(8,128)(2,1)S(1)} %get-tuple-element.90), channel_id=1, source_target_pairs={{0,4},{2,6},{4,0},{6,2},{8,12},{10,14},{12,8},{14,10},{1,5},{3,7},... | collective-permute-start | bytes 196616 | tf_op jit(solution)/shard_map/ppermute | solution.py:622
  33.9 4.3 %collective-permute-start.14 = (bf16[64,512]{1,0:T(8,128)(2,1)S(1)}, bf16[64,512]{1,0:T(8,128)(2,1)S(1)}, u32[]{:S(2)}, u32[]{:S(2)}) collective-permute-start(bf16[64,512]{1,0:T(8,128)(2,1)S(1)} %get-tuple-element.91), channel_id=1, source_target_pairs={{0,2},{2,0},{4,6},{6,4},{8,10},{10,8},{12,14},{14,12},{1,3},{3,1},... | collective-permute-start | bytes 196616 | tf_op jit(solution)/shard_map/ppermute | solution.py:622

commit v4 on v3

--- a/solution.py
+++ b/solution.py
@@ -426,26 +426,67 @@
     )(flags, *operands, *after)
 
 
+def project_heads(values, small_ref, weights, out_ref):
+    windows, tokens, width = values.shape
+    full = values.reshape(windows * tokens, width)
+    centred = full - jnp.mean(full, axis=-1, keepdims=True)
+    spread = jnp.mean(centred * centred, axis=-1, keepdims=True)
+    normed = (centred * lax.rsqrt(spread + 1e-05) * small_ref[GAIN, :width]).astype(jnp.bfloat16)
+    for side, weight in enumerate(weights):
+        half = weight.shape[2]
+        for kind in range(3):
+            projected = jnp.dot(normed, weight[kind], preferred_element_type=jnp.float32)
+            out_ref[kind, :, :, side * half : (side + 1) * half] = projected.astype(
+                jnp.bfloat16
+            ).reshape(windows, tokens, half)
+
+
+def gather(xs, values):
+    for source, x in enumerate(xs):
+        tokens, width = x.shape
+        values[:, source] = x[...].astype(jnp.float32).reshape(-1, SUBLANES, width)
+
+
+def early_kernel(wqkv_ref, wqkv_sib_ref, small_ref, *refs):
+    *xs, out_ref, values = refs
+    gather(xs, values)
+    windows, sources, _, width = values.shape
+    grouped = values[...].reshape(windows, sources * SUBLANES, width)
+    project_heads(grouped, small_ref, (wqkv_ref, wqkv_sib_ref), out_ref)
+
+
+def project_early(arrived, weights, small):
+    tokens, width = arrived[0].shape
+    windows, sources = tokens // SUBLANES, len(arrived)
+    operands = (*weights, small, *arrived)
+    return pl.pallas_call(
+        early_kernel,
+        in_specs=in_vmem(len(operands)),
+        out_specs=pl.BlockSpec(memory_space=pltpu.VMEM),
+        out_shape=jax.ShapeDtypeStruct((3, windows, sources * SUBLANES, width), jnp.bfloat16),
+        scratch_shapes=[pltpu.VMEM((windows, sources, SUBLANES, width), jnp.float32)],
+        compiler_params=pltpu.CompilerParams(vmem_limit_bytes=VMEM_BYTES),
+        cost_estimate=pl.CostEstimate(
+            flops=6 * sources * tokens * width * width, bytes_accessed=0, transcendentals=0
+        ),
+        name="project_early",
+    )(*operands)
+
+
 def attend_kernel(
-    plan, targets, flag_ref, wqkv_ref, wqkv_sib_ref, wo_ref, wo_sib_ref, small_ref, small_sib_ref, *rest
+    plan, targets, flag_ref, early_ref, wqkv_ref, wqkv_sib_ref, wo_ref, wo_sib_ref, small_ref, small_sib_ref,
+    *rest,
 ):
     sources = len(targets)
-    xs, (out_ref, values, qkv, attended) = rest[:sources], rest[sources:]
+    xs, (out_ref, values, late, attended) = rest[:sources], rest[sources:]
     tokens, width = xs[0].shape
     windows = tokens // SUBLANES
     span = sources * SUBLANES
     half = wo_ref.shape[0]
-    for source in range(sources):
-        values[:, source] = xs[source][...].astype(jnp.float32).reshape(windows, SUBLANES, width)
-    full = values[...].reshape(windows * span, width)
-    centred = full - jnp.mean(full, axis=-1, keepdims=True)
-    spread = jnp.mean(centred * centred, axis=-1, keepdims=True)
-    normed = (centred * lax.rsqrt(spread + 1e-05) * small_ref[GAIN, :width]).astype(jnp.bfloat16)
-    for side, weight in enumerate((wqkv_ref, wqkv_sib_ref)):
-        for kind in range(3):
-            qkv[kind, :, side * half : (side + 1) * half] = jnp.dot(
-                normed, weight[kind], preferred_element_type=jnp.float32
-            ).astype(jnp.bfloat16)
+    gather(xs, values)
+    first_late = early_ref.shape[2] // SUBLANES
+    grouped = values[:, first_late:].reshape(windows, span - first_late * SUBLANES, width)
+    project_heads(grouped, small_ref, (wqkv_ref, wqkv_sib_ref), late)
     heads = 128 // HEAD_DIM
     lane = lax.broadcasted_iota(jnp.int32, (1, 128), 1) // HEAD_DIM
     scale = HEAD_DIM ** (-0.5) * np.log2(np.e)
@@ -453,7 +494,10 @@
         rows = slice(window * span, (window + 1) * span)
         for low in range(0, width, 128):
             lanes = slice(low, low + 128)
-            query, keys, value = (qkv[kind, rows, lanes] for kind in range(3))
+            query, keys, value = (
+                jnp.concatenate([part[kind, window, :, lanes] for part in (early_ref, late)], axis=0)
+                for kind in range(3)
+            )
             spread_query = jnp.concatenate(
                 [jnp.where(lane == h, query, jnp.zeros_like(query)) for h in range(heads)], axis=0
             )
@@ -489,12 +533,12 @@
             out_ref[target, core] = part[:, core * half : (core + 1) * half]
 
 
-def attend_windows(plan, targets, flags, arrived, weights):
+def attend_windows(plan, targets, flags, early, arrived, weights):
     tokens, width = arrived[0].shape
     sources = len(targets)
     windows = tokens // SUBLANES
     half = width // plan.n_ch
-    operands = (*weights, *arrived)
+    operands = (early, *weights, *arrived)
     return pl.pallas_call(
         functools.partial(attend_kernel, plan, targets),
         in_specs=[pl.BlockSpec(memory_space=pltpu.SMEM)] + in_vmem(len(operands)),
@@ -502,7 +546,7 @@
         out_shape=jax.ShapeDtypeStruct((sources, plan.n_ch, tokens, half), jnp.bfloat16),
         scratch_shapes=[
             pltpu.VMEM((windows, sources, SUBLANES, width), jnp.float32),
-            pltpu.VMEM((3, sources * tokens, width), jnp.bfloat16),
+            pltpu.VMEM((3, windows, sources * SUBLANES - early.shape[2], width), jnp.bfloat16),
             pltpu.VMEM((sources * tokens, width), jnp.bfloat16),
         ],
         compiler_params=pltpu.CompilerParams(vmem_limit_bytes=VMEM_BYTES),
@@ -643,18 +687,18 @@
     def both(value):
         return value, lax.ppermute(value, "ch", [(0, 1), (1, 0)])
 
-    w_expand, w_project, small = both(w_expand), both(w_project), both(small)
-    flags, w_project_sib = lax.optimization_barrier((flags, w_project[1]))
-    e_sib, x, ordered = expand_first(plan, flags, cells, w_expand[1], small[1])
+    w_expand, small = both(w_expand), both(small)
+    e_sib, x, ordered = expand_first(plan, flags, both(cells)[1], w_expand[1], small[1])
     e_own, *kept = expand_second(
-        plan, ordered, w_expand[0], small[0], (w_project[0], w_qkv.transpose(1, 0, 2), w_out)
-    )
-    *rows, x = lax.optimization_barrier((*rows, x))
+        plan, ordered, w_expand[0], small[0], (w_project, w_qkv.transpose(1, 0, 2), w_out)
+    )
+    *rows, x, w_project = lax.optimization_barrier((*rows, x, w_project))
+    w_project = both(w_project)
     e = e_own, e_sib
     cols = halo_column(column, rows, index, even)
     cols, w_qkv, w_out = lax.optimization_barrier((cols, *kept[2:]))
     w_qkv, w_out = both(w_qkv), both(w_out)
-    w_project = kept[1], w_project_sib
+    w_project = kept[1], w_project[1]
     far = [(dy, dx) for dy in (2, 3) for dx in (0, 1)]
     near = [(1, 1), (1, 0), (0, 1), (0, 0)]
     outside = (*rows, cols, kept[0], w_expand[1])
@@ -672,9 +716,8 @@
         arrived += [
             value if target == (0, 0) else send_to(value, *target) for value, target in zip(sent, targets)
         ]
-    leaving = attend_windows(
-        plan, far + near, flags, arrived, (*w_qkv, *w_out, *small)
-    )
+    early = project_early(arrived[: len(far)], w_qkv, small[0])
+    leaving = attend_windows(plan, far + near, flags, early, arrived, (*w_qkv, *w_out, *small))
     leaving = leaving.reshape((n_rows * n_cols * n_ch,) + leaving.shape[2:])
     returned = lax.all_to_all(leaving, ("gy", "gx", "ch"), 0, 0, tiled=True)
     return lay_out(plan, returned).reshape(cells.shape[0], cells.shape[1], -1)

time: 62.3 us -> 60.3 us (0.968)
  blocking collectives: 19.2 us -> 17.6 us
  local copies, waits for them, and re-layouts: 1.34 us -> 0.12 us
  starting transfers between devices: 20.2 us -> 21.4 us
  waiting for transfers between devices: 4.31 us -> 3.6 us
    all_to_all x1, blocking collectives: 19.2 us -> 17.6 us  [fast_device(): returned = lax.all_to_all(leaving, ('gy', 'gx', 'ch'), 0, 0, tiled=True)]
    unnamed x14 -> x12, local copies, waits for them, and re-layouts: 1.25 us -> 0.03 us
    ppermute x7, starting transfers between devices: 12.5 us -> 13.5 us  [send_to(): return lax.ppermute(value, ('gy', 'gx'), pairs)]
    ppermute x7, waiting for transfers between devices: 3.73 us -> 2.96 us  [send_to(): return lax.ppermute(value, ('gy', 'gx'), pairs)]
    pallas_call x0 -> x1, Pallas kernels: none -> 0.76 us  [project_early(): pl.pallas_call(early_kernel, in_specs=in_vmem(len(operands)), out_specs=p...]
    ppermute x5 -> x6, starting transfers between devices: 1.54 us -> 1.95 us  [both(): return (value, lax.ppermute(value, 'ch', [(0, 1), (1, 0)]))]
  transfers between devices with their start and end apart: 15 -> 16, of which waited for: 5 -> 6; matrix products, arithmetic and copies ran while one was open for 0% -> 0% of each run, Pallas kernels for 17% -> 18%
where the time goes in v4:
time: 60.3 us; the launch traced here: 60.1 us
  starting transfers between devices  21.4 us (35%)
  blocking collectives  17.6 us (29%)
  Pallas kernels  17.1 us (28%)
  waiting for transfers between devices  3.6 us (6%)
    all_to_all x1, blocking collectives, fast_device(): returned = lax.all_to_all(leaving, ('gy', 'gx', 'ch'), 0, 0, tiled=True)  17.6 us
    ppermute x7, starting transfers between devices, send_to(): return lax.ppermute(value, ('gy', 'gx'), pairs)  13.5 us
    pallas_call x2, Pallas kernels, deepen(): pl.pallas_call(functools.partial(deepen_kernel, plan, targets, first), in...  7.07 us
    ppermute x2, starting transfers between devices, swap_rows(): lax.ppermute(value, 'gy', pairs + [(target, source) for source, target in...  3.3 us
    pallas_call x1, Pallas kernels, attend_windows(): pl.pallas_call(functools.partial(attend_kernel, plan, targets), in_specs=...  3.12 us
    ppermute x7, waiting for transfers between devices, send_to(): return lax.ppermute(value, ('gy', 'gx'), pairs)  2.96 us
    ppermute x1, starting transfers between devices, halo_column(): return lax.ppermute(jnp.concatenate(parts, axis=0), 'gx', [(0, 1), (1, 0)])  2.7 us
    ppermute x6, starting transfers between devices, both(): return (value, lax.ppermute(value, 'ch', [(0, 1), (1, 0)]))  1.95 us
  transfers between devices with their start and end apart: 16, of which 6 were waited for; matrix products, arithmetic and copies ran while one was open for 0% of the time, Pallas kernels for 18%

profile of v4, /device:TPU:0, one launch (start us, length us, event | category | flops | bytes accessed | tf_op | source)
XLA Modules:
  0.0 60.1 jit_solution(15988565212617697839)
XLA Ops:
  0.0 1.9 %edges.1 = (bf16[64,512]{1,0:T(8,128)(2,1)}, bf16[64,512]{1,0:T(8,128)(2,1)}, bf16[16,512]{1,0:T(8,128)(2,1)}, f32[16,1024]{1,0:T(8,128)}) custom-call(s32[1]{0:T(128)} %bitcast.7.column_ref, s32[1]{0:T(128)} %bitcast.8.row_ref, bf16[16,64,512]{2,1,0:T(8,128)(2,1)} %cells_hbm.1, bf16[3,3,1024]{2,1,0:T(4,128)(2,1)} %taps_hbm.1, f32[1,1024]{1,0:T(1,128)} %bitcast.21, ...), custom_call_target="tpu_custom_call" | custom-call | tf_op jit(solution)/shard_map/edges/pallas_call | solution.py:596
  1.9 0.5 collective-permute-start.3
  2.4 0.1 collective-permute-start.2
  2.5 0.4 collective-permute-start.4
  2.9 2.7 %collective-permute-start = (bf16[64,512]{1,0:T(8,128)(2,1)}, bf16[64,512]{1,0:T(8,128)(2,1)S(1)}, u32[]{:S(2)}, u32[]{:S(2)}) collective-permute-start(bf16[64,512]{1,0:T(8,128)(2,1)} %get-tuple-element.49), channel_id=1, source_target_pairs={{0,4},{8,12},{4,0},{12,8},{1,5},{9,13},{5,1},{13,9},{2,6},{10,14},... | collective-permute-start | bytes 196616 | tf_op jit(solution)/shard_map/ppermute | solution.py:650
  5.6 0.7 %collective-permute-start.1 = (bf16[64,512]{1,0:T(8,128)(2,1)}, bf16[64,512]{1,0:T(8,128)(2,1)S(1)}, u32[]{:S(2)}, u32[]{:S(2)}) collective-permute-start(bf16[64,512]{1,0:T(8,128)(2,1)} %get-tuple-element.50), channel_id=1, source_target_pairs={{4,8},{8,4},{5,9},{9,5},{6,10},{10,6},{7,11},{11,7},{20,24},{24,20... | collective-permute-start | bytes 196616 | tf_op jit(solution)/shard_map/ppermute | solution.py:650
  6.2 0.1 stack.47.flag_ref.refs_0_
  6.3 0.2 collective-permute-done.4.small_ref.refs_5_.small_sib_ref
  6.5 0.0 collective-permute-done.3.w_ref.refs_12_
  6.5 0.0 collective-permute-done.2
  6.5 0.0 copy-start
  6.5 0.0 copy-start.1
  6.5 0.0 copy-start.3
  6.5 0.0 copy-start.4
  6.6 1.8 %expand_first.1 = (bf16[8,80,1024]{2,1,0:T(8,128)(2,1)S(1)}, bf16[8,64,512]{2,1,0:T(8,128)(2,1)S(1)}, bf16[8,80,512]{2,1,0:T(8,128)(2,1)S(1)}) custom-call(s32[7]{0:T(128)S(1)} %stack.47.flag_ref.refs_0_, bf16[2,8,64,512]{3,2,1,0:T(8,128)(2,1)S(1)} %bitcast.20, bf16[512,1024]{1,0:T(8,128)(2,1)S(1)} %collective-permute-done.3.w_ref.refs_12_, ...), custom_call_target="tpu_custom_call" | custom-call | flops 4294967296 | bytes 4194304 | tf_op jit(solution)/shard_map/expand_first/pallas_call | solution.py:240
  8.4 0.1 collective-permute-done.refs_8_
  8.5 0.0 collective-permute-done.1.refs_9_
  8.5 0.4 collective-permute-start.6
  8.9 0.0 copy-done.5
  8.9 2.7 %collective-permute-start.5 = (bf16[18,512]{1,0:T(8,128)(2,1)S(1)}, bf16[18,512]{1,0:T(8,128)(2,1)S(1)}, u32[]{:S(2)}, u32[]{:S(2)}) collective-permute-start(bf16[18,512]{1,0:T(8,128)(2,1)S(1)} %pad_maximum_fusion), channel_id=1, source_target_pairs={{0,2},{2,0},{1,3},{3,1},{4,6},{6,4},{5,7},{7,5},{8,10},{10,8},{9,1... | collective-permute-start | bytes 55304 | tf_op jit(solution)/shard_map/ppermute | solution.py:658
  11.6 0.0 copy-done.4
  11.6 1.4 %expand_second.1 = (bf16[8,80,1024]{2,1,0:T(8,128)(2,1)S(1)}, bf16[512,1024]{1,0:T(8,128)(2,1)S(1)}, bf16[1024,512]{1,0:T(8,128)(2,1)S(1)}, bf16[3,512,256]{2,1,0:T(8,128)(2,1)S(1)}, bf16[256,512]{1,0:T(8,128)(2,1)S(1)}) custom-call(bf16[8,80,512]{2,1,0:T(8,128)(2,1)S(1)} %get-tuple-element.58.ordered_ref, bf16[512,1024]{1,0:T(8,128)(2,1)S(1)} %copy-done.1, ...), custom_call_target="tpu_custom_call" | custom-call | flops 671088640 | bytes 1310720 | tf_op jit(solution)/shard_map/expand_second/pallas_call | solution.py:272
  13.0 0.4 collective-permute-done.5.refs_10_
  13.4 0.0 collective-permute-start.7
  13.4 0.5 collective-permute-start.8
  13.9 0.0 collective-permute-done.6.refs_7_
  13.9 4.1 %deepen.2 = (bf16[64,512]{1,0:T(8,128)(2,1)S(1)}, bf16[64,512]{1,0:T(8,128)(2,1)S(1)}, bf16[64,512]{1,0:T(8,128)(2,1)S(1)}, bf16[64,512]{1,0:T(8,128)(2,1)S(1)},...) custom-call(s32[7]{0:T(128)S(1)} %stack.47.flag_ref.refs_0_, ...), custom_call_target="tpu_custom_call" | custom-call | flops 536870912 | bytes 2621440 | tf_op jit(solution)/shard_map/deepen/pallas_call | solution.py:410
  18.0 0.0 collective-permute-done.8.wo_sib_ref
  18.0 0.0 collective-permute-done.7.wqkv_sib_ref
  18.0 5.1 %collective-permute-start.9 = (bf16[64,512]{1,0:T(8,128)(2,1)S(1)}, bf16[64,512]{1,0:T(8,128)(2,1)S(1)}, u32[]{:S(2)}, u32[]{:S(2)}) collective-permute-start(bf16[64,512]{1,0:T(8,128)(2,1)S(1)} %get-tuple-element.77.refs_10_), channel_id=1, source_target_pairs={{0,8},{2,10},{4,12},{6,14},{8,0},{10,2},{12,4},{14,6},{1,9},{3,11}... | collective-permute-start | bytes 196616 | tf_op jit(solution)/shard_map/ppermute | solution.py:666
  23.1 1.0 %collective-permute-start.10 = (bf16[64,512]{1,0:T(8,128)(2,1)S(1)}, bf16[64,512]{1,0:T(8,128)(2,1)S(1)}, u32[]{:S(2)}, u32[]{:S(2)}) collective-permute-start(bf16[64,512]{1,0:T(8,128)(2,1)S(1)} %get-tuple-element.78.refs_11_), channel_id=1, source_target_pairs={{0,10},{2,8},{4,14},{6,12},{8,2},{10,0},{12,6},{14,4},{1,11},{3,9}... | collective-permute-start | bytes 196616 | tf_op jit(solution)/shard_map/ppermute | solution.py:666
  24.1 1.9 %collective-permute-start.11 = (bf16[64,512]{1,0:T(8,128)(2,1)S(1)}, bf16[64,512]{1,0:T(8,128)(2,1)S(1)}, u32[]{:S(2)}, u32[]{:S(2)}) collective-permute-start(bf16[64,512]{1,0:T(8,128)(2,1)S(1)} %get-tuple-element.79.refs_12_), channel_id=1, source_target_pairs={{0,12},{2,14},{4,8},{6,10},{8,4},{10,6},{12,0},{14,2},{1,13},{3,15... | collective-permute-start | bytes 196616 | tf_op jit(solution)/shard_map/ppermute | solution.py:666
  26.1 1.9 %collective-permute-start.12 = (bf16[64,512]{1,0:T(8,128)(2,1)S(1)}, bf16[64,512]{1,0:T(8,128)(2,1)S(1)}, u32[]{:S(2)}, u32[]{:S(2)}) collective-permute-start(bf16[64,512]{1,0:T(8,128)(2,1)S(1)} %get-tuple-element.80.refs_13_), channel_id=1, source_target_pairs={{0,14},{2,12},{4,10},{6,8},{8,6},{10,4},{12,2},{14,0},{1,15},{3,13... | collective-permute-start | bytes 196616 | tf_op jit(solution)/shard_map/ppermute | solution.py:666
  27.9 3.0 %deepen.3 = (bf16[64,512]{1,0:T(8,128)(2,1)S(1)}, bf16[64,512]{1,0:T(8,128)(2,1)S(1)}, bf16[64,512]{1,0:T(8,128)(2,1)S(1)}, bf16[64,512]{1,0:T(8,128)(2,1)S(1)}) custom-call(s32[7]{0:T(128)S(1)} %stack.47.flag_ref.refs_0_, bf16[8,80,1024]{2,1,0:T(8,128)(2,1)S(1)} %get-tuple-element.62.refs_1_, bf16[8,80,1024]{2,1,0:T(8,128)(2,1)S(1)} %get-tuple-element.63.refs_2_, ...), custom_call_target="tpu_custom_call" | custom-call | flops 536870912 | bytes 2621440 | tf_op jit(solution)/shard_map/deepen/pallas_call | solution.py:410
  31.0 0.0 collective-permute-done.9.refs_0_.rest_0_
  31.0 0.8 %collective-permute-start.13 = (bf16[64,512]{1,0:T(8,128)(2,1)S(1)}, bf16[64,512]{1,0:T(8,128)(2,1)S(1)}, u32[]{:S(2)}, u32[]{:S(2)}) collective-permute-start(bf16[64,512]{1,0:T(8,128)(2,1)S(1)} %get-tuple-element.87), channel_id=1, source_target_pairs={{0,6},{2,4},{4,2},{6,0},{8,14},{10,12},{12,10},{14,8},{1,7},{3,5},... | collective-permute-start | bytes 196616 | tf_op jit(solution)/shard_map/ppermute | solution.py:666
  31.7 2.2 %collective-permute-start.14 = (bf16[64,512]{1,0:T(8,128)(2,1)S(1)}, bf16[64,512]{1,0:T(8,128)(2,1)S(1)}, u32[]{:S(2)}, u32[]{:S(2)}) collective-permute-start(bf16[64,512]{1,0:T(8,128)(2,1)S(1)} %get-tuple-element.88), channel_id=1, source_target_pairs={{0,4},{2,6},{4,0},{6,2},{8,12},{10,14},{12,8},{14,10},{1,5},{3,7},... | collective-permute-start | bytes 196616 | tf_op jit(solution)/shard_map/ppermute | solution.py:666
  34.0 0.0 collective-permute-done.10.refs_1_.rest_1_
  34.0 0.5 collective-permute-start.15
  34.5 0.0 collective-permute-done.11.refs_2_.rest_2_
  34.5 0.0 collective-permute-done.12.refs_3_.rest_3_
  34.5 0.8 %project_early.1.early_ref = bf16[3,8,32,512]{3,2,1,0:T(8,128)(2,1)S(1)} custom-call(bf16[3,512,256]{2,1,0:T(8,128)(2,1)S(1)} %get-tuple-element.61.wqkv_ref, bf16[3,512,256]{2,1,0:T(8,128)(2,1)S(1)} %collective-permute-done.7.wqkv_sib_ref, f32[16,1024]{1,0:T(8,128)S(1)} %copy-done, bf16[64,512]{1,0:T(8,128)(2,1)S(1)} %collective-permute-done.9.refs_0_.rest_0_, ...), custom_call_target="tpu_custom_call" | custom-call | flops 402653184 | tf_op jit(solution)/shard_map/project_early/pallas_call | solution.py:462
  35.3 1.0 %collective-permute-done.13.rest_4_ = bf16[64,512]{1,0:T(8,128)(2,1)S(1)} collective-permute-done((bf16[64,512]{1,0:T(8,128)(2,1)S(1)}, bf16[64,512]{1,0:T(8,128)(2,1)S(1)}, u32[]{:S(2)}, u32[]{:S(2)}) %collective-permute-start.13) | collective-permute-done | bytes 65568 | tf_op jit(solution)/shard_map/ppermute | solution.py:666
  36.3 0.6 %collective-permute-done.14.rest_5_ = bf16[64,512]{1,0:T(8,128)(2,1)S(1)} collective-permute-done((bf16[64,512]{1,0:T(8,128)(2,1)S(1)}, bf16[64,512]{1,0:T(8,128)(2,1)S(1)}, u32[]{:S(2)}, u32[]{:S(2)}) %collective-permute-start.14) | collective-permute-done | bytes 65568 | tf_op jit(solution)/shard_map/ppermute | solution.py:666
  36.9 1.3 %collective-permute-done.15.rest_6_ = bf16[64,512]{1,0:T(8,128)(2,1)S(1)} collective-permute-done((bf16[64,512]{1,0:T(8,128)(2,1)S(1)}, bf16[64,512]{1,0:T(8,128)(2,1)S(1)}, u32[]{:S(2)}, u32[]{:S(2)}) %collective-permute-start.15) | collective-permute-done | bytes 65568 | tf_op jit(solution)/shard_map/ppermute | solution.py:666
  38.3 3.1 %attend.1 = bf16[8,2,64,256]{3,2,1,0:T(8,128)(2,1)S(1)} custom-call(s32[7]{0:T(128)S(1)} %stack.47.flag_ref.refs_0_, bf16[3,8,32,512]{3,2,1,0:T(8,128)(2,1)S(1)} %project_early.1.early_ref, bf16[3,512,256]{2,1,0:T(8,128)(2,1)S(1)} %get-tuple-element.61.wqkv_ref, bf16[3,512,256]{2,1,0:T(8,128)(2,1)S(1)} %collective-permute-done.7.wqkv_sib_ref, ...), custom_call_target="tpu_custom_call" | custom-call | flops 1073741824 | bytes 1048576 | tf_op jit(solution)/shard_map/attend/pallas_call | solution.py:542
  41.4 17.6 %all_to_all.5.arrived_ref = bf16[16,64,256]{2,1,0:T(8,128)(2,1)S(1)} all-to-all(bf16[16,64,256]{2,1,0:T(8,128)(2,1)S(1)} %bitcast.18), channel_id=1, replica_groups=mesh['grp'=2,'gy'=4,'gx'=2,'ch'=2] {'gy','gx','ch'}, dimensions={0} | all-to-all | bytes 1048576 | tf_op jit(solution)/shard_map/all_to_all | solution.py:722
  59.0 1.1 %lay_out.1 = bf16[2,8,64,256]{3,2,1,0:T(8,128)(2,1)} custom-call(bf16[16,64,256]{2,1,0:T(8,128)(2,1)S(1)} %all_to_all.5.arrived_ref), custom_call_target="tpu_custom_call" | custom-call | tf_op jit(solution)/shard_map/lay_out/pallas_call | solution.py:634
  (8 shorter events, 0.0 us)
Async XLA Ops:
  1.9 4.6 %collective-permute-start.3 = (bf16[512,1024]{1,0:T(8,128)(2,1)}, bf16[512,1024]{1,0:T(8,128)(2,1)S(1)}, u32[]{:S(2)}, u32[]{:S(2)}) collective-permute-start(bf16[512,1024]{1,0:T(8,128)(2,1)} %w_ref), channel_id=1, source_target_pairs={{0,1},{1,0},{2,3},{3,2},{4,5},{5,4},{6,7},{7,6},{8,9},{9,8},{10,11... | collective-permute-start | bytes 3145736 | tf_op jit(solution)/shard_map/ppermute | solution.py:688
  2.4 4.1 %collective-permute-start.2 = (bf16[16,64,512]{2,1,0:T(8,128)(2,1)}, bf16[16,64,512]{2,1,0:T(8,128)(2,1)S(1)}, u32[]{:S(2)}, u32[]{:S(2)}) collective-permute-start(bf16[16,64,512]{2,1,0:T(8,128)(2,1)} %cells_hbm.1), channel_id=1, source_target_pairs={{0,1},{1,0},{2,3},{3,2},{4,5},{5,4},{6,7},{7,6},{8,9},{9,8},{10,11... | collective-permute-start | bytes 3145736 | tf_op jit(solution)/shard_map/ppermute | solution.py:688
  2.5 4.0 %collective-permute-start.4 = (f32[16,1024]{1,0:T(8,128)}, f32[16,1024]{1,0:T(8,128)S(1)}, u32[]{:S(2)}, u32[]{:S(2)}) collective-permute-start(f32[16,1024]{1,0:T(8,128)} %get-tuple-element.52.small_ref.refs_4_), channel_id=1, source_target_pairs={{0,1},{1,0},{2,3},{3,2},{4,5},{5,4},{6,7},{7,6},{8,9},{9,8},{10,11... | collective-permute-start | bytes 196616 | tf_op jit(solution)/shard_map/ppermute | solution.py:688
  2.9 5.5 %collective-permute-start = (bf16[64,512]{1,0:T(8,128)(2,1)}, bf16[64,512]{1,0:T(8,128)(2,1)S(1)}, u32[]{:S(2)}, u32[]{:S(2)}) collective-permute-start(bf16[64,512]{1,0:T(8,128)(2,1)} %get-tuple-element.49), channel_id=1, source_target_pairs={{0,4},{8,12},{4,0},{12,8},{1,5},{9,13},{5,1},{13,9},{2,6},{10,14},... | collective-permute-start | bytes 196616 | tf_op jit(solution)/shard_map/ppermute | solution.py:650
  5.6 2.9 %collective-permute-start.1 = (bf16[64,512]{1,0:T(8,128)(2,1)}, bf16[64,512]{1,0:T(8,128)(2,1)S(1)}, u32[]{:S(2)}, u32[]{:S(2)}) collective-permute-start(bf16[64,512]{1,0:T(8,128)(2,1)} %get-tuple-element.50), channel_id=1, source_target_pairs={{4,8},{8,4},{5,9},{9,5},{6,10},{10,6},{7,11},{11,7},{20,24},{24,20... | collective-permute-start | bytes 196616 | tf_op jit(solution)/shard_map/ppermute | solution.py:650
  6.5 2.0 %copy-start.2 = (bf16[1024,512]{1,0:T(8,128)(2,1)S(1)}, bf16[1024,512]{1,0:T(8,128)(2,1)}, u32[]{:S(2)}) copy-start(bf16[1024,512]{1,0:T(8,128)(2,1)} %refs_0_) | copy-start | bytes 3145732
  6.5 2.4 %copy-start.5 = (bf16[16,512]{1,0:T(8,128)(2,1)S(1)}, bf16[16,512]{1,0:T(8,128)(2,1)}, u32[]{:S(2)}) copy-start(bf16[16,512]{1,0:T(8,128)(2,1)} %get-tuple-element.57) | copy-start | bytes 49156
  6.5 5.1 %copy-start = (f32[16,1024]{1,0:T(8,128)S(1)}, f32[16,1024]{1,0:T(8,128)}, u32[]{:S(2)}) copy-start(f32[16,1024]{1,0:T(8,128)} %get-tuple-element.52.small_ref.refs_4_) | copy-start | bytes 196612
  6.5 5.1 %copy-start.1 = (bf16[512,1024]{1,0:T(8,128)(2,1)S(1)}, bf16[512,1024]{1,0:T(8,128)(2,1)}, u32[]{:S(2)}) copy-start(bf16[512,1024]{1,0:T(8,128)(2,1)} %w_ref) | copy-start | bytes 3145732
  6.5 5.1 %copy-start.3 = (bf16[512,3,256]{2,0,1:T(8,128)(2,1)S(1)}, bf16[512,3,256]{2,0,1:T(8,128)(2,1)}, u32[]{:S(2)}) copy-start(bf16[512,3,256]{2,0,1:T(8,128)(2,1)} %param.19) | copy-start | bytes 2359300
  6.5 5.1 %copy-start.4 = (bf16[256,512]{1,0:T(8,128)(2,1)S(1)}, bf16[256,512]{1,0:T(8,128)(2,1)}, u32[]{:S(2)}) copy-start(bf16[256,512]{1,0:T(8,128)(2,1)} %refs_2_.1) | copy-start | bytes 786436
  8.5 5.5 %collective-permute-start.6 = (bf16[1024,512]{1,0:T(8,128)(2,1)S(1)}, bf16[1024,512]{1,0:T(8,128)(2,1)S(1)}, u32[]{:S(2)}, u32[]{:S(2)}) collective-permute-start(bf16[1024,512]{1,0:T(8,128)(2,1)S(1)} %copy-done.2), channel_id=1, source_target_pairs={{0,1},{1,0},{2,3},{3,2},{4,5},{5,4},{6,7},{7,6},{8,9},{9,8},{10,11... | collective-permute-start | bytes 3145736 | tf_op jit(solution)/shard_map/ppermute | solution.py:688
  8.9 4.5 %collective-permute-start.5 = (bf16[18,512]{1,0:T(8,128)(2,1)S(1)}, bf16[18,512]{1,0:T(8,128)(2,1)S(1)}, u32[]{:S(2)}, u32[]{:S(2)}) collective-permute-start(bf16[18,512]{1,0:T(8,128)(2,1)S(1)} %pad_maximum_fusion), channel_id=1, source_target_pairs={{0,2},{2,0},{1,3},{3,1},{4,6},{6,4},{5,7},{7,5},{8,10},{10,8},{9,1... | collective-permute-start | bytes 55304 | tf_op jit(solution)/shard_map/ppermute | solution.py:658
  13.4 4.6 %collective-permute-start.7 = (bf16[3,512,256]{2,1,0:T(8,128)(2,1)S(1)}, bf16[3,512,256]{2,1,0:T(8,128)(2,1)S(1)}, u32[]{:S(2)}, u32[]{:S(2)}) collective-permute-start(bf16[3,512,256]{2,1,0:T(8,128)(2,1)S(1)} %get-tuple-element.61.wqkv_ref), channel_id=1, source_target_pairs={{0,1},{1,0},{2,3},{3,2},{4,5},{5,4},{6,7},{7,6},{8,9},{9,8},{10,11... | collective-permute-start | bytes 2359304 | tf_op jit(solution)/shard_map/ppermute | solution.py:688
  13.4 4.6 %collective-permute-start.8 = (bf16[256,512]{1,0:T(8,128)(2,1)S(1)}, bf16[256,512]{1,0:T(8,128)(2,1)S(1)}, u32[]{:S(2)}, u32[]{:S(2)}) collective-permute-start(bf16[256,512]{1,0:T(8,128)(2,1)S(1)} %get-tuple-element.73.wo_ref), channel_id=1, source_target_pairs={{0,1},{1,0},{2,3},{3,2},{4,5},{5,4},{6,7},{7,6},{8,9},{9,8},{10,11... | collective-permute-start | bytes 786440 | tf_op jit(solution)/shard_map/ppermute | solution.py:688
  18.0 12.9 %collective-permute-start.9 = (bf16[64,512]{1,0:T(8,128)(2,1)S(1)}, bf16[64,512]{1,0:T(8,128)(2,1)S(1)}, u32[]{:S(2)}, u32[]{:S(2)}) collective-permute-start(bf16[64,512]{1,0:T(8,128)(2,1)S(1)} %get-tuple-element.77.refs_10_), channel_id=1, source_target_pairs={{0,8},{2,10},{4,12},{6,14},{8,0},{10,2},{12,4},{14,6},{1,9},{3,11}... | collective-permute-start | bytes 196616 | tf_op jit(solution)/shard_map/ppermute | solution.py:666
  23.1 10.8 %collective-permute-start.10 = (bf16[64,512]{1,0:T(8,128)(2,1)S(1)}, bf16[64,512]{1,0:T(8,128)(2,1)S(1)}, u32[]{:S(2)}, u32[]{:S(2)}) collective-permute-start(bf16[64,512]{1,0:T(8,128)(2,1)S(1)} %get-tuple-element.78.refs_11_), channel_id=1, source_target_pairs={{0,10},{2,8},{4,14},{6,12},{8,2},{10,0},{12,6},{14,4},{1,11},{3,9}... | collective-permute-start | bytes 196616 | tf_op jit(solution)/shard_map/ppermute | solution.py:666
  24.1 10.4 %collective-permute-start.11 = (bf16[64,512]{1,0:T(8,128)(2,1)S(1)}, bf16[64,512]{1,0:T(8,128)(2,1)S(1)}, u32[]{:S(2)}, u32[]{:S(2)}) collective-permute-start(bf16[64,512]{1,0:T(8,128)(2,1)S(1)} %get-tuple-element.79.refs_12_), channel_id=1, source_target_pairs={{0,12},{2,14},{4,8},{6,10},{8,4},{10,6},{12,0},{14,2},{1,13},{3,15... | collective-permute-start | bytes 196616 | tf_op jit(solution)/shard_map/ppermute | solution.py:666
  26.1 8.4 %collective-permute-start.12 = (bf16[64,512]{1,0:T(8,128)(2,1)S(1)}, bf16[64,512]{1,0:T(8,128)(2,1)S(1)}, u32[]{:S(2)}, u32[]{:S(2)}) collective-permute-start(bf16[64,512]{1,0:T(8,128)(2,1)S(1)} %get-tuple-element.80.refs_13_), channel_id=1, source_target_pairs={{0,14},{2,12},{4,10},{6,8},{8,6},{10,4},{12,2},{14,0},{1,15},{3,13... | collective-permute-start | bytes 196616 | tf_op jit(solution)/shard_map/ppermute | solution.py:666
  31.0 5.3 %collective-permute-start.13 = (bf16[64,512]{1,0:T(8,128)(2,1)S(1)}, bf16[64,512]{1,0:T(8,128)(2,1)S(1)}, u32[]{:S(2)}, u32[]{:S(2)}) collective-permute-start(bf16[64,512]{1,0:T(8,128)(2,1)S(1)} %get-tuple-element.87), channel_id=1, source_target_pairs={{0,6},{2,4},{4,2},{6,0},{8,14},{10,12},{12,10},{14,8},{1,7},{3,5},... | collective-permute-start | bytes 196616 | tf_op jit(solution)/shard_map/ppermute | solution.py:666
  31.7 5.2 %collective-permute-start.14 = (bf16[64,512]{1,0:T(8,128)(2,1)S(1)}, bf16[64,512]{1,0:T(8,128)(2,1)S(1)}, u32[]{:S(2)}, u32[]{:S(2)}) collective-permute-start(bf16[64,512]{1,0:T(8,128)(2,1)S(1)} %get-tuple-element.88), channel_id=1, source_target_pairs={{0,4},{2,6},{4,0},{6,2},{8,12},{10,14},{12,8},{14,10},{1,5},{3,7},... | collective-permute-start | bytes 196616 | tf_op jit(solution)/shard_map/ppermute | solution.py:666
  34.0 4.3 %collective-permute-start.15 = (bf16[64,512]{1,0:T(8,128)(2,1)S(1)}, bf16[64,512]{1,0:T(8,128)(2,1)S(1)}, u32[]{:S(2)}, u32[]{:S(2)}) collective-permute-start(bf16[64,512]{1,0:T(8,128)(2,1)S(1)} %get-tuple-element.89), channel_id=1, source_target_pairs={{0,2},{2,0},{4,6},{6,4},{8,10},{10,8},{12,14},{14,12},{1,3},{3,1},... | collective-permute-start | bytes 196616 | tf_op jit(solution)/shard_map/ppermute | solution.py:666

commit v5 on v4

--- a/solution.py
+++ b/solution.py
@@ -224,7 +224,13 @@
             )
 
 
-def expand_first_kernel(plan, flag_ref, cells_ref, w_ref, small_ref, e_ref, x_ref, ordered_ref):
+def expand_first_kernel(plan, flag_ref, cells_ref, w_ref, small_ref, e_ref, x_ref, ordered_ref, column_ref):
+    column, group, rows = flag_ref[7], 2 * SUBLANES, column_ref.shape[0]
+    start = pl.multiple_of(column // group * group, group)
+    shape = (rows, rows * group)
+    pick = one_hot(lax.broadcasted_iota(jnp.int32, shape, 0) * group + (column - start))
+    near = cells_ref[:, :, pl.ds(start, group)].reshape(rows * group, plan.width)
+    column_ref[...] = jnp.dot(pick, near, preferred_element_type=jnp.float32).astype(jnp.bfloat16)
     order = plan.order(flag_ref[0])
     for a in range(plan.depth_h):
         block = cells_ref[:, a].reshape(-1, plan.width)
@@ -240,11 +246,12 @@
     return pl.pallas_call(
         functools.partial(expand_first_kernel, plan),
         in_specs=[pl.BlockSpec(memory_space=pltpu.SMEM)] + in_vmem(3),
-        out_specs=in_vmem(3),
+        out_specs=in_vmem(4),
         out_shape=[
             jax.ShapeDtypeStruct((plan.depth_h, rows, weight.shape[1]), jnp.bfloat16),
             jax.ShapeDtypeStruct((plan.depth_h, plan.span_w * SUBLANES, plan.width), jnp.bfloat16),
             jax.ShapeDtypeStruct((plan.depth_h, rows, plan.width), jnp.bfloat16),
+            jax.ShapeDtypeStruct((cells.shape[0], plan.width), jnp.bfloat16),
         ],
         compiler_params=pltpu.CompilerParams(vmem_limit_bytes=VMEM_BYTES),
         cost_estimate=pl.CostEstimate(
@@ -528,7 +535,7 @@
     result = values[...] + (summed + bias).reshape(values.shape)
     for source, (dy, dx) in enumerate(targets):
         part = result[:, source].reshape(tokens, width).astype(jnp.bfloat16)
-        target = (flag_ref[5] ^ dy) * plan.n_cols + (flag_ref[6] ^ dx)
+        target = (flag_ref[6] ^ dx) * plan.n_rows + (flag_ref[5] ^ dy)
         for core in range(plan.n_ch):
             out_ref[target, core] = part[:, core * half : (core + 1) * half]
 
@@ -557,57 +564,47 @@
     )(flags, *operands)
 
 
-def edges_kernel(group, column_ref, row_ref, cells_hbm, taps_hbm, *refs):
-    count = (len(refs) - 6) // 2
-    vectors_hbm, (one_ref, other_ref, side_ref, small_ref, held, taps), (*vectors, sems) = (
-        refs[:count], refs[count : count + 6], refs[count + 6 :]
-    )
-    rows, width = cells_hbm.shape[0], cells_hbm.shape[2]
-    column, one = column_ref[0], row_ref[0]
-    start = pl.multiple_of(column // group * group, group)
+def edges_kernel(row_ref, cells_hbm, taps_hbm, *refs):
+    count = (len(refs) - 4) // 2
+    vectors_hbm, (one_ref, other_ref, small_ref, taps), (*vectors, sems) = (
+        refs[:count], refs[count : count + 4], refs[count + 4 :]
+    )
+    rows, one = cells_hbm.shape[0], row_ref[0]
     pairs = [
         (cells_hbm.at[one], one_ref),
         (cells_hbm.at[rows - 1 - one], other_ref),
-        (cells_hbm.at[:, pl.ds(start, group)], held),
         (taps_hbm, taps),
         *zip(vectors_hbm, vectors),
     ]
     copies = [pltpu.make_async_copy(*pair, sems.at[i]) for i, pair in enumerate(pairs)]
     for copy in copies:
         copy.start()
-    shape = (rows, rows * group)
-    pick = one_hot(lax.broadcasted_iota(jnp.int32, shape, 0) * group + (column - start))
     small_ref[...] = jnp.zeros_like(small_ref)
     for copy in copies:
         copy.wait()
-    side_ref[...] = jnp.dot(
-        pick, held[...].reshape(rows * group, width), preferred_element_type=jnp.float32
-    ).astype(jnp.bfloat16)
     for i in range(3):
         small_ref[3 * i : 3 * i + 3] = taps[i].astype(jnp.float32)
     for i, vector in enumerate(vectors):
         small_ref[9 + i : 10 + i, : vector.shape[1]] = vector[...]
 
 
-def edges(cells, column, row, w_depth, vectors):
-    rows, cols, width = cells.shape
-    group = 2 * SUBLANES
+def edges(cells, row, w_depth, vectors):
+    cols, width = cells.shape[1:]
     operands = (cells, w_depth, *vectors)
     return pl.pallas_call(
-        functools.partial(edges_kernel, group),
-        in_specs=[pl.BlockSpec(memory_space=pltpu.SMEM)] * 2
+        edges_kernel,
+        in_specs=[pl.BlockSpec(memory_space=pltpu.SMEM)]
         + [pl.BlockSpec(memory_space=pltpu.HBM)] * len(operands),
-        out_specs=in_vmem(4),
-        out_shape=[jax.ShapeDtypeStruct((count, width), cells.dtype) for count in (cols, cols, rows)]
-        + [jax.ShapeDtypeStruct((group, w_depth.shape[2]), jnp.float32)],
+        out_specs=in_vmem(3),
+        out_shape=[jax.ShapeDtypeStruct((cols, width), cells.dtype)] * 2
+        + [jax.ShapeDtypeStruct((2 * SUBLANES, w_depth.shape[2]), jnp.float32)],
         scratch_shapes=[
-            pltpu.VMEM((rows, group, width), cells.dtype),
             *(pltpu.VMEM(v.shape, v.dtype) for v in operands[1:]),
-            pltpu.SemaphoreType.DMA((len(operands) + 2,)),
+            pltpu.SemaphoreType.DMA((len(operands) + 1,)),
         ],
         compiler_params=pltpu.CompilerParams(vmem_limit_bytes=EDGES_VMEM_BYTES),
         name="edges",
-    )(column[None], row[None], *operands)
+    )(row[None], *operands)
 
 
 def lay_out_kernel(plan, arrived_ref, out_ref):
@@ -622,7 +619,13 @@
     )
     for block in range(plan.n_rows):
         for k in range(each):
-            source = arrived_ref[block * peers : (block + 1) * peers, k * tokens : (k + 1) * tokens]
+            source = jnp.concatenate(
+                [
+                    arrived_ref[low : low + plan.n_ch, k * tokens : (k + 1) * tokens]
+                    for low in range(block * plan.n_ch, arrived_ref.shape[0], plan.n_rows * plan.n_ch)
+                ],
+                axis=0,
+            )
             placed = jnp.dot(
                 order, source.reshape(peers * tokens, -1), preferred_element_type=jnp.float32
             ).astype(jnp.bfloat16)
@@ -672,15 +675,13 @@
     n_rows, n_cols, n_ch = plan.n_rows, plan.n_cols, plan.n_ch
     width = plan.width
     own_y, own_x, own_c = (lax.axis_index(axis) for axis in ("gy", "gx", "ch"))
+    index = jnp.where(own_x == 0, cells.shape[1] - 1, 0)
     flags = jnp.stack(
-        [own_c, own_y > 0, own_y < n_rows - 1, own_x > 0, own_x < n_cols - 1, own_y, own_x]
+        [own_c, own_y > 0, own_y < n_rows - 1, own_x > 0, own_x < n_cols - 1, own_y, own_x, index]
     ).astype(jnp.int32)
-    index = jnp.where(own_x == 0, cells.shape[1] - 1, 0)
     vectors = tuple(v[None] for v in (b_expand, b_depth, b_out, b_project, ln_gain))
     even = own_y % 2 == 0
-    one, other, column, small = edges(
-        cells, index, jnp.where(even, cells.shape[0] - 1, 0), w_depth, vectors
-    )
+    one, other, small = edges(cells, jnp.where(even, cells.shape[0] - 1, 0), w_depth, vectors)
     one, w_expand, w_project = lax.optimization_barrier((one, w_expand, w_project))
     rows = swap_rows(one, other)
 
@@ -688,11 +689,11 @@
         return value, lax.ppermute(value, "ch", [(0, 1), (1, 0)])
 
     w_expand, small = both(w_expand), both(small)
-    e_sib, x, ordered = expand_first(plan, flags, both(cells)[1], w_expand[1], small[1])
+    e_sib, x, ordered, column = expand_first(plan, flags, both(cells)[1], w_expand[1], small[1])
     e_own, *kept = expand_second(
         plan, ordered, w_expand[0], small[0], (w_project, w_qkv.transpose(1, 0, 2), w_out)
     )
-    *rows, x, w_project = lax.optimization_barrier((*rows, x, w_project))
+    *rows, x, w_project, column = lax.optimization_barrier((*rows, x, w_project, column))
     w_project = both(w_project)
     e = e_own, e_sib
     cols = halo_column(column, rows, index, even)
@@ -719,7 +720,7 @@
     early = project_early(arrived[: len(far)], w_qkv, small[0])
     leaving = attend_windows(plan, far + near, flags, early, arrived, (*w_qkv, *w_out, *small))
     leaving = leaving.reshape((n_rows * n_cols * n_ch,) + leaving.shape[2:])
-    returned = lax.all_to_all(leaving, ("gy", "gx", "ch"), 0, 0, tiled=True)
+    returned = lax.all_to_all(leaving, ("gx", "gy", "ch"), 0, 0, tiled=True)
     return lay_out(plan, returned).reshape(cells.shape[0], cells.shape[1], -1)
 
 

time: 60.3 us -> 59.9 us (level)
  transfers between devices with their start and end apart: 16 -> 16, of which waited for: 6 -> 5; matrix products, arithmetic and copies ran while one was open for 0% -> 0% of each run, Pallas kernels for 18% -> 19%
where the time goes in v5:
time: 59.9 us; the launch traced here: 59.7 us
  starting transfers between devices  21.4 us (36%)
  blocking collectives  17.4 us (29%)
  Pallas kernels  16.9 us (28%)
  waiting for transfers between devices  3.58 us (6%)
    all_to_all x1, blocking collectives, fast_device(): returned = lax.all_to_all(leaving, ('gx', 'gy', 'ch'), 0, 0, tiled=True)  17.4 us
    ppermute x7, starting transfers between devices, send_to(): return lax.ppermute(value, ('gy', 'gx'), pairs)  13.4 us
    pallas_call x2, Pallas kernels, deepen(): pl.pallas_call(functools.partial(deepen_kernel, plan, targets, first), in...  7.08 us
    ppermute x2, starting transfers between devices, swap_rows(): lax.ppermute(value, 'gy', pairs + [(target, source) for source, target in...  3.3 us
    pallas_call x1, Pallas kernels, attend_windows(): pl.pallas_call(functools.partial(attend_kernel, plan, targets), in_specs=...  3.12 us
    ppermute x7, waiting for transfers between devices, send_to(): return lax.ppermute(value, ('gy', 'gx'), pairs)  2.97 us
    ppermute x1, starting transfers between devices, halo_column(): return lax.ppermute(jnp.concatenate(parts, axis=0), 'gx', [(0, 1), (1, 0)])  2.7 us
    ppermute x6, starting transfers between devices, both(): return (value, lax.ppermute(value, 'ch', [(0, 1), (1, 0)]))  1.98 us
  transfers between devices with their start and end apart: 16, of which 5 were waited for; matrix products, arithmetic and copies ran while one was open for 0% of the time, Pallas kernels for 19%

profile of v5, /device:TPU:0, one launch (start us, length us, event | category | flops | bytes accessed | tf_op | source)
XLA Modules:
  0.0 59.7 jit_solution(13572712761016560603)
XLA Ops:
  0.0 1.6 %edges.1 = (bf16[64,512]{1,0:T(8,128)(2,1)}, bf16[64,512]{1,0:T(8,128)(2,1)}, f32[16,1024]{1,0:T(8,128)}) custom-call(s32[1]{0:T(128)} %bitcast.8.row_ref, bf16[16,64,512]{2,1,0:T(8,128)(2,1)} %cells_hbm.1, bf16[3,3,1024]{2,1,0:T(4,128)(2,1)} %taps_hbm.1, f32[1,1024]{1,0:T(1,128)} %bitcast.21, f32[1,1024]{1,0:T(1,128)} %bitcast.22, f32[1,256]{1,0:T(1,128)} %bitcast.25, ...), custom_call_target="tpu_custom_call" | custom-call | tf_op jit(solution)/shard_map/edges/pallas_call | solution.py:594
  1.6 0.5 collective-permute-start.3
  2.1 0.1 collective-permute-start.2
  2.2 0.4 collective-permute-start.4
  2.7 2.7 %collective-permute-start = (bf16[64,512]{1,0:T(8,128)(2,1)}, bf16[64,512]{1,0:T(8,128)(2,1)S(1)}, u32[]{:S(2)}, u32[]{:S(2)}) collective-permute-start(bf16[64,512]{1,0:T(8,128)(2,1)} %get-tuple-element.50), channel_id=1, source_target_pairs={{0,4},{8,12},{4,0},{12,8},{1,5},{9,13},{5,1},{13,9},{2,6},{10,14},... | collective-permute-start | bytes 196616 | tf_op jit(solution)/shard_map/ppermute | solution.py:653
  5.3 0.7 %collective-permute-start.1 = (bf16[64,512]{1,0:T(8,128)(2,1)}, bf16[64,512]{1,0:T(8,128)(2,1)S(1)}, u32[]{:S(2)}, u32[]{:S(2)}) collective-permute-start(bf16[64,512]{1,0:T(8,128)(2,1)} %get-tuple-element.51), channel_id=1, source_target_pairs={{4,8},{8,4},{5,9},{9,5},{6,10},{10,6},{7,11},{11,7},{20,24},{24,20... | collective-permute-start | bytes 196616 | tf_op jit(solution)/shard_map/ppermute | solution.py:653
  6.0 0.1 stack.51.flag_ref.refs_0_
  6.1 0.2 collective-permute-done.4.small_ref.refs_5_.small_sib_ref
  6.2 0.0 collective-permute-done.3.w_ref.refs_12_
  6.2 0.0 collective-permute-done.2
  6.3 0.0 copy-start.1
  6.3 0.0 copy-start.3
  6.3 0.0 copy-start.4
  6.3 1.9 %expand_first.1 = (bf16[8,80,1024]{2,1,0:T(8,128)(2,1)S(1)}, bf16[8,64,512]{2,1,0:T(8,128)(2,1)S(1)}, bf16[8,80,512]{2,1,0:T(8,128)(2,1)S(1)}, bf16[16,512]{1,0:T(8,128)(2,1)S(1)}) custom-call(s32[8]{0:T(128)S(1)} %stack.51.flag_ref.refs_0_, bf16[2,8,64,512]{3,2,1,0:T(8,128)(2,1)S(1)} %bitcast.20, ...), custom_call_target="tpu_custom_call" | custom-call | flops 4294967296 | bytes 4194304 | tf_op jit(solution)/shard_map/expand_first/pallas_call | solution.py:246
  8.2 0.0 collective-permute-done.refs_8_
  8.2 0.0 collective-permute-done.1.refs_9_
  8.2 0.0 copy-done.2
  8.2 0.4 collective-permute-start.6
  8.7 2.7 %collective-permute-start.5 = (bf16[18,512]{1,0:T(8,128)(2,1)S(1)}, bf16[18,512]{1,0:T(8,128)(2,1)S(1)}, u32[]{:S(2)}, u32[]{:S(2)}) collective-permute-start(bf16[18,512]{1,0:T(8,128)(2,1)S(1)} %pad_maximum_fusion), channel_id=1, source_target_pairs={{0,2},{2,0},{1,3},{3,1},{4,6},{6,4},{5,7},{7,5},{8,10},{10,8},{9,1... | collective-permute-start | bytes 55304 | tf_op jit(solution)/shard_map/ppermute | solution.py:661
  11.4 0.0 copy-done
  11.4 0.0 copy-done.3
  11.4 1.4 %expand_second.1 = (bf16[8,80,1024]{2,1,0:T(8,128)(2,1)S(1)}, bf16[512,1024]{1,0:T(8,128)(2,1)S(1)}, bf16[1024,512]{1,0:T(8,128)(2,1)S(1)}, bf16[3,512,256]{2,1,0:T(8,128)(2,1)S(1)}, bf16[256,512]{1,0:T(8,128)(2,1)S(1)}) custom-call(bf16[8,80,512]{2,1,0:T(8,128)(2,1)S(1)} %get-tuple-element.60.ordered_ref, bf16[512,1024]{1,0:T(8,128)(2,1)S(1)} %copy-done.1, ...), custom_call_target="tpu_custom_call" | custom-call | flops 671088640 | bytes 1310720 | tf_op jit(solution)/shard_map/expand_second/pallas_call | solution.py:279
  12.8 0.4 collective-permute-done.5.refs_10_
  13.2 0.0 collective-permute-start.7
  13.2 0.5 collective-permute-start.8
  13.7 0.0 collective-permute-done.6.refs_7_
  13.7 4.1 %deepen.2 = (bf16[64,512]{1,0:T(8,128)(2,1)S(1)}, bf16[64,512]{1,0:T(8,128)(2,1)S(1)}, bf16[64,512]{1,0:T(8,128)(2,1)S(1)}, bf16[64,512]{1,0:T(8,128)(2,1)S(1)},...) custom-call(s32[8]{0:T(128)S(1)} %stack.51.flag_ref.refs_0_, ...), custom_call_target="tpu_custom_call" | custom-call | flops 536870912 | bytes 2621440 | tf_op jit(solution)/shard_map/deepen/pallas_call | solution.py:417
  17.8 0.0 collective-permute-done.8.wo_sib_ref
  17.8 0.0 collective-permute-done.7.wqkv_sib_ref
  17.8 5.1 %collective-permute-start.9 = (bf16[64,512]{1,0:T(8,128)(2,1)S(1)}, bf16[64,512]{1,0:T(8,128)(2,1)S(1)}, u32[]{:S(2)}, u32[]{:S(2)}) collective-permute-start(bf16[64,512]{1,0:T(8,128)(2,1)S(1)} %get-tuple-element.79.refs_10_), channel_id=1, source_target_pairs={{0,8},{2,10},{4,12},{6,14},{8,0},{10,2},{12,4},{14,6},{1,9},{3,11}... | collective-permute-start | bytes 196616 | tf_op jit(solution)/shard_map/ppermute | solution.py:669
  22.9 1.0 %collective-permute-start.10 = (bf16[64,512]{1,0:T(8,128)(2,1)S(1)}, bf16[64,512]{1,0:T(8,128)(2,1)S(1)}, u32[]{:S(2)}, u32[]{:S(2)}) collective-permute-start(bf16[64,512]{1,0:T(8,128)(2,1)S(1)} %get-tuple-element.80.refs_11_), channel_id=1, source_target_pairs={{0,10},{2,8},{4,14},{6,12},{8,2},{10,0},{12,6},{14,4},{1,11},{3,9}... | collective-permute-start | bytes 196616 | tf_op jit(solution)/shard_map/ppermute | solution.py:669
  23.9 2.0 %collective-permute-start.11 = (bf16[64,512]{1,0:T(8,128)(2,1)S(1)}, bf16[64,512]{1,0:T(8,128)(2,1)S(1)}, u32[]{:S(2)}, u32[]{:S(2)}) collective-permute-start(bf16[64,512]{1,0:T(8,128)(2,1)S(1)} %get-tuple-element.81.refs_12_), channel_id=1, source_target_pairs={{0,12},{2,14},{4,8},{6,10},{8,4},{10,6},{12,0},{14,2},{1,13},{3,15... | collective-permute-start | bytes 196616 | tf_op jit(solution)/shard_map/ppermute | solution.py:669
  25.9 1.8 %collective-permute-start.12 = (bf16[64,512]{1,0:T(8,128)(2,1)S(1)}, bf16[64,512]{1,0:T(8,128)(2,1)S(1)}, u32[]{:S(2)}, u32[]{:S(2)}) collective-permute-start(bf16[64,512]{1,0:T(8,128)(2,1)S(1)} %get-tuple-element.82.refs_13_), channel_id=1, source_target_pairs={{0,14},{2,12},{4,10},{6,8},{8,6},{10,4},{12,2},{14,0},{1,15},{3,13... | collective-permute-start | bytes 196616 | tf_op jit(solution)/shard_map/ppermute | solution.py:669
  27.7 3.0 %deepen.3 = (bf16[64,512]{1,0:T(8,128)(2,1)S(1)}, bf16[64,512]{1,0:T(8,128)(2,1)S(1)}, bf16[64,512]{1,0:T(8,128)(2,1)S(1)}, bf16[64,512]{1,0:T(8,128)(2,1)S(1)}) custom-call(s32[8]{0:T(128)S(1)} %stack.51.flag_ref.refs_0_, bf16[8,80,1024]{2,1,0:T(8,128)(2,1)S(1)} %get-tuple-element.64.refs_1_, bf16[8,80,1024]{2,1,0:T(8,128)(2,1)S(1)} %get-tuple-element.65.refs_2_, ...), custom_call_target="tpu_custom_call" | custom-call | flops 536870912 | bytes 2621440 | tf_op jit(solution)/shard_map/deepen/pallas_call | solution.py:417
  30.7 0.0 collective-permute-done.9.refs_0_.rest_0_
  30.7 0.8 %collective-permute-start.13 = (bf16[64,512]{1,0:T(8,128)(2,1)S(1)}, bf16[64,512]{1,0:T(8,128)(2,1)S(1)}, u32[]{:S(2)}, u32[]{:S(2)}) collective-permute-start(bf16[64,512]{1,0:T(8,128)(2,1)S(1)} %get-tuple-element.89), channel_id=1, source_target_pairs={{0,6},{2,4},{4,2},{6,0},{8,14},{10,12},{12,10},{14,8},{1,7},{3,5},... | collective-permute-start | bytes 196616 | tf_op jit(solution)/shard_map/ppermute | solution.py:669
  31.5 2.2 %collective-permute-start.14 = (bf16[64,512]{1,0:T(8,128)(2,1)S(1)}, bf16[64,512]{1,0:T(8,128)(2,1)S(1)}, u32[]{:S(2)}, u32[]{:S(2)}) collective-permute-start(bf16[64,512]{1,0:T(8,128)(2,1)S(1)} %get-tuple-element.90), channel_id=1, source_target_pairs={{0,4},{2,6},{4,0},{6,2},{8,12},{10,14},{12,8},{14,10},{1,5},{3,7},... | collective-permute-start | bytes 196616 | tf_op jit(solution)/shard_map/ppermute | solution.py:669
  33.7 0.0 collective-permute-done.10.refs_1_.rest_1_
  33.7 0.5 collective-permute-start.15
  34.3 0.0 collective-permute-done.11.refs_2_.rest_2_
  34.3 0.0 collective-permute-done.12.refs_3_.rest_3_
  34.3 0.8 %project_early.1.early_ref = bf16[3,8,32,512]{3,2,1,0:T(8,128)(2,1)S(1)} custom-call(bf16[3,512,256]{2,1,0:T(8,128)(2,1)S(1)} %get-tuple-element.63.wqkv_ref, bf16[3,512,256]{2,1,0:T(8,128)(2,1)S(1)} %collective-permute-done.7.wqkv_sib_ref, f32[16,1024]{1,0:T(8,128)S(1)} %copy-done, bf16[64,512]{1,0:T(8,128)(2,1)S(1)} %collective-permute-done.9.refs_0_.rest_0_, ...), custom_call_target="tpu_custom_call" | custom-call | flops 402653184 | tf_op jit(solution)/shard_map/project_early/pallas_call | solution.py:469
  35.0 1.0 %collective-permute-done.13.rest_4_ = bf16[64,512]{1,0:T(8,128)(2,1)S(1)} collective-permute-done((bf16[64,512]{1,0:T(8,128)(2,1)S(1)}, bf16[64,512]{1,0:T(8,128)(2,1)S(1)}, u32[]{:S(2)}, u32[]{:S(2)}) %collective-permute-start.13) | collective-permute-done | bytes 65568 | tf_op jit(solution)/shard_map/ppermute | solution.py:669
  36.0 0.6 %collective-permute-done.14.rest_5_ = bf16[64,512]{1,0:T(8,128)(2,1)S(1)} collective-permute-done((bf16[64,512]{1,0:T(8,128)(2,1)S(1)}, bf16[64,512]{1,0:T(8,128)(2,1)S(1)}, u32[]{:S(2)}, u32[]{:S(2)}) %collective-permute-start.14) | collective-permute-done | bytes 65568 | tf_op jit(solution)/shard_map/ppermute | solution.py:669
  36.7 1.3 %collective-permute-done.15.rest_6_ = bf16[64,512]{1,0:T(8,128)(2,1)S(1)} collective-permute-done((bf16[64,512]{1,0:T(8,128)(2,1)S(1)}, bf16[64,512]{1,0:T(8,128)(2,1)S(1)}, u32[]{:S(2)}, u32[]{:S(2)}) %collective-permute-start.15) | collective-permute-done | bytes 65568 | tf_op jit(solution)/shard_map/ppermute | solution.py:669
  38.0 3.1 %attend.1 = bf16[8,2,64,256]{3,2,1,0:T(8,128)(2,1)S(1)} custom-call(s32[8]{0:T(128)S(1)} %stack.51.flag_ref.refs_0_, bf16[3,8,32,512]{3,2,1,0:T(8,128)(2,1)S(1)} %project_early.1.early_ref, bf16[3,512,256]{2,1,0:T(8,128)(2,1)S(1)} %get-tuple-element.63.wqkv_ref, bf16[3,512,256]{2,1,0:T(8,128)(2,1)S(1)} %collective-permute-done.7.wqkv_sib_ref, ...), custom_call_target="tpu_custom_call" | custom-call | flops 1073741824 | bytes 1048576 | tf_op jit(solution)/shard_map/attend/pallas_call | solution.py:549
  41.1 17.4 %all_to_all.5.arrived_ref = bf16[16,64,256]{2,1,0:T(8,128)(2,1)S(1)} all-to-all(bf16[16,64,256]{2,1,0:T(8,128)(2,1)S(1)} %bitcast.18), channel_id=1, replica_groups=mesh['grp'=2,'gy'=4,'gx'=2,'ch'=2] {'gx','gy','ch'}, dimensions={0} | all-to-all | bytes 1048576 | tf_op jit(solution)/shard_map/all_to_all | solution.py:723
  58.5 1.1 %lay_out.1 = bf16[2,8,64,256]{3,2,1,0:T(8,128)(2,1)} custom-call(bf16[16,64,256]{2,1,0:T(8,128)(2,1)S(1)} %all_to_all.5.arrived_ref), custom_call_target="tpu_custom_call" | custom-call | tf_op jit(solution)/shard_map/lay_out/pallas_call | solution.py:637
  (6 shorter events, 0.0 us)
Async XLA Ops:
  1.6 4.6 %collective-permute-start.3 = (bf16[512,1024]{1,0:T(8,128)(2,1)}, bf16[512,1024]{1,0:T(8,128)(2,1)S(1)}, u32[]{:S(2)}, u32[]{:S(2)}) collective-permute-start(bf16[512,1024]{1,0:T(8,128)(2,1)} %w_ref), channel_id=1, source_target_pairs={{0,1},{1,0},{2,3},{3,2},{4,5},{5,4},{6,7},{7,6},{8,9},{9,8},{10,11... | collective-permute-start | bytes 3145736 | tf_op jit(solution)/shard_map/ppermute | solution.py:689
  2.1 4.1 %collective-permute-start.2 = (bf16[16,64,512]{2,1,0:T(8,128)(2,1)}, bf16[16,64,512]{2,1,0:T(8,128)(2,1)S(1)}, u32[]{:S(2)}, u32[]{:S(2)}) collective-permute-start(bf16[16,64,512]{2,1,0:T(8,128)(2,1)} %cells_hbm.1), channel_id=1, source_target_pairs={{0,1},{1,0},{2,3},{3,2},{4,5},{5,4},{6,7},{7,6},{8,9},{9,8},{10,11... | collective-permute-start | bytes 3145736 | tf_op jit(solution)/shard_map/ppermute | solution.py:689
  2.2 4.0 %collective-permute-start.4 = (f32[16,1024]{1,0:T(8,128)}, f32[16,1024]{1,0:T(8,128)S(1)}, u32[]{:S(2)}, u32[]{:S(2)}) collective-permute-start(f32[16,1024]{1,0:T(8,128)} %get-tuple-element.53.small_ref.refs_4_), channel_id=1, source_target_pairs={{0,1},{1,0},{2,3},{3,2},{4,5},{5,4},{6,7},{7,6},{8,9},{9,8},{10,11... | collective-permute-start | bytes 196616 | tf_op jit(solution)/shard_map/ppermute | solution.py:689
  2.7 5.5 %collective-permute-start = (bf16[64,512]{1,0:T(8,128)(2,1)}, bf16[64,512]{1,0:T(8,128)(2,1)S(1)}, u32[]{:S(2)}, u32[]{:S(2)}) collective-permute-start(bf16[64,512]{1,0:T(8,128)(2,1)} %get-tuple-element.50), channel_id=1, source_target_pairs={{0,4},{8,12},{4,0},{12,8},{1,5},{9,13},{5,1},{13,9},{2,6},{10,14},... | collective-permute-start | bytes 196616 | tf_op jit(solution)/shard_map/ppermute | solution.py:653
  5.3 2.9 %collective-permute-start.1 = (bf16[64,512]{1,0:T(8,128)(2,1)}, bf16[64,512]{1,0:T(8,128)(2,1)S(1)}, u32[]{:S(2)}, u32[]{:S(2)}) collective-permute-start(bf16[64,512]{1,0:T(8,128)(2,1)} %get-tuple-element.51), channel_id=1, source_target_pairs={{4,8},{8,4},{5,9},{9,5},{6,10},{10,6},{7,11},{11,7},{20,24},{24,20... | collective-permute-start | bytes 196616 | tf_op jit(solution)/shard_map/ppermute | solution.py:653
  6.2 2.0 %copy-start.2 = (bf16[1024,512]{1,0:T(8,128)(2,1)S(1)}, bf16[1024,512]{1,0:T(8,128)(2,1)}, u32[]{:S(2)}) copy-start(bf16[1024,512]{1,0:T(8,128)(2,1)} %refs_0_) | copy-start | bytes 3145732
  6.2 5.1 %copy-start = (f32[16,1024]{1,0:T(8,128)S(1)}, f32[16,1024]{1,0:T(8,128)}, u32[]{:S(2)}) copy-start(f32[16,1024]{1,0:T(8,128)} %get-tuple-element.53.small_ref.refs_4_) | copy-start | bytes 196612
  6.3 5.1 %copy-start.1 = (bf16[512,1024]{1,0:T(8,128)(2,1)S(1)}, bf16[512,1024]{1,0:T(8,128)(2,1)}, u32[]{:S(2)}) copy-start(bf16[512,1024]{1,0:T(8,128)(2,1)} %w_ref) | copy-start | bytes 3145732
  6.3 5.1 %copy-start.3 = (bf16[512,3,256]{2,0,1:T(8,128)(2,1)S(1)}, bf16[512,3,256]{2,0,1:T(8,128)(2,1)}, u32[]{:S(2)}) copy-start(bf16[512,3,256]{2,0,1:T(8,128)(2,1)} %param.19) | copy-start | bytes 2359300
  6.3 5.1 %copy-start.4 = (bf16[256,512]{1,0:T(8,128)(2,1)S(1)}, bf16[256,512]{1,0:T(8,128)(2,1)}, u32[]{:S(2)}) copy-start(bf16[256,512]{1,0:T(8,128)(2,1)} %refs_2_.1) | copy-start | bytes 786436
  8.2 5.5 %collective-permute-start.6 = (bf16[1024,512]{1,0:T(8,128)(2,1)S(1)}, bf16[1024,512]{1,0:T(8,128)(2,1)S(1)}, u32[]{:S(2)}, u32[]{:S(2)}) collective-permute-start(bf16[1024,512]{1,0:T(8,128)(2,1)S(1)} %copy-done.2), channel_id=1, source_target_pairs={{0,1},{1,0},{2,3},{3,2},{4,5},{5,4},{6,7},{7,6},{8,9},{9,8},{10,11... | collective-permute-start | bytes 3145736 | tf_op jit(solution)/shard_map/ppermute | solution.py:689
  8.7 4.5 %collective-permute-start.5 = (bf16[18,512]{1,0:T(8,128)(2,1)S(1)}, bf16[18,512]{1,0:T(8,128)(2,1)S(1)}, u32[]{:S(2)}, u32[]{:S(2)}) collective-permute-start(bf16[18,512]{1,0:T(8,128)(2,1)S(1)} %pad_maximum_fusion), channel_id=1, source_target_pairs={{0,2},{2,0},{1,3},{3,1},{4,6},{6,4},{5,7},{7,5},{8,10},{10,8},{9,1... | collective-permute-start | bytes 55304 | tf_op jit(solution)/shard_map/ppermute | solution.py:661
  13.2 4.6 %collective-permute-start.7 = (bf16[3,512,256]{2,1,0:T(8,128)(2,1)S(1)}, bf16[3,512,256]{2,1,0:T(8,128)(2,1)S(1)}, u32[]{:S(2)}, u32[]{:S(2)}) collective-permute-start(bf16[3,512,256]{2,1,0:T(8,128)(2,1)S(1)} %get-tuple-element.63.wqkv_ref), channel_id=1, source_target_pairs={{0,1},{1,0},{2,3},{3,2},{4,5},{5,4},{6,7},{7,6},{8,9},{9,8},{10,11... | collective-permute-start | bytes 2359304 | tf_op jit(solution)/shard_map/ppermute | solution.py:689
  13.2 4.6 %collective-permute-start.8 = (bf16[256,512]{1,0:T(8,128)(2,1)S(1)}, bf16[256,512]{1,0:T(8,128)(2,1)S(1)}, u32[]{:S(2)}, u32[]{:S(2)}) collective-permute-start(bf16[256,512]{1,0:T(8,128)(2,1)S(1)} %get-tuple-element.75.wo_ref), channel_id=1, source_target_pairs={{0,1},{1,0},{2,3},{3,2},{4,5},{5,4},{6,7},{7,6},{8,9},{9,8},{10,11... | collective-permute-start | bytes 786440 | tf_op jit(solution)/shard_map/ppermute | solution.py:689
  17.8 12.9 %collective-permute-start.9 = (bf16[64,512]{1,0:T(8,128)(2,1)S(1)}, bf16[64,512]{1,0:T(8,128)(2,1)S(1)}, u32[]{:S(2)}, u32[]{:S(2)}) collective-permute-start(bf16[64,512]{1,0:T(8,128)(2,1)S(1)} %get-tuple-element.79.refs_10_), channel_id=1, source_target_pairs={{0,8},{2,10},{4,12},{6,14},{8,0},{10,2},{12,4},{14,6},{1,9},{3,11}... | collective-permute-start | bytes 196616 | tf_op jit(solution)/shard_map/ppermute | solution.py:669
  22.9 10.9 %collective-permute-start.10 = (bf16[64,512]{1,0:T(8,128)(2,1)S(1)}, bf16[64,512]{1,0:T(8,128)(2,1)S(1)}, u32[]{:S(2)}, u32[]{:S(2)}) collective-permute-start(bf16[64,512]{1,0:T(8,128)(2,1)S(1)} %get-tuple-element.80.refs_11_), channel_id=1, source_target_pairs={{0,10},{2,8},{4,14},{6,12},{8,2},{10,0},{12,6},{14,4},{1,11},{3,9}... | collective-permute-start | bytes 196616 | tf_op jit(solution)/shard_map/ppermute | solution.py:669
  23.9 10.4 %collective-permute-start.11 = (bf16[64,512]{1,0:T(8,128)(2,1)S(1)}, bf16[64,512]{1,0:T(8,128)(2,1)S(1)}, u32[]{:S(2)}, u32[]{:S(2)}) collective-permute-start(bf16[64,512]{1,0:T(8,128)(2,1)S(1)} %get-tuple-element.81.refs_12_), channel_id=1, source_target_pairs={{0,12},{2,14},{4,8},{6,10},{8,4},{10,6},{12,0},{14,2},{1,13},{3,15... | collective-permute-start | bytes 196616 | tf_op jit(solution)/shard_map/ppermute | solution.py:669
  25.9 8.4 %collective-permute-start.12 = (bf16[64,512]{1,0:T(8,128)(2,1)S(1)}, bf16[64,512]{1,0:T(8,128)(2,1)S(1)}, u32[]{:S(2)}, u32[]{:S(2)}) collective-permute-start(bf16[64,512]{1,0:T(8,128)(2,1)S(1)} %get-tuple-element.82.refs_13_), channel_id=1, source_target_pairs={{0,14},{2,12},{4,10},{6,8},{8,6},{10,4},{12,2},{14,0},{1,15},{3,13... | collective-permute-start | bytes 196616 | tf_op jit(solution)/shard_map/ppermute | solution.py:669
  30.7 5.3 %collective-permute-start.13 = (bf16[64,512]{1,0:T(8,128)(2,1)S(1)}, bf16[64,512]{1,0:T(8,128)(2,1)S(1)}, u32[]{:S(2)}, u32[]{:S(2)}) collective-permute-start(bf16[64,512]{1,0:T(8,128)(2,1)S(1)} %get-tuple-element.89), channel_id=1, source_target_pairs={{0,6},{2,4},{4,2},{6,0},{8,14},{10,12},{12,10},{14,8},{1,7},{3,5},... | collective-permute-start | bytes 196616 | tf_op jit(solution)/shard_map/ppermute | solution.py:669
  31.5 5.2 %collective-permute-start.14 = (bf16[64,512]{1,0:T(8,128)(2,1)S(1)}, bf16[64,512]{1,0:T(8,128)(2,1)S(1)}, u32[]{:S(2)}, u32[]{:S(2)}) collective-permute-start(bf16[64,512]{1,0:T(8,128)(2,1)S(1)} %get-tuple-element.90), channel_id=1, source_target_pairs={{0,4},{2,6},{4,0},{6,2},{8,12},{10,14},{12,8},{14,10},{1,5},{3,7},... | collective-permute-start | bytes 196616 | tf_op jit(solution)/shard_map/ppermute | solution.py:669
  33.7 4.3 %collective-permute-start.15 = (bf16[64,512]{1,0:T(8,128)(2,1)S(1)}, bf16[64,512]{1,0:T(8,128)(2,1)S(1)}, u32[]{:S(2)}, u32[]{:S(2)}) collective-permute-start(bf16[64,512]{1,0:T(8,128)(2,1)S(1)} %get-tuple-element.91), channel_id=1, source_target_pairs={{0,2},{2,0},{4,6},{6,4},{8,10},{10,8},{12,14},{14,12},{1,3},{3,1},... | collective-permute-start | bytes 196616 | tf_op jit(solution)/shard_map/ppermute | solution.py:669

commit v6 on v5

--- a/solution.py
+++ b/solution.py
@@ -689,12 +689,12 @@
         return value, lax.ppermute(value, "ch", [(0, 1), (1, 0)])
 
     w_expand, small = both(w_expand), both(small)
+    w_project = both(w_project)
     e_sib, x, ordered, column = expand_first(plan, flags, both(cells)[1], w_expand[1], small[1])
     e_own, *kept = expand_second(
-        plan, ordered, w_expand[0], small[0], (w_project, w_qkv.transpose(1, 0, 2), w_out)
-    )
-    *rows, x, w_project, column = lax.optimization_barrier((*rows, x, w_project, column))
-    w_project = both(w_project)
+        plan, ordered, w_expand[0], small[0], (w_project[0], w_qkv.transpose(1, 0, 2), w_out)
+    )
+    *rows, x, column = lax.optimization_barrier((*rows, x, column))
     e = e_own, e_sib
     cols = halo_column(column, rows, index, even)
     cols, w_qkv, w_out = lax.optimization_barrier((cols, *kept[2:]))

time: 59.9 us -> 59.8 us (level)
  no operation moved by 1% of the time
where the time goes in v6:
time: 59.8 us; the launch traced here: 59.6 us
  starting transfers between devices  21.4 us (36%)
  blocking collectives  17.4 us (29%)
  Pallas kernels  17 us (28%)
  waiting for transfers between devices  3.53 us (6%)
    all_to_all x1, blocking collectives, fast_device(): returned = lax.all_to_all(leaving, ('gx', 'gy', 'ch'), 0, 0, tiled=True)  17.4 us
    ppermute x7, starting transfers between devices, send_to(): return lax.ppermute(value, ('gy', 'gx'), pairs)  13.5 us
    pallas_call x2, Pallas kernels, deepen(): pl.pallas_call(functools.partial(deepen_kernel, plan, targets, first), in...  7.07 us
    ppermute x2, starting transfers between devices, swap_rows(): lax.ppermute(value, 'gy', pairs + [(target, source) for source, target in...  3.3 us
    pallas_call x1, Pallas kernels, attend_windows(): pl.pallas_call(functools.partial(attend_kernel, plan, targets), in_specs=...  3.13 us
    ppermute x7, waiting for transfers between devices, send_to(): return lax.ppermute(value, ('gy', 'gx'), pairs)  2.97 us
    ppermute x1, starting transfers between devices, halo_column(): return lax.ppermute(jnp.concatenate(parts, axis=0), 'gx', [(0, 1), (1, 0)])  2.7 us
    ppermute x6, starting transfers between devices, both(): return (value, lax.ppermute(value, 'ch', [(0, 1), (1, 0)]))  1.91 us
  transfers between devices with their start and end apart: 16, of which 5 were waited for; matrix products, arithmetic and copies ran while one was open for 0% of the time, Pallas kernels for 19%

profile of v6, /device:TPU:0, one launch (start us, length us, event | category | flops | bytes accessed | tf_op | source)
XLA Modules:
  0.0 59.6 jit_solution(14772063627717914737)
XLA Ops:
  0.0 1.6 %edges.1 = (bf16[64,512]{1,0:T(8,128)(2,1)}, bf16[64,512]{1,0:T(8,128)(2,1)}, f32[16,1024]{1,0:T(8,128)}) custom-call(s32[1]{0:T(128)} %bitcast.8.row_ref, bf16[16,64,512]{2,1,0:T(8,128)(2,1)} %cells_hbm.1, bf16[3,3,1024]{2,1,0:T(4,128)(2,1)} %taps_hbm.1, f32[1,1024]{1,0:T(1,128)} %bitcast.21, f32[1,1024]{1,0:T(1,128)} %bitcast.22, f32[1,256]{1,0:T(1,128)} %bitcast.25, ...), custom_call_target="tpu_custom_call" | custom-call | tf_op jit(solution)/shard_map/edges/pallas_call | solution.py:594
  1.6 0.5 collective-permute-start.3
  2.1 0.1 collective-permute-start.2
  2.2 0.4 collective-permute-start.4
  2.7 2.7 %collective-permute-start = (bf16[64,512]{1,0:T(8,128)(2,1)}, bf16[64,512]{1,0:T(8,128)(2,1)S(1)}, u32[]{:S(2)}, u32[]{:S(2)}) collective-permute-start(bf16[64,512]{1,0:T(8,128)(2,1)} %get-tuple-element.49), channel_id=1, source_target_pairs={{0,4},{8,12},{4,0},{12,8},{1,5},{9,13},{5,1},{13,9},{2,6},{10,14},... | collective-permute-start | bytes 196616 | tf_op jit(solution)/shard_map/ppermute | solution.py:653
  5.3 0.7 %collective-permute-start.1 = (bf16[64,512]{1,0:T(8,128)(2,1)}, bf16[64,512]{1,0:T(8,128)(2,1)S(1)}, u32[]{:S(2)}, u32[]{:S(2)}) collective-permute-start(bf16[64,512]{1,0:T(8,128)(2,1)} %get-tuple-element.50), channel_id=1, source_target_pairs={{4,8},{8,4},{5,9},{9,5},{6,10},{10,6},{7,11},{11,7},{20,24},{24,20... | collective-permute-start | bytes 196616 | tf_op jit(solution)/shard_map/ppermute | solution.py:653
  6.0 0.1 stack.51.flag_ref.refs_0_
  6.1 0.2 collective-permute-done.4.small_ref.refs_5_.small_sib_ref
  6.2 0.4 collective-permute-start.6
  6.6 0.0 collective-permute-done.3.w_ref.refs_12_
  6.6 0.0 collective-permute-done.2
  6.6 0.0 copy-start.1
  6.6 0.0 copy-start.2
  6.6 0.0 copy-start.3
  6.7 0.0 copy-start.4
  6.7 1.9 %expand_first.1 = (bf16[8,80,1024]{2,1,0:T(8,128)(2,1)S(1)}, bf16[8,64,512]{2,1,0:T(8,128)(2,1)S(1)}, bf16[8,80,512]{2,1,0:T(8,128)(2,1)S(1)}, bf16[16,512]{1,0:T(8,128)(2,1)S(1)}) custom-call(s32[8]{0:T(128)S(1)} %stack.51.flag_ref.refs_0_, bf16[2,8,64,512]{3,2,1,0:T(8,128)(2,1)S(1)} %bitcast.20, ...), custom_call_target="tpu_custom_call" | custom-call | flops 4294967296 | bytes 4194304 | tf_op jit(solution)/shard_map/expand_first/pallas_call | solution.py:246
  8.6 0.0 collective-permute-done.refs_8_
  8.6 0.0 collective-permute-done.1.refs_9_
  8.6 2.7 %collective-permute-start.5 = (bf16[18,512]{1,0:T(8,128)(2,1)S(1)}, bf16[18,512]{1,0:T(8,128)(2,1)S(1)}, u32[]{:S(2)}, u32[]{:S(2)}) collective-permute-start(bf16[18,512]{1,0:T(8,128)(2,1)S(1)} %pad_maximum_fusion), channel_id=1, source_target_pairs={{0,2},{2,0},{1,3},{3,1},{4,6},{6,4},{5,7},{7,5},{8,10},{10,8},{9,1... | collective-permute-start | bytes 55304 | tf_op jit(solution)/shard_map/ppermute | solution.py:661
  11.3 0.0 copy-done
  11.3 0.0 copy-done.3
  11.4 1.4 %expand_second.1 = (bf16[8,80,1024]{2,1,0:T(8,128)(2,1)S(1)}, bf16[512,1024]{1,0:T(8,128)(2,1)S(1)}, bf16[1024,512]{1,0:T(8,128)(2,1)S(1)}, bf16[3,512,256]{2,1,0:T(8,128)(2,1)S(1)}, bf16[256,512]{1,0:T(8,128)(2,1)S(1)}) custom-call(bf16[8,80,512]{2,1,0:T(8,128)(2,1)S(1)} %get-tuple-element.58.ordered_ref, bf16[512,1024]{1,0:T(8,128)(2,1)S(1)} %copy-done.1, ...), custom_call_target="tpu_custom_call" | custom-call | flops 671088640 | bytes 1310720 | tf_op jit(solution)/shard_map/expand_second/pallas_call | solution.py:279
  12.7 0.4 collective-permute-done.5.refs_10_
  13.1 0.0 collective-permute-start.7
  13.1 0.5 collective-permute-start.8
  13.6 0.0 collective-permute-done.6.refs_7_
  13.6 4.1 %deepen.2 = (bf16[64,512]{1,0:T(8,128)(2,1)S(1)}, bf16[64,512]{1,0:T(8,128)(2,1)S(1)}, bf16[64,512]{1,0:T(8,128)(2,1)S(1)}, bf16[64,512]{1,0:T(8,128)(2,1)S(1)},...) custom-call(s32[8]{0:T(128)S(1)} %stack.51.flag_ref.refs_0_, ...), custom_call_target="tpu_custom_call" | custom-call | flops 536870912 | bytes 2621440 | tf_op jit(solution)/shard_map/deepen/pallas_call | solution.py:417
  17.7 0.0 collective-permute-done.8.wo_sib_ref
  17.7 0.0 collective-permute-done.7.wqkv_sib_ref
  17.7 5.1 %collective-permute-start.9 = (bf16[64,512]{1,0:T(8,128)(2,1)S(1)}, bf16[64,512]{1,0:T(8,128)(2,1)S(1)}, u32[]{:S(2)}, u32[]{:S(2)}) collective-permute-start(bf16[64,512]{1,0:T(8,128)(2,1)S(1)} %get-tuple-element.77.refs_10_), channel_id=1, source_target_pairs={{0,8},{2,10},{4,12},{6,14},{8,0},{10,2},{12,4},{14,6},{1,9},{3,11}... | collective-permute-start | bytes 196616 | tf_op jit(solution)/shard_map/ppermute | solution.py:669
  22.9 1.0 %collective-permute-start.10 = (bf16[64,512]{1,0:T(8,128)(2,1)S(1)}, bf16[64,512]{1,0:T(8,128)(2,1)S(1)}, u32[]{:S(2)}, u32[]{:S(2)}) collective-permute-start(bf16[64,512]{1,0:T(8,128)(2,1)S(1)} %get-tuple-element.78.refs_11_), channel_id=1, source_target_pairs={{0,10},{2,8},{4,14},{6,12},{8,2},{10,0},{12,6},{14,4},{1,11},{3,9}... | collective-permute-start | bytes 196616 | tf_op jit(solution)/shard_map/ppermute | solution.py:669
  23.9 1.9 %collective-permute-start.11 = (bf16[64,512]{1,0:T(8,128)(2,1)S(1)}, bf16[64,512]{1,0:T(8,128)(2,1)S(1)}, u32[]{:S(2)}, u32[]{:S(2)}) collective-permute-start(bf16[64,512]{1,0:T(8,128)(2,1)S(1)} %get-tuple-element.79.refs_12_), channel_id=1, source_target_pairs={{0,12},{2,14},{4,8},{6,10},{8,4},{10,6},{12,0},{14,2},{1,13},{3,15... | collective-permute-start | bytes 196616 | tf_op jit(solution)/shard_map/ppermute | solution.py:669
  25.8 1.9 %collective-permute-start.12 = (bf16[64,512]{1,0:T(8,128)(2,1)S(1)}, bf16[64,512]{1,0:T(8,128)(2,1)S(1)}, u32[]{:S(2)}, u32[]{:S(2)}) collective-permute-start(bf16[64,512]{1,0:T(8,128)(2,1)S(1)} %get-tuple-element.80.refs_13_), channel_id=1, source_target_pairs={{0,14},{2,12},{4,10},{6,8},{8,6},{10,4},{12,2},{14,0},{1,15},{3,13... | collective-permute-start | bytes 196616 | tf_op jit(solution)/shard_map/ppermute | solution.py:669
  27.7 3.0 %deepen.3 = (bf16[64,512]{1,0:T(8,128)(2,1)S(1)}, bf16[64,512]{1,0:T(8,128)(2,1)S(1)}, bf16[64,512]{1,0:T(8,128)(2,1)S(1)}, bf16[64,512]{1,0:T(8,128)(2,1)S(1)}) custom-call(s32[8]{0:T(128)S(1)} %stack.51.flag_ref.refs_0_, bf16[8,80,1024]{2,1,0:T(8,128)(2,1)S(1)} %get-tuple-element.63.refs_1_, bf16[8,80,1024]{2,1,0:T(8,128)(2,1)S(1)} %get-tuple-element.64.refs_2_, ...), custom_call_target="tpu_custom_call" | custom-call | flops 536870912 | bytes 2621440 | tf_op jit(solution)/shard_map/deepen/pallas_call | solution.py:417
  30.7 0.0 collective-permute-done.9.refs_0_.rest_0_
  30.7 0.8 %collective-permute-start.13 = (bf16[64,512]{1,0:T(8,128)(2,1)S(1)}, bf16[64,512]{1,0:T(8,128)(2,1)S(1)}, u32[]{:S(2)}, u32[]{:S(2)}) collective-permute-start(bf16[64,512]{1,0:T(8,128)(2,1)S(1)} %get-tuple-element.87), channel_id=1, source_target_pairs={{0,6},{2,4},{4,2},{6,0},{8,14},{10,12},{12,10},{14,8},{1,7},{3,5},... | collective-permute-start | bytes 196616 | tf_op jit(solution)/shard_map/ppermute | solution.py:669
  31.5 2.2 %collective-permute-start.14 = (bf16[64,512]{1,0:T(8,128)(2,1)S(1)}, bf16[64,512]{1,0:T(8,128)(2,1)S(1)}, u32[]{:S(2)}, u32[]{:S(2)}) collective-permute-start(bf16[64,512]{1,0:T(8,128)(2,1)S(1)} %get-tuple-element.88), channel_id=1, source_target_pairs={{0,4},{2,6},{4,0},{6,2},{8,12},{10,14},{12,8},{14,10},{1,5},{3,7},... | collective-permute-start | bytes 196616 | tf_op jit(solution)/shard_map/ppermute | solution.py:669
  33.7 0.0 collective-permute-done.10.refs_1_.rest_1_
  33.7 0.5 collective-permute-start.15
  34.3 0.0 collective-permute-done.11.refs_2_.rest_2_
  34.3 0.0 collective-permute-done.12.refs_3_.rest_3_
  34.3 0.8 %project_early.1.early_ref = bf16[3,8,32,512]{3,2,1,0:T(8,128)(2,1)S(1)} custom-call(bf16[3,512,256]{2,1,0:T(8,128)(2,1)S(1)} %get-tuple-element.62.wqkv_ref, bf16[3,512,256]{2,1,0:T(8,128)(2,1)S(1)} %collective-permute-done.7.wqkv_sib_ref, f32[16,1024]{1,0:T(8,128)S(1)} %copy-done, bf16[64,512]{1,0:T(8,128)(2,1)S(1)} %collective-permute-done.9.refs_0_.rest_0_, ...), custom_call_target="tpu_custom_call" | custom-call | flops 402653184 | tf_op jit(solution)/shard_map/project_early/pallas_call | solution.py:469
  35.0 1.0 %collective-permute-done.13.rest_4_ = bf16[64,512]{1,0:T(8,128)(2,1)S(1)} collective-permute-done((bf16[64,512]{1,0:T(8,128)(2,1)S(1)}, bf16[64,512]{1,0:T(8,128)(2,1)S(1)}, u32[]{:S(2)}, u32[]{:S(2)}) %collective-permute-start.13) | collective-permute-done | bytes 65568 | tf_op jit(solution)/shard_map/ppermute | solution.py:669
  36.0 0.6 %collective-permute-done.14.rest_5_ = bf16[64,512]{1,0:T(8,128)(2,1)S(1)} collective-permute-done((bf16[64,512]{1,0:T(8,128)(2,1)S(1)}, bf16[64,512]{1,0:T(8,128)(2,1)S(1)}, u32[]{:S(2)}, u32[]{:S(2)}) %collective-permute-start.14) | collective-permute-done | bytes 65568 | tf_op jit(solution)/shard_map/ppermute | solution.py:669
  36.7 1.3 %collective-permute-done.15.rest_6_ = bf16[64,512]{1,0:T(8,128)(2,1)S(1)} collective-permute-done((bf16[64,512]{1,0:T(8,128)(2,1)S(1)}, bf16[64,512]{1,0:T(8,128)(2,1)S(1)}, u32[]{:S(2)}, u32[]{:S(2)}) %collective-permute-start.15) | collective-permute-done | bytes 65568 | tf_op jit(solution)/shard_map/ppermute | solution.py:669
  38.0 3.1 %attend.1 = bf16[8,2,64,256]{3,2,1,0:T(8,128)(2,1)S(1)} custom-call(s32[8]{0:T(128)S(1)} %stack.51.flag_ref.refs_0_, bf16[3,8,32,512]{3,2,1,0:T(8,128)(2,1)S(1)} %project_early.1.early_ref, bf16[3,512,256]{2,1,0:T(8,128)(2,1)S(1)} %get-tuple-element.62.wqkv_ref, bf16[3,512,256]{2,1,0:T(8,128)(2,1)S(1)} %collective-permute-done.7.wqkv_sib_ref, ...), custom_call_target="tpu_custom_call" | custom-call | flops 1073741824 | bytes 1048576 | tf_op jit(solution)/shard_map/attend/pallas_call | solution.py:549
  41.1 17.4 %all_to_all.5.arrived_ref = bf16[16,64,256]{2,1,0:T(8,128)(2,1)S(1)} all-to-all(bf16[16,64,256]{2,1,0:T(8,128)(2,1)S(1)} %bitcast.18), channel_id=1, replica_groups=mesh['grp'=2,'gy'=4,'gx'=2,'ch'=2] {'gx','gy','ch'}, dimensions={0} | all-to-all | bytes 1048576 | tf_op jit(solution)/shard_map/all_to_all | solution.py:723
  58.5 1.1 %lay_out.1 = bf16[2,8,64,256]{3,2,1,0:T(8,128)(2,1)} custom-call(bf16[16,64,256]{2,1,0:T(8,128)(2,1)S(1)} %all_to_all.5.arrived_ref), custom_call_target="tpu_custom_call" | custom-call | tf_op jit(solution)/shard_map/lay_out/pallas_call | solution.py:637
  (6 shorter events, 0.0 us)
Async XLA Ops:
  1.6 5.0 %collective-permute-start.3 = (bf16[512,1024]{1,0:T(8,128)(2,1)}, bf16[512,1024]{1,0:T(8,128)(2,1)S(1)}, u32[]{:S(2)}, u32[]{:S(2)}) collective-permute-start(bf16[512,1024]{1,0:T(8,128)(2,1)} %w_ref), channel_id=1, source_target_pairs={{0,1},{1,0},{2,3},{3,2},{4,5},{5,4},{6,7},{7,6},{8,9},{9,8},{10,11... | collective-permute-start | bytes 3145736 | tf_op jit(solution)/shard_map/ppermute | solution.py:689
  2.1 4.5 %collective-permute-start.2 = (bf16[16,64,512]{2,1,0:T(8,128)(2,1)}, bf16[16,64,512]{2,1,0:T(8,128)(2,1)S(1)}, u32[]{:S(2)}, u32[]{:S(2)}) collective-permute-start(bf16[16,64,512]{2,1,0:T(8,128)(2,1)} %cells_hbm.1), channel_id=1, source_target_pairs={{0,1},{1,0},{2,3},{3,2},{4,5},{5,4},{6,7},{7,6},{8,9},{9,8},{10,11... | collective-permute-start | bytes 3145736 | tf_op jit(solution)/shard_map/ppermute | solution.py:689
  2.2 4.0 %collective-permute-start.4 = (f32[16,1024]{1,0:T(8,128)}, f32[16,1024]{1,0:T(8,128)S(1)}, u32[]{:S(2)}, u32[]{:S(2)}) collective-permute-start(f32[16,1024]{1,0:T(8,128)} %get-tuple-element.52.small_ref.refs_4_), channel_id=1, source_target_pairs={{0,1},{1,0},{2,3},{3,2},{4,5},{5,4},{6,7},{7,6},{8,9},{9,8},{10,11... | collective-permute-start | bytes 196616 | tf_op jit(solution)/shard_map/ppermute | solution.py:689
  2.7 5.9 %collective-permute-start = (bf16[64,512]{1,0:T(8,128)(2,1)}, bf16[64,512]{1,0:T(8,128)(2,1)S(1)}, u32[]{:S(2)}, u32[]{:S(2)}) collective-permute-start(bf16[64,512]{1,0:T(8,128)(2,1)} %get-tuple-element.49), channel_id=1, source_target_pairs={{0,4},{8,12},{4,0},{12,8},{1,5},{9,13},{5,1},{13,9},{2,6},{10,14},... | collective-permute-start | bytes 196616 | tf_op jit(solution)/shard_map/ppermute | solution.py:653
  5.3 3.3 %collective-permute-start.1 = (bf16[64,512]{1,0:T(8,128)(2,1)}, bf16[64,512]{1,0:T(8,128)(2,1)S(1)}, u32[]{:S(2)}, u32[]{:S(2)}) collective-permute-start(bf16[64,512]{1,0:T(8,128)(2,1)} %get-tuple-element.50), channel_id=1, source_target_pairs={{4,8},{8,4},{5,9},{9,5},{6,10},{10,6},{7,11},{11,7},{20,24},{24,20... | collective-permute-start | bytes 196616 | tf_op jit(solution)/shard_map/ppermute | solution.py:653
  6.2 7.4 %collective-permute-start.6 = (bf16[1024,512]{1,0:T(8,128)(2,1)}, bf16[1024,512]{1,0:T(8,128)(2,1)S(1)}, u32[]{:S(2)}, u32[]{:S(2)}) collective-permute-start(bf16[1024,512]{1,0:T(8,128)(2,1)} %refs_0_), channel_id=1, source_target_pairs={{0,1},{1,0},{2,3},{3,2},{4,5},{5,4},{6,7},{7,6},{8,9},{9,8},{10,11... | collective-permute-start | bytes 3145736 | tf_op jit(solution)/shard_map/ppermute | solution.py:689
  6.6 4.7 %copy-start = (f32[16,1024]{1,0:T(8,128)S(1)}, f32[16,1024]{1,0:T(8,128)}, u32[]{:S(2)}) copy-start(f32[16,1024]{1,0:T(8,128)} %get-tuple-element.52.small_ref.refs_4_) | copy-start | bytes 196612
  6.6 4.7 %copy-start.1 = (bf16[512,1024]{1,0:T(8,128)(2,1)S(1)}, bf16[512,1024]{1,0:T(8,128)(2,1)}, u32[]{:S(2)}) copy-start(bf16[512,1024]{1,0:T(8,128)(2,1)} %w_ref) | copy-start | bytes 3145732
  6.6 4.7 %copy-start.2 = (bf16[1024,512]{1,0:T(8,128)(2,1)S(1)}, bf16[1024,512]{1,0:T(8,128)(2,1)}, u32[]{:S(2)}) copy-start(bf16[1024,512]{1,0:T(8,128)(2,1)} %refs_0_) | copy-start | bytes 3145732
  6.6 4.7 %copy-start.3 = (bf16[512,3,256]{2,0,1:T(8,128)(2,1)S(1)}, bf16[512,3,256]{2,0,1:T(8,128)(2,1)}, u32[]{:S(2)}) copy-start(bf16[512,3,256]{2,0,1:T(8,128)(2,1)} %param.19) | copy-start | bytes 2359300
  6.7 4.7 %copy-start.4 = (bf16[256,512]{1,0:T(8,128)(2,1)S(1)}, bf16[256,512]{1,0:T(8,128)(2,1)}, u32[]{:S(2)}) copy-start(bf16[256,512]{1,0:T(8,128)(2,1)} %refs_2_.1) | copy-start | bytes 786436
  8.6 4.5 %collective-permute-start.5 = (bf16[18,512]{1,0:T(8,128)(2,1)S(1)}, bf16[18,512]{1,0:T(8,128)(2,1)S(1)}, u32[]{:S(2)}, u32[]{:S(2)}) collective-permute-start(bf16[18,512]{1,0:T(8,128)(2,1)S(1)} %pad_maximum_fusion), channel_id=1, source_target_pairs={{0,2},{2,0},{1,3},{3,1},{4,6},{6,4},{5,7},{7,5},{8,10},{10,8},{9,1... | collective-permute-start | bytes 55304 | tf_op jit(solution)/shard_map/ppermute | solution.py:661
  13.1 4.6 %collective-permute-start.7 = (bf16[3,512,256]{2,1,0:T(8,128)(2,1)S(1)}, bf16[3,512,256]{2,1,0:T(8,128)(2,1)S(1)}, u32[]{:S(2)}, u32[]{:S(2)}) collective-permute-start(bf16[3,512,256]{2,1,0:T(8,128)(2,1)S(1)} %get-tuple-element.62.wqkv_ref), channel_id=1, source_target_pairs={{0,1},{1,0},{2,3},{3,2},{4,5},{5,4},{6,7},{7,6},{8,9},{9,8},{10,11... | collective-permute-start | bytes 2359304 | tf_op jit(solution)/shard_map/ppermute | solution.py:689
  13.1 4.6 %collective-permute-start.8 = (bf16[256,512]{1,0:T(8,128)(2,1)S(1)}, bf16[256,512]{1,0:T(8,128)(2,1)S(1)}, u32[]{:S(2)}, u32[]{:S(2)}) collective-permute-start(bf16[256,512]{1,0:T(8,128)(2,1)S(1)} %get-tuple-element.73.wo_ref), channel_id=1, source_target_pairs={{0,1},{1,0},{2,3},{3,2},{4,5},{5,4},{6,7},{7,6},{8,9},{9,8},{10,11... | collective-permute-start | bytes 786440 | tf_op jit(solution)/shard_map/ppermute | solution.py:689
  17.7 12.9 %collective-permute-start.9 = (bf16[64,512]{1,0:T(8,128)(2,1)S(1)}, bf16[64,512]{1,0:T(8,128)(2,1)S(1)}, u32[]{:S(2)}, u32[]{:S(2)}) collective-permute-start(bf16[64,512]{1,0:T(8,128)(2,1)S(1)} %get-tuple-element.77.refs_10_), channel_id=1, source_target_pairs={{0,8},{2,10},{4,12},{6,14},{8,0},{10,2},{12,4},{14,6},{1,9},{3,11}... | collective-permute-start | bytes 196616 | tf_op jit(solution)/shard_map/ppermute | solution.py:669
  22.9 10.9 %collective-permute-start.10 = (bf16[64,512]{1,0:T(8,128)(2,1)S(1)}, bf16[64,512]{1,0:T(8,128)(2,1)S(1)}, u32[]{:S(2)}, u32[]{:S(2)}) collective-permute-start(bf16[64,512]{1,0:T(8,128)(2,1)S(1)} %get-tuple-element.78.refs_11_), channel_id=1, source_target_pairs={{0,10},{2,8},{4,14},{6,12},{8,2},{10,0},{12,6},{14,4},{1,11},{3,9}... | collective-permute-start | bytes 196616 | tf_op jit(solution)/shard_map/ppermute | solution.py:669
  23.9 10.4 %collective-permute-start.11 = (bf16[64,512]{1,0:T(8,128)(2,1)S(1)}, bf16[64,512]{1,0:T(8,128)(2,1)S(1)}, u32[]{:S(2)}, u32[]{:S(2)}) collective-permute-start(bf16[64,512]{1,0:T(8,128)(2,1)S(1)} %get-tuple-element.79.refs_12_), channel_id=1, source_target_pairs={{0,12},{2,14},{4,8},{6,10},{8,4},{10,6},{12,0},{14,2},{1,13},{3,15... | collective-permute-start | bytes 196616 | tf_op jit(solution)/shard_map/ppermute | solution.py:669
  25.8 8.5 %collective-permute-start.12 = (bf16[64,512]{1,0:T(8,128)(2,1)S(1)}, bf16[64,512]{1,0:T(8,128)(2,1)S(1)}, u32[]{:S(2)}, u32[]{:S(2)}) collective-permute-start(bf16[64,512]{1,0:T(8,128)(2,1)S(1)} %get-tuple-element.80.refs_13_), channel_id=1, source_target_pairs={{0,14},{2,12},{4,10},{6,8},{8,6},{10,4},{12,2},{14,0},{1,15},{3,13... | collective-permute-start | bytes 196616 | tf_op jit(solution)/shard_map/ppermute | solution.py:669
  30.7 5.3 %collective-permute-start.13 = (bf16[64,512]{1,0:T(8,128)(2,1)S(1)}, bf16[64,512]{1,0:T(8,128)(2,1)S(1)}, u32[]{:S(2)}, u32[]{:S(2)}) collective-permute-start(bf16[64,512]{1,0:T(8,128)(2,1)S(1)} %get-tuple-element.87), channel_id=1, source_target_pairs={{0,6},{2,4},{4,2},{6,0},{8,14},{10,12},{12,10},{14,8},{1,7},{3,5},... | collective-permute-start | bytes 196616 | tf_op jit(solution)/shard_map/ppermute | solution.py:669
  31.5 5.2 %collective-permute-start.14 = (bf16[64,512]{1,0:T(8,128)(2,1)S(1)}, bf16[64,512]{1,0:T(8,128)(2,1)S(1)}, u32[]{:S(2)}, u32[]{:S(2)}) collective-permute-start(bf16[64,512]{1,0:T(8,128)(2,1)S(1)} %get-tuple-element.88), channel_id=1, source_target_pairs={{0,4},{2,6},{4,0},{6,2},{8,12},{10,14},{12,8},{14,10},{1,5},{3,7},... | collective-permute-start | bytes 196616 | tf_op jit(solution)/shard_map/ppermute | solution.py:669
  33.7 4.3 %collective-permute-start.15 = (bf16[64,512]{1,0:T(8,128)(2,1)S(1)}, bf16[64,512]{1,0:T(8,128)(2,1)S(1)}, u32[]{:S(2)}, u32[]{:S(2)}) collective-permute-start(bf16[64,512]{1,0:T(8,128)(2,1)S(1)} %get-tuple-element.89), channel_id=1, source_target_pairs={{0,2},{2,0},{4,6},{6,4},{8,10},{10,8},{12,14},{14,12},{1,3},{3,1},... | collective-permute-start | bytes 196616 | tf_op jit(solution)/shard_map/ppermute | solution.py:669

commit v7 on v6

--- a/solution.py
+++ b/solution.py
@@ -701,7 +701,7 @@
     w_qkv, w_out = both(w_qkv), both(w_out)
     w_project = kept[1], w_project[1]
     far = [(dy, dx) for dy in (2, 3) for dx in (0, 1)]
-    near = [(1, 1), (1, 0), (0, 1), (0, 0)]
+    near = [(1, 0), (1, 1), (0, 1), (0, 0)]
     outside = (*rows, cols, kept[0], w_expand[1])
     *sent, halo, sides = deepen(plan, far, flags, e, x, small, w_project, outside, True)
     *sent, w_qkv_sib, w_out_sib = lax.optimization_barrier((*sent, w_qkv[1], w_out[1]))

time: 59.8 us -> 60 us (level)
  transfers between devices with their start and end apart: 16 -> 16, of which waited for: 5 -> 4; matrix products, arithmetic and copies ran while one was open for 0% -> 0% of each run, Pallas kernels for 19% -> 19%
where the time goes in v7:
time: 60 us; the launch traced here: 59.8 us
  starting transfers between devices  21.4 us (36%)
  blocking collectives  17.5 us (29%)
  Pallas kernels  17 us (28%)
  waiting for transfers between devices  3.52 us (6%)
    all_to_all x1, blocking collectives, fast_device(): returned = lax.all_to_all(leaving, ('gx', 'gy', 'ch'), 0, 0, tiled=True)  17.5 us
    ppermute x7, starting transfers between devices, send_to(): return lax.ppermute(value, ('gy', 'gx'), pairs)  13.5 us
    pallas_call x2, Pallas kernels, deepen(): pl.pallas_call(functools.partial(deepen_kernel, plan, targets, first), in...  7.07 us
    ppermute x2, starting transfers between devices, swap_rows(): lax.ppermute(value, 'gy', pairs + [(target, source) for source, target in...  3.3 us
    pallas_call x1, Pallas kernels, attend_windows(): pl.pallas_call(functools.partial(attend_kernel, plan, targets), in_specs=...  3.13 us
    ppermute x7, waiting for transfers between devices, send_to(): return lax.ppermute(value, ('gy', 'gx'), pairs)  2.96 us
    ppermute x1, starting transfers between devices, halo_column(): return lax.ppermute(jnp.concatenate(parts, axis=0), 'gx', [(0, 1), (1, 0)])  2.7 us
    ppermute x6, starting transfers between devices, both(): return (value, lax.ppermute(value, 'ch', [(0, 1), (1, 0)]))  1.91 us
  transfers between devices with their start and end apart: 16, of which 4 were waited for; matrix products, arithmetic and copies ran while one was open for 0% of the time, Pallas kernels for 19%

profile of v7, /device:TPU:0, one launch (start us, length us, event | category | flops | bytes accessed | tf_op | source)
XLA Modules:
  0.0 59.8 jit_solution(15387333241292435178)
XLA Ops:
  0.0 1.6 %edges.1 = (bf16[64,512]{1,0:T(8,128)(2,1)}, bf16[64,512]{1,0:T(8,128)(2,1)}, f32[16,1024]{1,0:T(8,128)}) custom-call(s32[1]{0:T(128)} %bitcast.8.row_ref, bf16[16,64,512]{2,1,0:T(8,128)(2,1)} %cells_hbm.1, bf16[3,3,1024]{2,1,0:T(4,128)(2,1)} %taps_hbm.1, f32[1,1024]{1,0:T(1,128)} %bitcast.21, f32[1,1024]{1,0:T(1,128)} %bitcast.22, f32[1,256]{1,0:T(1,128)} %bitcast.25, ...), custom_call_target="tpu_custom_call" | custom-call | tf_op jit(solution)/shard_map/edges/pallas_call | solution.py:594
  1.6 0.5 collective-permute-start.3
  2.1 0.1 collective-permute-start.2
  2.2 0.4 collective-permute-start.4
  2.7 2.7 %collective-permute-start = (bf16[64,512]{1,0:T(8,128)(2,1)}, bf16[64,512]{1,0:T(8,128)(2,1)S(1)}, u32[]{:S(2)}, u32[]{:S(2)}) collective-permute-start(bf16[64,512]{1,0:T(8,128)(2,1)} %get-tuple-element.49), channel_id=1, source_target_pairs={{0,4},{8,12},{4,0},{12,8},{1,5},{9,13},{5,1},{13,9},{2,6},{10,14},... | collective-permute-start | bytes 196616 | tf_op jit(solution)/shard_map/ppermute | solution.py:653
  5.3 0.7 %collective-permute-start.1 = (bf16[64,512]{1,0:T(8,128)(2,1)}, bf16[64,512]{1,0:T(8,128)(2,1)S(1)}, u32[]{:S(2)}, u32[]{:S(2)}) collective-permute-start(bf16[64,512]{1,0:T(8,128)(2,1)} %get-tuple-element.50), channel_id=1, source_target_pairs={{4,8},{8,4},{5,9},{9,5},{6,10},{10,6},{7,11},{11,7},{20,24},{24,20... | collective-permute-start | bytes 196616 | tf_op jit(solution)/shard_map/ppermute | solution.py:653
  6.0 0.1 stack.51.flag_ref.refs_0_
  6.1 0.2 collective-permute-done.4.small_ref.refs_5_.small_sib_ref
  6.2 0.4 collective-permute-start.6
  6.6 0.0 collective-permute-done.3.w_ref.refs_12_
  6.6 0.0 collective-permute-done.2
  6.6 0.0 copy-start.1
  6.6 0.0 copy-start.2
  6.6 0.0 copy-start.3
  6.7 0.0 copy-start.4
  6.7 1.9 %expand_first.1 = (bf16[8,80,1024]{2,1,0:T(8,128)(2,1)S(1)}, bf16[8,64,512]{2,1,0:T(8,128)(2,1)S(1)}, bf16[8,80,512]{2,1,0:T(8,128)(2,1)S(1)}, bf16[16,512]{1,0:T(8,128)(2,1)S(1)}) custom-call(s32[8]{0:T(128)S(1)} %stack.51.flag_ref.refs_0_, bf16[2,8,64,512]{3,2,1,0:T(8,128)(2,1)S(1)} %bitcast.20, ...), custom_call_target="tpu_custom_call" | custom-call | flops 4294967296 | bytes 4194304 | tf_op jit(solution)/shard_map/expand_first/pallas_call | solution.py:246
  8.6 0.0 collective-permute-done.refs_8_
  8.6 0.0 collective-permute-done.1.refs_9_
  8.6 2.7 %collective-permute-start.5 = (bf16[18,512]{1,0:T(8,128)(2,1)S(1)}, bf16[18,512]{1,0:T(8,128)(2,1)S(1)}, u32[]{:S(2)}, u32[]{:S(2)}) collective-permute-start(bf16[18,512]{1,0:T(8,128)(2,1)S(1)} %pad_maximum_fusion), channel_id=1, source_target_pairs={{0,2},{2,0},{1,3},{3,1},{4,6},{6,4},{5,7},{7,5},{8,10},{10,8},{9,1... | collective-permute-start | bytes 55304 | tf_op jit(solution)/shard_map/ppermute | solution.py:661
  11.3 0.0 copy-done
  11.3 0.0 copy-done.2
  11.4 1.4 %expand_second.1 = (bf16[8,80,1024]{2,1,0:T(8,128)(2,1)S(1)}, bf16[512,1024]{1,0:T(8,128)(2,1)S(1)}, bf16[1024,512]{1,0:T(8,128)(2,1)S(1)}, bf16[3,512,256]{2,1,0:T(8,128)(2,1)S(1)}, bf16[256,512]{1,0:T(8,128)(2,1)S(1)}) custom-call(bf16[8,80,512]{2,1,0:T(8,128)(2,1)S(1)} %get-tuple-element.58.ordered_ref, bf16[512,1024]{1,0:T(8,128)(2,1)S(1)} %copy-done.1, ...), custom_call_target="tpu_custom_call" | custom-call | flops 671088640 | bytes 1310720 | tf_op jit(solution)/shard_map/expand_second/pallas_call | solution.py:279
  12.7 0.4 collective-permute-done.5.refs_10_
  13.1 0.0 collective-permute-start.7
  13.1 0.5 collective-permute-start.8
  13.6 0.0 collective-permute-done.6.refs_7_
  13.6 4.1 %deepen.2 = (bf16[64,512]{1,0:T(8,128)(2,1)S(1)}, bf16[64,512]{1,0:T(8,128)(2,1)S(1)}, bf16[64,512]{1,0:T(8,128)(2,1)S(1)}, bf16[64,512]{1,0:T(8,128)(2,1)S(1)},...) custom-call(s32[8]{0:T(128)S(1)} %stack.51.flag_ref.refs_0_, ...), custom_call_target="tpu_custom_call" | custom-call | flops 536870912 | bytes 2621440 | tf_op jit(solution)/shard_map/deepen/pallas_call | solution.py:417
  17.7 0.0 collective-permute-done.8.wo_sib_ref
  17.7 0.0 collective-permute-done.7.wqkv_sib_ref
  17.7 5.1 %collective-permute-start.9 = (bf16[64,512]{1,0:T(8,128)(2,1)S(1)}, bf16[64,512]{1,0:T(8,128)(2,1)S(1)}, u32[]{:S(2)}, u32[]{:S(2)}) collective-permute-start(bf16[64,512]{1,0:T(8,128)(2,1)S(1)} %get-tuple-element.77.refs_10_), channel_id=1, source_target_pairs={{0,8},{2,10},{4,12},{6,14},{8,0},{10,2},{12,4},{14,6},{1,9},{3,11}... | collective-permute-start | bytes 196616 | tf_op jit(solution)/shard_map/ppermute | solution.py:669
  22.9 1.0 %collective-permute-start.10 = (bf16[64,512]{1,0:T(8,128)(2,1)S(1)}, bf16[64,512]{1,0:T(8,128)(2,1)S(1)}, u32[]{:S(2)}, u32[]{:S(2)}) collective-permute-start(bf16[64,512]{1,0:T(8,128)(2,1)S(1)} %get-tuple-element.78.refs_11_), channel_id=1, source_target_pairs={{0,10},{2,8},{4,14},{6,12},{8,2},{10,0},{12,6},{14,4},{1,11},{3,9}... | collective-permute-start | bytes 196616 | tf_op jit(solution)/shard_map/ppermute | solution.py:669
  23.9 1.9 %collective-permute-start.11 = (bf16[64,512]{1,0:T(8,128)(2,1)S(1)}, bf16[64,512]{1,0:T(8,128)(2,1)S(1)}, u32[]{:S(2)}, u32[]{:S(2)}) collective-permute-start(bf16[64,512]{1,0:T(8,128)(2,1)S(1)} %get-tuple-element.79.refs_12_), channel_id=1, source_target_pairs={{0,12},{2,14},{4,8},{6,10},{8,4},{10,6},{12,0},{14,2},{1,13},{3,15... | collective-permute-start | bytes 196616 | tf_op jit(solution)/shard_map/ppermute | solution.py:669
  25.8 1.9 %collective-permute-start.12 = (bf16[64,512]{1,0:T(8,128)(2,1)S(1)}, bf16[64,512]{1,0:T(8,128)(2,1)S(1)}, u32[]{:S(2)}, u32[]{:S(2)}) collective-permute-start(bf16[64,512]{1,0:T(8,128)(2,1)S(1)} %get-tuple-element.80.refs_13_), channel_id=1, source_target_pairs={{0,14},{2,12},{4,10},{6,8},{8,6},{10,4},{12,2},{14,0},{1,15},{3,13... | collective-permute-start | bytes 196616 | tf_op jit(solution)/shard_map/ppermute | solution.py:669
  27.7 3.0 %deepen.3 = (bf16[64,512]{1,0:T(8,128)(2,1)S(1)}, bf16[64,512]{1,0:T(8,128)(2,1)S(1)}, bf16[64,512]{1,0:T(8,128)(2,1)S(1)}, bf16[64,512]{1,0:T(8,128)(2,1)S(1)}) custom-call(s32[8]{0:T(128)S(1)} %stack.51.flag_ref.refs_0_, bf16[8,80,1024]{2,1,0:T(8,128)(2,1)S(1)} %get-tuple-element.63.refs_1_, bf16[8,80,1024]{2,1,0:T(8,128)(2,1)S(1)} %get-tuple-element.64.refs_2_, ...), custom_call_target="tpu_custom_call" | custom-call | flops 536870912 | bytes 2621440 | tf_op jit(solution)/shard_map/deepen/pallas_call | solution.py:417
  30.7 0.0 collective-permute-done.9.refs_0_.rest_0_
  30.7 0.1 collective-permute-start.13
  30.8 2.9 %collective-permute-start.14 = (bf16[64,512]{1,0:T(8,128)(2,1)S(1)}, bf16[64,512]{1,0:T(8,128)(2,1)S(1)}, u32[]{:S(2)}, u32[]{:S(2)}) collective-permute-start(bf16[64,512]{1,0:T(8,128)(2,1)S(1)} %get-tuple-element.88), channel_id=1, source_target_pairs={{0,6},{2,4},{4,2},{6,0},{8,14},{10,12},{12,10},{14,8},{1,7},{3,5},... | collective-permute-start | bytes 196616 | tf_op jit(solution)/shard_map/ppermute | solution.py:669
  33.7 0.0 collective-permute-done.10.refs_1_.rest_1_
  33.7 0.5 collective-permute-start.15
  34.3 0.0 collective-permute-done.11.refs_2_.rest_2_
  34.3 0.0 collective-permute-done.12.refs_3_.rest_3_
  34.3 0.8 %project_early.1.early_ref = bf16[3,8,32,512]{3,2,1,0:T(8,128)(2,1)S(1)} custom-call(bf16[3,512,256]{2,1,0:T(8,128)(2,1)S(1)} %get-tuple-element.62.wqkv_ref, bf16[3,512,256]{2,1,0:T(8,128)(2,1)S(1)} %collective-permute-done.7.wqkv_sib_ref, f32[16,1024]{1,0:T(8,128)S(1)} %copy-done, bf16[64,512]{1,0:T(8,128)(2,1)S(1)} %collective-permute-done.9.refs_0_.rest_0_, ...), custom_call_target="tpu_custom_call" | custom-call | flops 402653184 | tf_op jit(solution)/shard_map/project_early/pallas_call | solution.py:469
  35.0 0.0 collective-permute-done.13.rest_4_
  35.0 1.6 %collective-permute-done.14.rest_5_ = bf16[64,512]{1,0:T(8,128)(2,1)S(1)} collective-permute-done((bf16[64,512]{1,0:T(8,128)(2,1)S(1)}, bf16[64,512]{1,0:T(8,128)(2,1)S(1)}, u32[]{:S(2)}, u32[]{:S(2)}) %collective-permute-start.14) | collective-permute-done | bytes 65568 | tf_op jit(solution)/shard_map/ppermute | solution.py:669
  36.7 1.3 %collective-permute-done.15.rest_6_ = bf16[64,512]{1,0:T(8,128)(2,1)S(1)} collective-permute-done((bf16[64,512]{1,0:T(8,128)(2,1)S(1)}, bf16[64,512]{1,0:T(8,128)(2,1)S(1)}, u32[]{:S(2)}, u32[]{:S(2)}) %collective-permute-start.15) | collective-permute-done | bytes 65568 | tf_op jit(solution)/shard_map/ppermute | solution.py:669
  38.0 3.1 %attend.1 = bf16[8,2,64,256]{3,2,1,0:T(8,128)(2,1)S(1)} custom-call(s32[8]{0:T(128)S(1)} %stack.51.flag_ref.refs_0_, bf16[3,8,32,512]{3,2,1,0:T(8,128)(2,1)S(1)} %project_early.1.early_ref, bf16[3,512,256]{2,1,0:T(8,128)(2,1)S(1)} %get-tuple-element.62.wqkv_ref, bf16[3,512,256]{2,1,0:T(8,128)(2,1)S(1)} %collective-permute-done.7.wqkv_sib_ref, ...), custom_call_target="tpu_custom_call" | custom-call | flops 1073741824 | bytes 1048576 | tf_op jit(solution)/shard_map/attend/pallas_call | solution.py:549
  41.1 17.5 %all_to_all.5.arrived_ref = bf16[16,64,256]{2,1,0:T(8,128)(2,1)S(1)} all-to-all(bf16[16,64,256]{2,1,0:T(8,128)(2,1)S(1)} %bitcast.18), channel_id=1, replica_groups=mesh['grp'=2,'gy'=4,'gx'=2,'ch'=2] {'gx','gy','ch'}, dimensions={0} | all-to-all | bytes 1048576 | tf_op jit(solution)/shard_map/all_to_all | solution.py:723
  58.6 1.1 %lay_out.1 = bf16[2,8,64,256]{3,2,1,0:T(8,128)(2,1)} custom-call(bf16[16,64,256]{2,1,0:T(8,128)(2,1)S(1)} %all_to_all.5.arrived_ref), custom_call_target="tpu_custom_call" | custom-call | tf_op jit(solution)/shard_map/lay_out/pallas_call | solution.py:637
  (6 shorter events, 0.0 us)
Async XLA Ops:
  1.6 5.0 %collective-permute-start.3 = (bf16[512,1024]{1,0:T(8,128)(2,1)}, bf16[512,1024]{1,0:T(8,128)(2,1)S(1)}, u32[]{:S(2)}, u32[]{:S(2)}) collective-permute-start(bf16[512,1024]{1,0:T(8,128)(2,1)} %w_ref), channel_id=1, source_target_pairs={{0,1},{1,0},{2,3},{3,2},{4,5},{5,4},{6,7},{7,6},{8,9},{9,8},{10,11... | collective-permute-start | bytes 3145736 | tf_op jit(solution)/shard_map/ppermute | solution.py:689
  2.1 4.5 %collective-permute-start.2 = (bf16[16,64,512]{2,1,0:T(8,128)(2,1)}, bf16[16,64,512]{2,1,0:T(8,128)(2,1)S(1)}, u32[]{:S(2)}, u32[]{:S(2)}) collective-permute-start(bf16[16,64,512]{2,1,0:T(8,128)(2,1)} %cells_hbm.1), channel_id=1, source_target_pairs={{0,1},{1,0},{2,3},{3,2},{4,5},{5,4},{6,7},{7,6},{8,9},{9,8},{10,11... | collective-permute-start | bytes 3145736 | tf_op jit(solution)/shard_map/ppermute | solution.py:689
  2.2 4.0 %collective-permute-start.4 = (f32[16,1024]{1,0:T(8,128)}, f32[16,1024]{1,0:T(8,128)S(1)}, u32[]{:S(2)}, u32[]{:S(2)}) collective-permute-start(f32[16,1024]{1,0:T(8,128)} %get-tuple-element.52.small_ref.refs_4_), channel_id=1, source_target_pairs={{0,1},{1,0},{2,3},{3,2},{4,5},{5,4},{6,7},{7,6},{8,9},{9,8},{10,11... | collective-permute-start | bytes 196616 | tf_op jit(solution)/shard_map/ppermute | solution.py:689
  2.7 5.9 %collective-permute-start = (bf16[64,512]{1,0:T(8,128)(2,1)}, bf16[64,512]{1,0:T(8,128)(2,1)S(1)}, u32[]{:S(2)}, u32[]{:S(2)}) collective-permute-start(bf16[64,512]{1,0:T(8,128)(2,1)} %get-tuple-element.49), channel_id=1, source_target_pairs={{0,4},{8,12},{4,0},{12,8},{1,5},{9,13},{5,1},{13,9},{2,6},{10,14},... | collective-permute-start | bytes 196616 | tf_op jit(solution)/shard_map/ppermute | solution.py:653
  5.3 3.3 %collective-permute-start.1 = (bf16[64,512]{1,0:T(8,128)(2,1)}, bf16[64,512]{1,0:T(8,128)(2,1)S(1)}, u32[]{:S(2)}, u32[]{:S(2)}) collective-permute-start(bf16[64,512]{1,0:T(8,128)(2,1)} %get-tuple-element.50), channel_id=1, source_target_pairs={{4,8},{8,4},{5,9},{9,5},{6,10},{10,6},{7,11},{11,7},{20,24},{24,20... | collective-permute-start | bytes 196616 | tf_op jit(solution)/shard_map/ppermute | solution.py:653
  6.2 7.4 %collective-permute-start.6 = (bf16[1024,512]{1,0:T(8,128)(2,1)}, bf16[1024,512]{1,0:T(8,128)(2,1)S(1)}, u32[]{:S(2)}, u32[]{:S(2)}) collective-permute-start(bf16[1024,512]{1,0:T(8,128)(2,1)} %refs_0_), channel_id=1, source_target_pairs={{0,1},{1,0},{2,3},{3,2},{4,5},{5,4},{6,7},{7,6},{8,9},{9,8},{10,11... | collective-permute-start | bytes 3145736 | tf_op jit(solution)/shard_map/ppermute | solution.py:689
  6.6 4.7 %copy-start = (f32[16,1024]{1,0:T(8,128)S(1)}, f32[16,1024]{1,0:T(8,128)}, u32[]{:S(2)}) copy-start(f32[16,1024]{1,0:T(8,128)} %get-tuple-element.52.small_ref.refs_4_) | copy-start | bytes 196612
  6.6 4.7 %copy-start.1 = (bf16[512,1024]{1,0:T(8,128)(2,1)S(1)}, bf16[512,1024]{1,0:T(8,128)(2,1)}, u32[]{:S(2)}) copy-start(bf16[512,1024]{1,0:T(8,128)(2,1)} %w_ref) | copy-start | bytes 3145732
  6.6 4.7 %copy-start.2 = (bf16[1024,512]{1,0:T(8,128)(2,1)S(1)}, bf16[1024,512]{1,0:T(8,128)(2,1)}, u32[]{:S(2)}) copy-start(bf16[1024,512]{1,0:T(8,128)(2,1)} %refs_0_) | copy-start | bytes 3145732
  6.6 4.7 %copy-start.3 = (bf16[512,3,256]{2,0,1:T(8,128)(2,1)S(1)}, bf16[512,3,256]{2,0,1:T(8,128)(2,1)}, u32[]{:S(2)}) copy-start(bf16[512,3,256]{2,0,1:T(8,128)(2,1)} %param.19) | copy-start | bytes 2359300
  6.7 4.7 %copy-start.4 = (bf16[256,512]{1,0:T(8,128)(2,1)S(1)}, bf16[256,512]{1,0:T(8,128)(2,1)}, u32[]{:S(2)}) copy-start(bf16[256,512]{1,0:T(8,128)(2,1)} %refs_2_.1) | copy-start | bytes 786436
  8.6 4.5 %collective-permute-start.5 = (bf16[18,512]{1,0:T(8,128)(2,1)S(1)}, bf16[18,512]{1,0:T(8,128)(2,1)S(1)}, u32[]{:S(2)}, u32[]{:S(2)}) collective-permute-start(bf16[18,512]{1,0:T(8,128)(2,1)S(1)} %pad_maximum_fusion), channel_id=1, source_target_pairs={{0,2},{2,0},{1,3},{3,1},{4,6},{6,4},{5,7},{7,5},{8,10},{10,8},{9,1... | collective-permute-start | bytes 55304 | tf_op jit(solution)/shard_map/ppermute | solution.py:661
  13.1 4.6 %collective-permute-start.7 = (bf16[3,512,256]{2,1,0:T(8,128)(2,1)S(1)}, bf16[3,512,256]{2,1,0:T(8,128)(2,1)S(1)}, u32[]{:S(2)}, u32[]{:S(2)}) collective-permute-start(bf16[3,512,256]{2,1,0:T(8,128)(2,1)S(1)} %get-tuple-element.62.wqkv_ref), channel_id=1, source_target_pairs={{0,1},{1,0},{2,3},{3,2},{4,5},{5,4},{6,7},{7,6},{8,9},{9,8},{10,11... | collective-permute-start | bytes 2359304 | tf_op jit(solution)/shard_map/ppermute | solution.py:689
  13.1 4.6 %collective-permute-start.8 = (bf16[256,512]{1,0:T(8,128)(2,1)S(1)}, bf16[256,512]{1,0:T(8,128)(2,1)S(1)}, u32[]{:S(2)}, u32[]{:S(2)}) collective-permute-start(bf16[256,512]{1,0:T(8,128)(2,1)S(1)} %get-tuple-element.73.wo_ref), channel_id=1, source_target_pairs={{0,1},{1,0},{2,3},{3,2},{4,5},{5,4},{6,7},{7,6},{8,9},{9,8},{10,11... | collective-permute-start | bytes 786440 | tf_op jit(solution)/shard_map/ppermute | solution.py:689
  17.7 12.9 %collective-permute-start.9 = (bf16[64,512]{1,0:T(8,128)(2,1)S(1)}, bf16[64,512]{1,0:T(8,128)(2,1)S(1)}, u32[]{:S(2)}, u32[]{:S(2)}) collective-permute-start(bf16[64,512]{1,0:T(8,128)(2,1)S(1)} %get-tuple-element.77.refs_10_), channel_id=1, source_target_pairs={{0,8},{2,10},{4,12},{6,14},{8,0},{10,2},{12,4},{14,6},{1,9},{3,11}... | collective-permute-start | bytes 196616 | tf_op jit(solution)/shard_map/ppermute | solution.py:669
  22.9 10.9 %collective-permute-start.10 = (bf16[64,512]{1,0:T(8,128)(2,1)S(1)}, bf16[64,512]{1,0:T(8,128)(2,1)S(1)}, u32[]{:S(2)}, u32[]{:S(2)}) collective-permute-start(bf16[64,512]{1,0:T(8,128)(2,1)S(1)} %get-tuple-element.78.refs_11_), channel_id=1, source_target_pairs={{0,10},{2,8},{4,14},{6,12},{8,2},{10,0},{12,6},{14,4},{1,11},{3,9}... | collective-permute-start | bytes 196616 | tf_op jit(solution)/shard_map/ppermute | solution.py:669
  23.9 10.4 %collective-permute-start.11 = (bf16[64,512]{1,0:T(8,128)(2,1)S(1)}, bf16[64,512]{1,0:T(8,128)(2,1)S(1)}, u32[]{:S(2)}, u32[]{:S(2)}) collective-permute-start(bf16[64,512]{1,0:T(8,128)(2,1)S(1)} %get-tuple-element.79.refs_12_), channel_id=1, source_target_pairs={{0,12},{2,14},{4,8},{6,10},{8,4},{10,6},{12,0},{14,2},{1,13},{3,15... | collective-permute-start | bytes 196616 | tf_op jit(solution)/shard_map/ppermute | solution.py:669
  25.8 8.5 %collective-permute-start.12 = (bf16[64,512]{1,0:T(8,128)(2,1)S(1)}, bf16[64,512]{1,0:T(8,128)(2,1)S(1)}, u32[]{:S(2)}, u32[]{:S(2)}) collective-permute-start(bf16[64,512]{1,0:T(8,128)(2,1)S(1)} %get-tuple-element.80.refs_13_), channel_id=1, source_target_pairs={{0,14},{2,12},{4,10},{6,8},{8,6},{10,4},{12,2},{14,0},{1,15},{3,13... | collective-permute-start | bytes 196616 | tf_op jit(solution)/shard_map/ppermute | solution.py:669
  30.7 4.3 %collective-permute-start.13 = (bf16[64,512]{1,0:T(8,128)(2,1)S(1)}, bf16[64,512]{1,0:T(8,128)(2,1)S(1)}, u32[]{:S(2)}, u32[]{:S(2)}) collective-permute-start(bf16[64,512]{1,0:T(8,128)(2,1)S(1)} %get-tuple-element.87), channel_id=1, source_target_pairs={{0,4},{2,6},{4,0},{6,2},{8,12},{10,14},{12,8},{14,10},{1,5},{3,7},... | collective-permute-start | bytes 196616 | tf_op jit(solution)/shard_map/ppermute | solution.py:669
  30.8 5.9 %collective-permute-start.14 = (bf16[64,512]{1,0:T(8,128)(2,1)S(1)}, bf16[64,512]{1,0:T(8,128)(2,1)S(1)}, u32[]{:S(2)}, u32[]{:S(2)}) collective-permute-start(bf16[64,512]{1,0:T(8,128)(2,1)S(1)} %get-tuple-element.88), channel_id=1, source_target_pairs={{0,6},{2,4},{4,2},{6,0},{8,14},{10,12},{12,10},{14,8},{1,7},{3,5},... | collective-permute-start | bytes 196616 | tf_op jit(solution)/shard_map/ppermute | solution.py:669
  33.7 4.3 %collective-permute-start.15 = (bf16[64,512]{1,0:T(8,128)(2,1)S(1)}, bf16[64,512]{1,0:T(8,128)(2,1)S(1)}, u32[]{:S(2)}, u32[]{:S(2)}) collective-permute-start(bf16[64,512]{1,0:T(8,128)(2,1)S(1)} %get-tuple-element.89), channel_id=1, source_target_pairs={{0,2},{2,0},{4,6},{6,4},{8,10},{10,8},{12,14},{14,12},{1,3},{3,1},... | collective-permute-start | bytes 196616 | tf_op jit(solution)/shard_map/ppermute | solution.py:669
